TPU v7x, 32 devices: a whole 2x2x4 slice. The times are simulated.
32 devices in a mesh: groups: 2 (over y), tile: 4 (over z), vec: 4 (over x, core).
Axes of the slice: x: 2, y: 2, z: 4, core: 2. Of those that a mesh axis runs over, the one named last changes fastest.
Arguments:
- vectors: float32 [2, 256, 3, 8192], P(None, 'vec', None, ('groups', 'tile')), parts along dimension 3, may hold values from -6 to 6
- links: float32 [3, 2, 3, 3, 8192], P(None, None, None, None, ('groups', 'tile')), parts along dimension 4, may hold values from -2.5 to 2.5
- momenta: int32 [8, 3], replicated, may hold values from -2 to 2
- directions: int32 [2], replicated, may hold values from 0 to 5
Outputs:
- elementals: float32 [512, 2, 2, 8, 256], P(('groups', 'tile'), None, None, None, 'vec'), parts along dimension 0
There are 2 independent parts, one for each index of `groups`. A program takes and returns all parts, laid end to end along the dimension named above; an argument that names none is the same for every part. Nothing has to cross between parts.
Inputs may be any that keep to these rules, and one draw needn't show every extreme that they name: directions 0, 1, 2 step forward along the first, second, third dimension; 3, 4, 5 step backward along them.
All inputs are finite; a program needn't handle non-finite values.
Results may differ from a plain program's by a relative error of at most 0.00012.
Values sent between devices are 32-bit elements; how exact they have to be, the bound alone decides.
No kernel may reach another device: no remote copies, remote signals or barrier semaphores. Data moves between devices by JAX's collectives and lax.ppermute only.
A program may use at most 128 MiB of HBM per device.

v0:
```python
import math

import jax
import jax.numpy as jnp
from jax import lax
from jax.sharding import PartitionSpec as P

LY = 16
LZ = 32
ITERS = 4


hop_scale = 0.125


def passed_along(value, axis, steps):
    count = lax.axis_size(axis)
    pairs = [(source, (source + steps) % count) for source in range(count)]
    return lax.ppermute(value, axis, pairs)


def extended(x, sides, width):
    for axis, dim in sides:
        count, length = (lax.axis_size(axis), x.shape[dim])
        up = [(i, (i + 1) % count) for i in range(count)]
        down = [(j, i) for i, j in up]
        last = lax.slice_in_dim(x, length - width, length, axis=dim)
        first = lax.slice_in_dim(x, 0, width, axis=dim)
        before = lax.ppermute(last, axis, up)
        after = lax.ppermute(first, axis, down)
        x = jnp.concatenate([before, x, after], axis=dim)
    return x


def link_apply(link_real, link_imag, field_real, field_imag, dagger):
    if dagger:
        link_real = jnp.swapaxes(link_real, 0, 1)
        link_imag = -jnp.swapaxes(link_imag, 0, 1)
    out_real = 0.0
    out_imag = 0.0
    for column in range(3):
        left_real = link_real[:, column][None]
        left_imag = link_imag[:, column][None]
        right_real = field_real[:, column][:, None]
        right_imag = field_imag[:, column][:, None]
        out_real = out_real + left_real * right_real - left_imag * right_imag
        out_imag = out_imag + left_real * right_imag + left_imag * right_real
    return (out_real, out_imag)


def roll_depth(center, step):
    plane_size = center.shape[-1]
    depth_index = jnp.arange(plane_size, dtype=jnp.int32) % LZ
    if step < 0:
        at_edge = depth_index == LZ - 1
        wrapped = jnp.roll(center, LZ - 1, axis=-1)
        plain = jnp.roll(center, -1, axis=-1)
    else:
        at_edge = depth_index == 0
        wrapped = jnp.roll(center, 1 - LZ, axis=-1)
        plain = jnp.roll(center, 1, axis=-1)
    return jnp.where(at_edge, wrapped, plain)


def neighbours(padded):
    center = padded[:, :, :, 1:-1]
    ahead = (padded[:, :, :, 2:], jnp.roll(center, -LZ, axis=4), roll_depth(center, -1))
    behind = (padded[:, :, :, :-2], jnp.roll(center, LZ, axis=4), roll_depth(center, 1))
    return (ahead, behind)


def hop_padded(padded, forward, backward):
    ahead, behind = neighbours(padded)
    total_real = 0.0
    total_imag = 0.0
    for spatial in range(3):
        ahead_real, ahead_imag = link_apply(
            forward[spatial][0], forward[spatial][1], ahead[spatial][0], ahead[spatial][1], False
        )
        behind_real, behind_imag = link_apply(
            backward[spatial][0], backward[spatial][1], behind[spatial][0], behind[spatial][1], True
        )
        total_real = total_real + ahead_real + behind_real
        total_imag = total_imag + ahead_imag + behind_imag
    return hop_scale * jnp.stack([total_real, total_imag])


def phases(momenta, flat_index, extent_x):
    plane_size = LY * LZ
    coord_x = flat_index // plane_size
    coord_y = flat_index % plane_size // LZ
    coord_z = flat_index % LZ
    part_x = jnp.mod(momenta[:, 0:1] * coord_x[None], extent_x).astype(jnp.float32) / extent_x
    part_y = jnp.mod(momenta[:, 1:2] * coord_y[None], LY).astype(jnp.float32) / LY
    part_z = jnp.mod(momenta[:, 2:3] * coord_z[None], LZ).astype(jnp.float32) / LZ
    angle = 2.0 * math.pi * (part_x + part_y + part_z)
    return (jnp.cos(angle), jnp.sin(angle))


def right_matrix(right_stack):
    disp_count = right_stack.shape[0]
    column_count = right_stack.shape[2]
    flat_real = right_stack[:, 0].reshape(disp_count, column_count, -1)
    flat_imag = right_stack[:, 1].reshape(disp_count, column_count, -1)
    real_side = jnp.concatenate([flat_real, flat_imag], axis=2)
    imag_side = jnp.concatenate([flat_imag, -flat_real], axis=2)
    return jnp.stack([real_side, imag_side], axis=1)


def twist_left(left_field, cos_row, sin_row):
    row_count = left_field.shape[1]
    twisted_real = cos_row * left_field[0] - sin_row * left_field[1]
    twisted_imag = cos_row * left_field[1] + sin_row * left_field[0]
    return jnp.concatenate(
        [twisted_real.reshape(row_count, -1), twisted_imag.reshape(row_count, -1)], axis=1
    )


def elemental_each(left_field, right_mat, cosine, sine, norm_factor):

    def one_momentum(phase_pair):
        left_flat = twist_left(left_field, phase_pair[0], phase_pair[1])
        return jnp.einsum("ik,dcjk->idcj", left_flat, right_mat, precision=lax.Precision.HIGHEST)

    result = lax.map(one_momentum, (cosine, sine))
    return jnp.transpose(result, (1, 2, 3, 0, 4)) * norm_factor


def make_shift(link_pair, source, dagger, vector_count, site_count):

    def branch_fn():
        moved = link_apply(link_pair[0], link_pair[1], source[0], source[1], dagger)
        return jnp.stack(moved).reshape(2, vector_count, 3, site_count)

    return branch_fn


def local(vectors, links, momenta, directions):
    nv_dev = vectors.shape[1]
    site_count = vectors.shape[3]
    plane_size = LY * LZ
    plane_count = site_count // plane_size
    tile_count = lax.axis_size("tile")
    disp_count = directions.shape[0]
    extent_x = plane_count * tile_count
    norm_factor = 1.0 / math.sqrt(3.0 * site_count * tile_count)
    gauge = links.reshape(3, 2, 3, 3, plane_count, plane_size)
    last_plane = links[0, :, :, :, site_count - plane_size :]
    rim = passed_along(last_plane, "tile", 1)
    behind_x = jnp.concatenate(
        [rim.reshape(2, 3, 3, 1, plane_size), gauge[0][:, :, :, : plane_count - 1]], axis=3
    )
    forward = [gauge[spatial] for spatial in range(3)]
    backward = [behind_x, jnp.roll(gauge[1], LZ, axis=4), roll_depth(gauge[2], 1)]

    def apply_hop(source):
        padded = extended(source, (("tile", 3),), plane_size)
        padded = padded.reshape(2, nv_dev, 3, plane_count + 2, plane_size)
        return hop_padded(padded, forward, backward).reshape(2, nv_dev, 3, site_count)

    previous = vectors
    current = apply_hop(vectors)
    for order in range(ITERS - 1):
        following = 2.0 * apply_hop(current) - previous
        previous, current = (current, following)
    padded_field = extended(current, (("tile", 3),), plane_size)
    padded_field = padded_field.reshape(2, nv_dev, 3, plane_count + 2, plane_size)
    ahead, behind = neighbours(padded_field)
    branches = [
        make_shift(forward[heading], ahead[heading], False, nv_dev, site_count)
        for heading in range(3)
    ]
    branches = branches + [
        make_shift(backward[heading], behind[heading], True, nv_dev, site_count)
        for heading in range(3)
    ]
    displaced = jnp.stack(
        [lax.switch(directions[disp_slot], branches) for disp_slot in range(disp_count)]
    )
    flat_index = lax.axis_index("tile") * site_count + jnp.arange(site_count, dtype=jnp.int32)
    cosine, sine = phases(momenta, flat_index, extent_x)
    right_mat = right_matrix(displaced)
    partial_rows = elemental_each(
        lax.all_gather(current, "vec", axis=1, tiled=True), right_mat, cosine, sine, norm_factor
    )
    return lax.psum_scatter(partial_rows, "tile", scatter_dimension=0, tiled=True)


def solution(mesh):
    return jax.shard_map(
        local,
        mesh=mesh,
        in_specs=(
            P(None, "vec", None, ("groups", "tile")),
            P(None, None, None, None, ("groups", "tile")),
            P(),
            P(),
        ),
        out_specs=P(("groups", "tile"), None, None, None, "vec"),
        check_vma=False,
    )
```

profile of v0, /device:TPU:9, one launch (start us, length us, event | category | flops | bytes accessed | tf_op | source)
XLA Modules:
  0.0 776.3 jit_solution(13172530853241620579)
XLA Ops:
  18.6 27.1 %collective-permute-done.2 = f32[2,3,3,512]{3,0,2,1:T(2,128)S(1)} collective-permute-done((f32[2,3,3,512]{3,0,2,1:T(2,128)S(1)}, f32[2,3,3,512]{3,0,2,1:T(2,128)S(1)}, u32[]{:S(2)}, u32[]{:S(2)}) %collective-permute-start.2) | collective-permute-done | bytes 36896 | tf_op jit(solution)/shard_map/ppermute | solution.py:19
  69.2 5.7 maximum_select_fusion
  94.7 16.3 %collective-permute-done.3 = f32[2,64,3,512]{3,1,2,0:T(8,128)S(1)} collective-permute-done((f32[2,64,3,512]{3,1,2,0:T(8,128)S(1)}, f32[2,64,3,512]{3,1,2,0:T(8,128)S(1)}, u32[]{:S(2)}, u32[]{:S(2)}) %collective-permute-start.3) | collective-permute-done | bytes 786464 | tf_op jit(solution)/shard_map/ppermute | solution.py:29
  111.0 16.0 %collective-permute-done.4 = f32[2,64,3,512]{3,1,2,0:T(8,128)S(1)} collective-permute-done((f32[2,64,3,512]{3,1,2,0:T(8,128)S(1)}, f32[2,64,3,512]{3,1,2,0:T(8,128)S(1)}, u32[]{:S(2)}, u32[]{:S(2)}) %collective-permute-start.4) | collective-permute-done | bytes 786464 | tf_op jit(solution)/shard_map/ppermute | solution.py:30
  173.0 14.7 %collective-permute-done.5 = f32[2,64,3,512]{3,1,2,0:T(8,128)S(1)} collective-permute-done((f32[2,64,3,512]{3,1,2,0:T(8,128)S(1)}, f32[2,64,3,512]{3,1,2,0:T(8,128)S(1)}, u32[]{:S(2)}, u32[]{:S(2)}) %collective-permute-start.5) | collective-permute-done | bytes 786464 | tf_op jit(solution)/shard_map/ppermute | solution.py:29
  187.7 21.4 %collective-permute-done.6 = f32[2,64,3,512]{3,1,2,0:T(8,128)S(1)} collective-permute-done((f32[2,64,3,512]{3,1,2,0:T(8,128)S(1)}, f32[2,64,3,512]{3,1,2,0:T(8,128)S(1)}, u32[]{:S(2)}, u32[]{:S(2)}) %collective-permute-start.6) | collective-permute-done | bytes 786464 | tf_op jit(solution)/shard_map/ppermute | solution.py:30
  252.9 17.2 %collective-permute-done.7 = f32[2,64,3,512]{3,1,2,0:T(8,128)S(1)} collective-permute-done((f32[2,64,3,512]{3,1,2,0:T(8,128)S(1)}, f32[2,64,3,512]{3,1,2,0:T(8,128)S(1)}, u32[]{:S(2)}, u32[]{:S(2)}) %collective-permute-start.7) | collective-permute-done | bytes 786464 | tf_op jit(solution)/shard_map/ppermute | solution.py:29
  270.1 17.4 %collective-permute-done.8 = f32[2,64,3,512]{3,1,2,0:T(8,128)S(1)} collective-permute-done((f32[2,64,3,512]{3,1,2,0:T(8,128)S(1)}, f32[2,64,3,512]{3,1,2,0:T(8,128)S(1)}, u32[]{:S(2)}, u32[]{:S(2)}) %collective-permute-start.8) | collective-permute-done | bytes 786464 | tf_op jit(solution)/shard_map/ppermute | solution.py:30
  338.4 16.8 %collective-permute-done.10 = f32[2,64,3,512]{3,1,2,0:T(8,128)S(1)} collective-permute-done((f32[2,64,3,512]{3,1,2,0:T(8,128)S(1)}, f32[2,64,3,512]{3,1,2,0:T(8,128)S(1)}, u32[]{:S(2)}, u32[]{:S(2)}) %collective-permute-start.10) | collective-permute-done | bytes 786464 | tf_op jit(solution)/shard_map/ppermute | solution.py:30
  355.3 16.8 %collective-permute-done.9 = f32[2,64,3,512]{3,1,2,0:T(8,128)S(1)} collective-permute-done((f32[2,64,3,512]{3,1,2,0:T(8,128)S(1)}, f32[2,64,3,512]{3,1,2,0:T(8,128)S(1)}, u32[]{:S(2)}, u32[]{:S(2)}) %collective-permute-start.9) | collective-permute-done | bytes 786464 | tf_op jit(solution)/shard_map/ppermute | solution.py:29
  403.3 11.6 %conditional.2 = (f32[1,2,64,3,1024]{4,3,2,1,0:T(4,128)}) conditional(s32[]{:T(128)} %bitcast.162, (f32[2,3,3,2,512]{4,3,0,2,1:T(2,128)S(1)}, f32[2,64,3,2,512]{4,3,1,2,0:T(2,128)S(1)}) %tuple.597, (f32[2,3,3,2,512]{4,3,0,2,1:T(2,128)S(1)}, f32[2,64,3,2,512]{4,3,1,2,0:T(2,128)S(1)}) %tuple.593, ...), branch_computations={%region_0.1_spmd, %region_1.2_spmd, %region_2.3_spmd, %region_3.4_... | conditional | flops 4727808 | bytes 16539684 | solution.py:178
  414.9 19.1 %conditional.3 = (f32[1,2,64,3,1024]{4,3,2,1,0:T(4,128)S(1)}) conditional(s32[]{:T(128)} %bitcast.163, (f32[2,3,3,2,512]{4,3,0,2,1:T(2,128)S(1)}, f32[2,64,3,2,512]{4,3,1,2,0:T(2,128)}) %tuple.598, (f32[2,3,3,2,512]{4,3,0,2,1:T(2,128)S(1)}, f32[2,64,3,2,512]{4,3,1,2,0:T(2,128)S(1)}) %tuple.594, ...), branch_computations={%region_6.7_spmd, %region_7.8_spmd, %region_8.9_spmd, %region_9.10... | conditional | flops 4727808 | bytes 16539684 | solution.py:178
  450.8 10.2 %copy.471 = f32[2,256,3,1024]{1,3,2,0:T(8,128)} copy(f32[2,256,3,1024]{3,0,2,1:T(2,128)} %all-gather.2.cloned.1.call-done) | data formatting | bytes 12582912 | tf_op jit(solution)/shard_map/while | solution.py:125
  461.0 250.6 %while.10 = (s32[]{:T(128)}, f32[8,256,2,2,64]{1,4,3,2,0:T(8,128)}, f32[8,1024]{1,0:T(8,128)}, f32[2,256,3,1024]{1,3,2,0:T(8,128)}, f32[8,1024]{1,0:T(8,128)S(1)}, /*index=5*/f32[2,2,64,6144]{3,2,1,0:T(8,128)}, s32[]{:T(128)}) while((s32[]{:T(128)}, f32[8,256,2,2,64]{1,4,3,2,0:T(8,128)}, f32[8,1024]{1,0:T(8,128)}, ...), condition=%wide.region_13.14_spmd, body=%wide.region_12.13_spmd.sunk | while | flops 4838129664 | bytes 50717264 | solution.py:125
  461.8 6.4 fusion.220
  477.0 15.3 %fusion.221 = f32[8,256,2,2,64]{1,4,3,2,0:T(8,128)} fusion(f32[8,256,2,2,64]{1,4,3,2,0:T(8,128)} %get-tuple-element.986, s32[]{:T(128)} %get-tuple-element.985, f32[2,2,64,6144]{3,2,1,0:T(8,128)} %get-tuple-element.997, f32[256,3072]{1,0:T(8,128)S(1)} %get-tuple-element.976, f32[256,3072]{1,0:T(8,128)S(1)} %get-tuple-element.977), kind=kOutput, calls=%fused_computation.167.clone.1 | convolution fusion | flops 4833411072 | bytes 12845568 | tf_op jit(solution)/shard_map/while/body/eval_jaxpr/ik,dcjk->idcj/dot_general | solution.py:123
  493.1 6.4 fusion.220
  508.3 15.3 %fusion.221 = f32[8,256,2,2,64]{1,4,3,2,0:T(8,128)} fusion(f32[8,256,2,2,64]{1,4,3,2,0:T(8,128)} %get-tuple-element.986, s32[]{:T(128)} %get-tuple-element.985, f32[2,2,64,6144]{3,2,1,0:T(8,128)} %get-tuple-element.997, f32[256,3072]{1,0:T(8,128)S(1)} %get-tuple-element.976, f32[256,3072]{1,0:T(8,128)S(1)} %get-tuple-element.977), kind=kOutput, calls=%fused_computation.167.clone.1 | convolution fusion | flops 4833411072 | bytes 12845568 | tf_op jit(solution)/shard_map/while/body/eval_jaxpr/ik,dcjk->idcj/dot_general | solution.py:123
  524.4 6.4 fusion.220
  539.7 15.3 %fusion.221 = f32[8,256,2,2,64]{1,4,3,2,0:T(8,128)} fusion(f32[8,256,2,2,64]{1,4,3,2,0:T(8,128)} %get-tuple-element.986, s32[]{:T(128)} %get-tuple-element.985, f32[2,2,64,6144]{3,2,1,0:T(8,128)} %get-tuple-element.997, f32[256,3072]{1,0:T(8,128)S(1)} %get-tuple-element.976, f32[256,3072]{1,0:T(8,128)S(1)} %get-tuple-element.977), kind=kOutput, calls=%fused_computation.167.clone.1 | convolution fusion | flops 4833411072 | bytes 12845568 | tf_op jit(solution)/shard_map/while/body/eval_jaxpr/ik,dcjk->idcj/dot_general | solution.py:123
  555.8 6.4 fusion.220
  571.0 15.3 %fusion.221 = f32[8,256,2,2,64]{1,4,3,2,0:T(8,128)} fusion(f32[8,256,2,2,64]{1,4,3,2,0:T(8,128)} %get-tuple-element.986, s32[]{:T(128)} %get-tuple-element.985, f32[2,2,64,6144]{3,2,1,0:T(8,128)} %get-tuple-element.997, f32[256,3072]{1,0:T(8,128)S(1)} %get-tuple-element.976, f32[256,3072]{1,0:T(8,128)S(1)} %get-tuple-element.977), kind=kOutput, calls=%fused_computation.167.clone.1 | convolution fusion | flops 4833411072 | bytes 12845568 | tf_op jit(solution)/shard_map/while/body/eval_jaxpr/ik,dcjk->idcj/dot_general | solution.py:123
  587.1 6.4 fusion.220
  602.3 15.3 %fusion.221 = f32[8,256,2,2,64]{1,4,3,2,0:T(8,128)} fusion(f32[8,256,2,2,64]{1,4,3,2,0:T(8,128)} %get-tuple-element.986, s32[]{:T(128)} %get-tuple-element.985, f32[2,2,64,6144]{3,2,1,0:T(8,128)} %get-tuple-element.997, f32[256,3072]{1,0:T(8,128)S(1)} %get-tuple-element.976, f32[256,3072]{1,0:T(8,128)S(1)} %get-tuple-element.977), kind=kOutput, calls=%fused_computation.167.clone.1 | convolution fusion | flops 4833411072 | bytes 12845568 | tf_op jit(solution)/shard_map/while/body/eval_jaxpr/ik,dcjk->idcj/dot_general | solution.py:123
  618.4 6.4 fusion.220
  633.7 15.3 %fusion.221 = f32[8,256,2,2,64]{1,4,3,2,0:T(8,128)} fusion(f32[8,256,2,2,64]{1,4,3,2,0:T(8,128)} %get-tuple-element.986, s32[]{:T(128)} %get-tuple-element.985, f32[2,2,64,6144]{3,2,1,0:T(8,128)} %get-tuple-element.997, f32[256,3072]{1,0:T(8,128)S(1)} %get-tuple-element.976, f32[256,3072]{1,0:T(8,128)S(1)} %get-tuple-element.977), kind=kOutput, calls=%fused_computation.167.clone.1 | convolution fusion | flops 4833411072 | bytes 12845568 | tf_op jit(solution)/shard_map/while/body/eval_jaxpr/ik,dcjk->idcj/dot_general | solution.py:123
  649.8 6.4 fusion.220
  665.0 15.3 %fusion.221 = f32[8,256,2,2,64]{1,4,3,2,0:T(8,128)} fusion(f32[8,256,2,2,64]{1,4,3,2,0:T(8,128)} %get-tuple-element.986, s32[]{:T(128)} %get-tuple-element.985, f32[2,2,64,6144]{3,2,1,0:T(8,128)} %get-tuple-element.997, f32[256,3072]{1,0:T(8,128)S(1)} %get-tuple-element.976, f32[256,3072]{1,0:T(8,128)S(1)} %get-tuple-element.977), kind=kOutput, calls=%fused_computation.167.clone.1 | convolution fusion | flops 4833411072 | bytes 12845568 | tf_op jit(solution)/shard_map/while/body/eval_jaxpr/ik,dcjk->idcj/dot_general | solution.py:123
  681.1 6.4 fusion.220
  696.3 15.3 %fusion.221 = f32[8,256,2,2,64]{1,4,3,2,0:T(8,128)} fusion(f32[8,256,2,2,64]{1,4,3,2,0:T(8,128)} %get-tuple-element.986, s32[]{:T(128)} %get-tuple-element.985, f32[2,2,64,6144]{3,2,1,0:T(8,128)} %get-tuple-element.997, f32[256,3072]{1,0:T(8,128)S(1)} %get-tuple-element.976, f32[256,3072]{1,0:T(8,128)S(1)} %get-tuple-element.977), kind=kOutput, calls=%fused_computation.167.clone.1 | convolution fusion | flops 4833411072 | bytes 12845568 | tf_op jit(solution)/shard_map/while/body/eval_jaxpr/ik,dcjk->idcj/dot_general | solution.py:123
  718.0 6.6 reshape.4513
  724.6 41.8 %reduce-scatter.4.cloned.1.call-done = f32[64,2048]{1,0:T(8,128)} async-done(((f32[256,2048]{1,0:T(8,128)}), f32[64,2048]{1,0:T(8,128)}) %reduce-scatter.4.cloned.1.call-update) | async-done | bytes 524304
  (649 shorter events, 337.1 us)
Async XLA Ops:
  6.5 4.1 copy-start.65
  6.5 444.3 %all-gather.2.cloned.1.call-start = ((), (), s32[]{:S(2)}) async-start(), calls=%async_computation.1 | async-start | bytes 7864320 | tf_op jit(solution)/shard_map/all_gather | solution.py:184
  9.2 40.2 %collective-permute-start = (f32[2,64,3,512]{3,1,2,0:T(8,128)}, f32[2,64,3,512]{3,1,2,0:T(8,128)S(1)}, u32[]{:S(2)}, u32[]{:S(2)}) collective-permute-start(f32[2,64,3,512]{3,1,2,0:T(8,128)} %get-tuple-element.710), channel_id=1, source_target_pairs={{0,4},{4,8},{8,12},{12,0},{1,5},{5,9},{9,13},{13,1},{2,6},{6,10},{... | collective-permute-start | bytes 2359304 | tf_op jit(solution)/shard_map/ppermute | solution.py:29
  10.5 38.9 %collective-permute-start.1 = (f32[2,64,3,512]{3,1,2,0:T(8,128)}, f32[2,64,3,512]{3,1,2,0:T(8,128)}, u32[]{:S(2)}, u32[]{:S(2)}) collective-permute-start(f32[2,64,3,512]{3,1,2,0:T(8,128)} %get-tuple-element.711), channel_id=1, source_target_pairs={{4,0},{8,4},{12,8},{0,12},{5,1},{9,5},{13,9},{1,13},{6,2},{10,6},{... | collective-permute-start | bytes 2359304 | tf_op jit(solution)/shard_map/ppermute | solution.py:30
  10.7 34.9 %collective-permute-start.2 = (f32[2,3,3,512]{3,0,2,1:T(2,128)S(1)}, f32[2,3,3,512]{3,0,2,1:T(2,128)S(1)}, u32[]{:S(2)}, u32[]{:S(2)}) collective-permute-start(f32[2,3,3,512]{3,0,2,1:T(2,128)S(1)} %slice_bitcast_fusion.147), channel_id=1, source_target_pairs={{0,4},{4,8},{8,12},{12,0},{1,5},{5,9},{9,13},{13,1},{2,6},{6,10},{... | collective-permute-start | bytes 110600 | tf_op jit(solution)/shard_map/ppermute | solution.py:19
  13.9 35.5 %copy-start.15 = (f32[2,3,3,2,512]{4,3,0,2,1:T(2,128)}, f32[2,3,3,2,512]{4,3,0,2,1:T(2,128)S(1)}, u32[]{:S(2)}) copy-start(f32[2,3,3,2,512]{4,3,0,2,1:T(2,128)S(1)} %squeeze.345) | copy-start | bytes 221188
  13.9 35.5 %copy-start = (f32[2,64,3,1024]{3,1,2,0:T(8,128)S(1)}, f32[2,64,3,1024]{3,1,2,0:T(8,128)}, u32[]{:S(2)}) copy-start(f32[2,64,3,1024]{3,1,2,0:T(8,128)} %param.18) | copy-start | bytes 4718596
  15.4 34.0 %copy-start.63 = (f32[2,3,3,2,512]{4,3,0,2,1:T(2,128)}, f32[2,3,3,2,512]{4,3,0,2,1:T(2,128)S(1)}, u32[]{:S(2)}) copy-start(f32[2,3,3,2,512]{4,3,0,2,1:T(2,128)S(1)} %squeeze.327) | copy-start | bytes 221188
  45.7 3.8 copy-start.68
  88.2 3.4 copy-start.9
  92.7 18.3 %collective-permute-start.3 = (f32[2,64,3,512]{3,1,2,0:T(8,128)S(1)}, f32[2,64,3,512]{3,1,2,0:T(8,128)S(1)}, u32[]{:S(2)}, u32[]{:S(2)}) collective-permute-start(f32[2,64,3,512]{3,1,2,0:T(8,128)S(1)} %get-tuple-element.704), channel_id=1, source_target_pairs={{0,4},{4,8},{8,12},{12,0},{1,5},{5,9},{9,13},{13,1},{2,6},{6,10},{... | collective-permute-start | bytes 2359304 | tf_op jit(solution)/shard_map/ppermute | solution.py:29
  92.7 34.3 %collective-permute-start.4 = (f32[2,64,3,512]{3,1,2,0:T(8,128)S(1)}, f32[2,64,3,512]{3,1,2,0:T(8,128)S(1)}, u32[]{:S(2)}, u32[]{:S(2)}) collective-permute-start(f32[2,64,3,512]{3,1,2,0:T(8,128)S(1)} %get-tuple-element.705), channel_id=1, source_target_pairs={{4,0},{8,4},{12,8},{0,12},{5,1},{9,5},{13,9},{1,13},{6,2},{10,6},{... | collective-permute-start | bytes 2359304 | tf_op jit(solution)/shard_map/ppermute | solution.py:30
  165.5 3.4 copy-start.5
  165.5 3.4 copy-start.1
  169.9 17.8 %collective-permute-start.5 = (f32[2,64,3,512]{3,1,2,0:T(8,128)S(1)}, f32[2,64,3,512]{3,1,2,0:T(8,128)S(1)}, u32[]{:S(2)}, u32[]{:S(2)}) collective-permute-start(f32[2,64,3,512]{3,1,2,0:T(8,128)S(1)} %get-tuple-element.698), channel_id=1, source_target_pairs={{0,4},{4,8},{8,12},{12,0},{1,5},{5,9},{9,13},{13,1},{2,6},{6,10},{... | collective-permute-start | bytes 2359304 | tf_op jit(solution)/shard_map/ppermute | solution.py:29
  173.0 36.1 %collective-permute-start.6 = (f32[2,64,3,512]{3,1,2,0:T(8,128)S(1)}, f32[2,64,3,512]{3,1,2,0:T(8,128)S(1)}, u32[]{:S(2)}, u32[]{:S(2)}) collective-permute-start(f32[2,64,3,512]{3,1,2,0:T(8,128)S(1)} %get-tuple-element.699), channel_id=1, source_target_pairs={{4,0},{8,4},{12,8},{0,12},{5,1},{9,5},{13,9},{1,13},{6,2},{10,6},{... | collective-permute-start | bytes 2359304 | tf_op jit(solution)/shard_map/ppermute | solution.py:30
  247.6 3.4 copy-start.10
  247.6 3.4 copy-start.12
  251.4 18.7 %collective-permute-start.7 = (f32[2,64,3,512]{3,1,2,0:T(8,128)S(1)}, f32[2,64,3,512]{3,1,2,0:T(8,128)S(1)}, u32[]{:S(2)}, u32[]{:S(2)}) collective-permute-start(f32[2,64,3,512]{3,1,2,0:T(8,128)S(1)} %get-tuple-element.692), channel_id=1, source_target_pairs={{0,4},{4,8},{8,12},{12,0},{1,5},{5,9},{9,13},{13,1},{2,6},{6,10},{... | collective-permute-start | bytes 2359304 | tf_op jit(solution)/shard_map/ppermute | solution.py:29
  251.5 36.0 %collective-permute-start.8 = (f32[2,64,3,512]{3,1,2,0:T(8,128)S(1)}, f32[2,64,3,512]{3,1,2,0:T(8,128)S(1)}, u32[]{:S(2)}, u32[]{:S(2)}) collective-permute-start(f32[2,64,3,512]{3,1,2,0:T(8,128)S(1)} %get-tuple-element.693), channel_id=1, source_target_pairs={{4,0},{8,4},{12,8},{0,12},{5,1},{9,5},{13,9},{1,13},{6,2},{10,6},{... | collective-permute-start | bytes 2359304 | tf_op jit(solution)/shard_map/ppermute | solution.py:30
  326.0 3.4 copy-start.2
  326.0 3.4 copy-start.6
  326.0 3.4 copy-start.8
  332.4 2.6 copy-start.16
  332.4 2.6 copy-start.71
  332.5 433.9 %reduce-scatter.4.cloned.1.call-start = ((), (), s32[]{:S(2)}) async-start(), calls=%async_computation.2 | async-start | bytes 2621440
  335.8 2.6 copy-start.64
  335.8 2.6 copy-start.69
  336.0 19.3 %collective-permute-start.10 = (f32[2,64,3,512]{3,1,2,0:T(8,128)S(1)}, f32[2,64,3,512]{3,1,2,0:T(8,128)S(1)}, u32[]{:S(2)}, u32[]{:S(2)}) collective-permute-start(f32[2,64,3,512]{3,1,2,0:T(8,128)S(1)} %get-tuple-element.687), channel_id=1, source_target_pairs={{4,0},{8,4},{12,8},{0,12},{5,1},{9,5},{13,9},{1,13},{6,2},{10,6},{... | collective-permute-start | bytes 2359304 | tf_op jit(solution)/shard_map/ppermute | solution.py:30
  337.2 34.9 %collective-permute-start.9 = (f32[2,64,3,512]{3,1,2,0:T(8,128)S(1)}, f32[2,64,3,512]{3,1,2,0:T(8,128)S(1)}, u32[]{:S(2)}, u32[]{:S(2)}) collective-permute-start(f32[2,64,3,512]{3,1,2,0:T(8,128)S(1)} %get-tuple-element.686), channel_id=1, source_target_pairs={{0,4},{4,8},{8,12},{12,0},{1,5},{5,9},{9,13},{13,1},{2,6},{6,10},{... | collective-permute-start | bytes 2359304 | tf_op jit(solution)/shard_map/ppermute | solution.py:29
  382.4 3.0 copy-start.77
  385.4 3.8 copy-start.82
  (64 other events, 57.3 us)
Sparse Core Ops, SparseCore 0:
  332.6 47.4 all-gather.1
  724.7 41.6 reduce-scatter.3
where the time goes:
time: 786 us; the launch traced here: 776 us
  local copies, waits for them, and re-layouts  273 us (35%)
  waiting for transfers between devices  205 us (26%)
  other arithmetic  126 us (16%)
  matrix products  122 us (16%)
  loops' own time  19.8 us (3%)
  between operations  18.1 us (2%)
  starting transfers between devices  10.9 us (1%)
    dot_general x8, matrix products, one_momentum(): jnp.einsum('ik,dcjk->idcj', left_flat, right_mat, precision=lax.Precision...  122 us
    ppermute x5, waiting for transfers between devices, extended(): after = lax.ppermute(first, axis, down)  71.6 us
    ppermute x5, waiting for transfers between devices, extended(): before = lax.ppermute(last, axis, up)  64.9 us
    slice x8, local copies, waits for them, and re-layouts, twist_left(): twisted_real = cos_row * left_field[0] - sin_row * left_field[1]  51.1 us
    squeeze x16, local copies, waits for them, and re-layouts, twist_left(): twisted_real = cos_row * left_field[0] - sin_row * left_field[1]  48.1 us
    unnamed x3, waiting for transfers between devices  41.8 us
    unnamed x358, local copies, waits for them, and re-layouts  34.1 us
    select_n x10, other arithmetic, roll_depth(): return jnp.where(at_edge, wrapped, plain)  32.2 us
  transfers between devices with their start and end apart: 13, of which 10 were waited for; matrix products, arithmetic and copies ran while one was open for 9% of the time, Pallas kernels for 0%

commit v1 on v0

v1 whole, which is shorter than its diff:
```python
import functools
import math

import jax
import jax.numpy as jnp
from jax import lax
from jax.experimental import pallas as pl
from jax.experimental.pallas import tpu as pltpu
from jax.sharding import PartitionSpec as P

LY = 16
LZ = 32
ITERS = 4
LANES = 128
PLANE = LY * LZ
QP = PLANE // LANES
YLO = LANES // LZ

hop_scale = 0.125


def piece_coords(mode, tile, tiles, k, lane):
    wy = (LY // tiles) * LZ
    bz = LZ // tiles
    if mode == 0:
        site = k * LANES + lane
        return site // PLANE, site % PLANE // LZ, site % LZ
    if mode == 1:
        flat = k * LANES + lane
        return flat // wy, tile * (LY // tiles) + flat % wy // LZ, lane % LZ
    slot = k * tiles + (lane % LZ) // bz
    return slot // QP, YLO * (slot % QP) + lane // LZ, tile * bz + lane % bz


def piece_index(mode, tile, tiles, x, y, z):
    wy = (LY // tiles) * LZ
    bz = LZ // tiles
    if mode == 0:
        site = x * PLANE + y * LZ + z
        return site // LANES, site % LANES
    if mode == 1:
        flat = x * wy + (y - tile * (LY // tiles)) * LZ + z
        return flat // LANES, flat % LANES
    slot = x * QP + y // YLO
    return slot // tiles, (y % YLO) * LZ + (slot % tiles) * bz + (z - tile * bz)


def pack_piece(mode, tiles, tile, read, write, kt):
    lane = lax.broadcasted_iota(jnp.int32, (1, LANES), 1)
    if mode == 0:
        for k in range(kt):
            write(k, read(tile * kt + k))
    elif mode == 1:
        wy = (LY // tiles) * LZ
        if wy >= LANES:
            per = wy // LANES
            for k in range(kt):
                write(k, read((k // per) * QP + tile * per + k % per))
        else:
            nx = LANES // wy
            row = (tile * wy) // LANES
            off = (tile * wy) % LANES
            for k in range(kt):
                out = None
                for j in range(nx):
                    part = pltpu.roll(read((k * nx + j) * QP + row), lax.rem(w_shift(wy * j - off), LANES), 1)
                    out = part if out is None else jnp.where(lane // wy == j, part, out)
                write(k, out)
    else:
        bz = LZ // tiles
        for k in range(kt):
            out = None
            for slot in range(tiles):
                index = k * tiles + slot
                part = pltpu.roll(read(index), lax.rem(w_shift((slot - tile) * bz), LANES), 1)
                out = part if out is None else jnp.where((lane % LZ) // bz == slot, part, out)
            write(k, out)


def w_shift(shift):
    return shift + 2 * LANES


def filter_kernel(tiles, kt, scal, field_ref, link_ref, piece_ref, glink_ref, a_ref, b_ref, l_ref):
    comps = 6
    nt = tiles * kt
    lx = nt // QP
    lane = lax.broadcasted_iota(jnp.int32, (1, LANES), 1)
    depth = lane % LZ
    rows = field_ref.shape[2]

    def at(x, q):
        return x * QP + q

    def moved(get, n, axis, step):
        x, q = n // QP, lax.rem(n, QP)
        if axis == 0:
            return get(at(lax.rem(x + step + lx, lx), q))
        if axis == 1:
            here, there = get(n), get(at(x, lax.rem(q + step + QP, QP)))
            if step > 0:
                return rolled(jnp.where(lane < LZ, there, here), LANES - LZ)
            return rolled(jnp.where(lane >= LANES - LZ, there, here), LZ)
        here = get(n)
        if step > 0:
            return jnp.where(depth == LZ - 1, rolled(here, LZ - 1), rolled(here, LANES - 1))
        return jnp.where(depth == 0, rolled(here, LANES - LZ + 1), rolled(here, 1))

    def rolled(value, shift):
        return pltpu.roll(value, shift, value.ndim - 1)

    def load_slab(t, carry):
        for k in range(kt):
            for c in range(comps):
                a_ref[t * kt + k, c] = field_ref[t, c, :, k * LANES : (k + 1) * LANES]
            for m in range(3):
                l_ref[m, t * kt + k] = link_ref[t, m, :, k * LANES : (k + 1) * LANES]
        return carry

    lax.fori_loop(0, tiles, load_slab, 0)

    def shift_links(n, carry):
        for m in range(3):
            l_ref[3 + m, n] = moved(lambda i: l_ref[m, i], n, m, -1)
        return carry

    lax.fori_loop(0, nt, shift_links, 0)

    def hop(src, n):
        acc = [None] * comps
        for m in range(3):
            for side in (0, 1):
                near = [moved(lambda i: src[i, c], n, m, 1 - 2 * side) for c in range(comps)]
                for i in range(3):
                    for j in range(3):
                        row = i * 3 + j if side == 0 else j * 3 + i
                        lr = l_ref[3 * side + m, n, row : row + 1, :]
                        li = l_ref[3 * side + m, n, 9 + row : 10 + row, :]
                        fr, fi = near[j], near[3 + j]
                        if side == 0:
                            re = lr * fr - li * fi
                            im = lr * fi + li * fr
                        else:
                            re = lr * fr + li * fi
                            im = lr * fi - li * fr
                        acc[i] = re if acc[i] is None else acc[i] + re
                        acc[3 + i] = im if acc[3 + i] is None else acc[3 + i] + im
        return acc

    src, dst = a_ref, b_ref
    for order in range(ITERS):

        def body(n, carry, src=src, dst=dst, order=order):
            acc = hop(src, n)
            for c in range(comps):
                if order == 0:
                    dst[n, c] = hop_scale * acc[c]
                else:
                    dst[n, c] = (2.0 * hop_scale) * acc[c] - dst[n, c]
            return carry

        lax.fori_loop(0, nt, body, 0)
        src, dst = dst, src

    slots = glink_ref.shape[0]
    mine = scal[1]
    for mode in range(3):

        @pl.when(scal[0] == mode)
        def _():
            def one_piece(t, carry):
                for c in range(comps):

                    def write(k, value, c=c):
                        piece_ref[t, k, c] = value

                    pack_piece(mode, tiles, t, lambda n, c=c: src[n, c], write, kt)
                return carry

            lax.fori_loop(0, tiles, one_piece, 0)
            for slot in range(slots):

                def write(k, value, slot=slot):
                    glink_ref[slot, k] = value

                pack_piece(mode, tiles, mine, lambda n, slot=slot: l_ref[scal[2 + slot], n], write, kt)


def contract_kernel(
    nvt, slots, moms, norm, scal, left_ref, own_ref, trig_ref, glink_ref, index_ref, out_ref, whi, wlo, dhi, dlo, acc_ref
):
    k = pl.program_id(0)
    vecs, tiles = left_ref.shape[0], left_ref.shape[1]
    rows = vecs * tiles * nvt
    cols = tiles * nvt
    comps = 6
    kt = pl.num_programs(0)

    def split(value):
        high = value.astype(jnp.bfloat16)
        return high, (value - high.astype(jnp.float32)).astype(jnp.bfloat16)

    for v in range(vecs):
        for t in range(tiles):
            base = (v * tiles + t) * nvt
            for c in range(3):
                rh, rl = split(left_ref[v, t, 0, c])
                ih, il = split(left_ref[v, t, 0, 3 + c])
                for ref, re, im in ((whi, rh, ih), (wlo, rl, il)):
                    ref[base : base + nvt, c * LANES : (c + 1) * LANES] = re
                    ref[base : base + nvt, (3 + c) * LANES : (4 + c) * LANES] = im
                    ref[rows + base : rows + base + nvt, c * LANES : (c + 1) * LANES] = -im
                    ref[rows + base : rows + base + nvt, (3 + c) * LANES : (4 + c) * LANES] = re

    for slot in range(slots):
        ka, kb = scal[slot, k], scal[slot, kt + k]
        forward = scal[slot, 2 * kt] > 0
        sign = jnp.where(forward, 1.0, -1.0)
        lanes = jnp.broadcast_to(index_ref[slot, k, 0:1, :], (nvt, LANES))
        take_b = jnp.broadcast_to(index_ref[slot, k, 1:2, :], (nvt, LANES)) > 0
        link = []
        for i in range(3):
            for j in range(3):
                row = jnp.where(forward, i * 3 + j, j * 3 + i)
                link.append((glink_ref[slot, k, pl.ds(row, 1), :], sign * glink_ref[slot, k, pl.ds(9 + row, 1), :]))
        for t in range(tiles):
            near = []
            for c in range(comps):
                first = jnp.take_along_axis(own_ref[t, ka, c], lanes, axis=1)
                second = jnp.take_along_axis(own_ref[t, kb, c], lanes, axis=1)
                near.append(jnp.where(take_b, second, first))
            for i in range(3):
                dr, di = 0.0, 0.0
                for j in range(3):
                    lr, li = link[i * 3 + j]
                    dr = dr + lr * near[j] - li * near[3 + j]
                    di = di + lr * near[3 + j] + li * near[j]
                for p in range(moms):
                    co = trig_ref[k, p : p + 1, :]
                    si = trig_ref[k, moms + p : moms + p + 1, :]
                    base = ((slot * moms + p) * tiles + t) * nvt
                    for half, value in ((0, co * dr + si * di), (1, co * di - si * dr)):
                        high, low = split(value)
                        at = (half * 3 + i) * LANES
                        dhi[base : base + nvt, at : at + LANES] = high
                        dlo[base : base + nvt, at : at + LANES] = low

    step = 256

    @pl.when(k == 0)
    def _():
        acc_ref[...] = jnp.zeros_like(acc_ref)

    def mul(m, carry):
        at = pl.ds(pl.multiple_of(m * step, step), step)
        dims = (((1,), (1,)), ((), ()))
        dot = functools.partial(lax.dot_general, dimension_numbers=dims, preferred_element_type=jnp.float32)
        acc_ref[at, :] += dot(dhi[at, :], whi[...]) + (dot(dhi[at, :], wlo[...]) + dot(dlo[at, :], whi[...]))
        return carry

    lax.fori_loop(0, acc_ref.shape[0] // step, mul, 0)

    @pl.when(k == kt - 1)
    def _():
        per = moms * cols
        for slot in range(slots):
            for part in range(2):
                block = acc_ref[slot * per : (slot + 1) * per, part * rows : (part + 1) * rows]
                at = (slot * 2 + part) * per
                out_ref[:, at : at + per] = norm * block.T


def local(vectors, links, momenta, directions):
    nv = vectors.shape[1]
    sites = vectors.shape[3]
    tiles = lax.axis_size("tile")
    vecs = lax.axis_size("vec")
    tile = lax.axis_index("tile")
    slots = directions.shape[0]
    moms = momenta.shape[0]
    nvt = nv // tiles
    kt = sites // LANES
    nt = kt * tiles
    extent_x = sites * tiles // PLANE
    norm = 1.0 / math.sqrt(3.0 * sites * tiles)
    f32 = jnp.float32

    gauge = lax.all_gather(links.reshape(3, 18, sites), "tile", axis=0)
    field = jnp.transpose(vectors, (0, 2, 1, 3)).reshape(6, tiles, nvt, sites)
    field = lax.all_to_all(jnp.transpose(field, (1, 0, 2, 3)), "tile", 0, 0)

    heading = directions % 3
    uses_y = jnp.any(heading == 1)
    uses_x = jnp.any(heading == 0)
    mode = jnp.where(uses_y, jnp.where(uses_x, 2, 0), 1).astype(jnp.int32)

    scal = jnp.concatenate([jnp.stack([mode, tile.astype(jnp.int32)]), directions.astype(jnp.int32)])
    smem = pl.BlockSpec(memory_space=pltpu.SMEM)
    vmem = pl.BlockSpec(memory_space=pltpu.VMEM)
    piece, glink = pl.pallas_call(
        functools.partial(filter_kernel, tiles, kt),
        out_shape=(
            jax.ShapeDtypeStruct((tiles, kt, 6, nvt, LANES), f32),
            jax.ShapeDtypeStruct((slots, kt, 18, LANES), f32),
        ),
        in_specs=[smem, vmem, vmem],
        out_specs=(vmem, vmem),
        scratch_shapes=[
            pltpu.VMEM((nt, 6, nvt, LANES), f32),
            pltpu.VMEM((nt, 6, nvt, LANES), f32),
            pltpu.VMEM((6, nt, 18, LANES), f32),
        ],
        compiler_params=pltpu.CompilerParams(vmem_limit_bytes=48 << 20),
        name="chebyshev",
    )(scal, field, gauge)

    own = lax.all_to_all(piece, "tile", 0, 0)
    left = lax.all_gather(own, "vec", axis=0)

    k = jnp.arange(kt, dtype=jnp.int32)[:, None]
    lane = jnp.arange(LANES, dtype=jnp.int32)[None]

    def pick(options):
        return jnp.where(mode == 0, options[0], jnp.where(mode == 1, options[1], options[2]))

    coords = [piece_coords(m, tile, tiles, k, lane) for m in range(3)]
    x, y, z = (pick([jnp.broadcast_to(c[axis], (kt, LANES)) for c in coords]) for axis in range(3))
    start_x = jnp.where(mode == 0, tile * (sites // PLANE), 0)

    def part(axis, coord, extent):
        return jnp.mod(momenta[:, axis, None, None] * coord[None], extent).astype(f32) / extent

    angle = 2.0 * math.pi * (part(0, x + start_x, extent_x) + part(1, y, LY) + part(2, z, LZ))
    trig = jnp.transpose(jnp.concatenate([jnp.cos(angle), jnp.sin(angle)]), (1, 0, 2))

    index, spots = [], []
    for slot in range(slots):
        d = directions[slot]
        step = jnp.where(d < 3, 1, -1)
        xs = jnp.mod(x + jnp.where(heading[slot] == 0, step, 0), extent_x)
        ys = jnp.mod(y + jnp.where(heading[slot] == 1, step, 0), LY)
        zs = jnp.mod(z + jnp.where(heading[slot] == 2, step, 0), LZ)
        found = [piece_index(m, tile, tiles, xs, ys, zs) for m in range(3)]
        ks, ls = (pick([f[i] for f in found]) for i in range(2))
        ka, kb = jnp.min(ks, axis=1), jnp.max(ks, axis=1)
        index.append(jnp.stack([ls, (ks == kb[:, None]).astype(jnp.int32)], axis=1))
        spots.append(jnp.concatenate([ka, kb, (d < 3).astype(jnp.int32)[None]]))
    index, spots = jnp.stack(index), jnp.stack(spots).astype(jnp.int32)

    rows, cols = nv * vecs, nv
    bf16 = jnp.bfloat16
    partial_rows = pl.pallas_call(
        functools.partial(contract_kernel, nvt, slots, moms, norm),
        grid=(kt,),
        out_shape=jax.ShapeDtypeStruct((rows, slots * 2 * moms * cols), f32),
        in_specs=[
            smem,
            pl.BlockSpec((vecs, tiles, 1, 6, nvt, LANES), lambda i: (0, 0, i, 0, 0, 0)),
            vmem,
            vmem,
            vmem,
            vmem,
        ],
        out_specs=vmem,
        scratch_shapes=[
            pltpu.VMEM((2 * rows, 6 * LANES), bf16),
            pltpu.VMEM((2 * rows, 6 * LANES), bf16),
            pltpu.VMEM((slots * moms * cols, 6 * LANES), bf16),
            pltpu.VMEM((slots * moms * cols, 6 * LANES), bf16),
            pltpu.VMEM((slots * moms * cols, 2 * rows), f32),
        ],
        compiler_params=pltpu.CompilerParams(vmem_limit_bytes=48 << 20),
        name="contract",
    )(spots, left, own, trig, glink, index)
    mine = lax.psum_scatter(partial_rows, "tile", scatter_dimension=0, tiled=True)
    return mine.reshape(nv * vecs // tiles, slots, 2, moms, cols)


def solution(mesh):
    return jax.shard_map(
        local,
        mesh=mesh,
        in_specs=(
            P(None, "vec", None, ("groups", "tile")),
            P(None, None, None, None, ("groups", "tile")),
            P(),
            P(),
        ),
        out_specs=P(("groups", "tile"), None, None, None, "vec"),
        check_vma=False,
    )
```

time: 786 us -> 274 us (0.35)
  local copies, waits for them, and re-layouts: 273 us -> 7.97 us
  other arithmetic: 126 us -> 2.21 us
  matrix products: 122 us -> 0 us
  waiting for transfers between devices: 205 us -> 83 us
  blocking collectives: 0 us -> 87.7 us
  Pallas kernels: 0 us -> 65.1 us
  loops' own time: 19.8 us -> 0 us
    ppermute x11 -> x0, waiting for transfers between devices: 164 us -> none  [the longest x5 71.6 us: extended(): after = lax.ppermute(first, axis, down)]
    slice x99 -> x2, local copies, waits for them, and re-layouts: 126 us -> 1.2 us  [the longest x1 0.64 us: local(): xs = jnp.mod(x + jnp.where(heading[slot] == 0, step, 0), extent_x)]
    dot_general x8 -> x0, matrix products: 122 us -> none  [one_momentum(): jnp.einsum('ik,dcjk->idcj', left_flat, right_mat, precision=lax.Precision...]
    pallas_call x0 -> x2, Pallas kernels: none -> 65.1 us  [the longest x1 38.2 us: local(): pl.pallas_call(functools.partial(contract_kernel, nvt, slots, moms, norm)...]
    squeeze x41 -> x0, local copies, waits for them, and re-layouts: 63.2 us -> none  [the longest x16 48.1 us: twist_left(): twisted_real = cos_row * left_field[0] - sin_row * left_field[1]]
    all_gather x0 -> x1, blocking collectives: none -> 51.6 us  [local(): gauge = lax.all_gather(links.reshape(3, 18, sites), 'tile', axis=0)]
    unnamed x3 -> x2, waiting for transfers between devices: 41.8 us -> 0.03 us
    all_gather x1, waiting for transfers between devices: 0.01 us -> 41.7 us  [local(): left = lax.all_gather(own, 'vec', axis=0)]
  transfers between devices with their start and end apart: 13 -> 3, of which waited for: 10 -> 2; matrix products, arithmetic and copies ran while one was open for 9% -> 1% of each run, Pallas kernels for 0% -> 0%
where the time goes in v1:
time: 274 us; the launch traced here: 271 us
  blocking collectives  87.7 us (32%)
  waiting for transfers between devices  83 us (30%)
  Pallas kernels  65.1 us (24%)
  between operations  19.9 us (7%)
  local copies, waits for them, and re-layouts  7.97 us (3%)
  starting transfers between devices  4.93 us (2%)
    all_gather x1, blocking collectives, local(): gauge = lax.all_gather(links.reshape(3, 18, sites), 'tile', axis=0)  51.6 us
    all_gather x1, waiting for transfers between devices, local(): left = lax.all_gather(own, 'vec', axis=0)  41.7 us
    reduce_scatter x1, waiting for transfers between devices, local(): lax.psum_scatter(partial_rows, 'tile', scatter_dimension=0, tiled=True)  41.2 us
    pallas_call x1, Pallas kernels, local(): pl.pallas_call(functools.partial(contract_kernel, nvt, slots, moms, norm)...  38.2 us
    all_to_all x1, blocking collectives, local(): own = lax.all_to_all(piece, 'tile', 0, 0)  36.1 us
    pallas_call x1, Pallas kernels, local(): pl.pallas_call(functools.partial(filter_kernel, tiles, kt), out_shape=(ja...  26.9 us
  transfers between devices with their start and end apart: 3, of which 2 were waited for; matrix products, arithmetic and copies ran while one was open for 1% of the time, Pallas kernels for 0%

profile of v1, /device:TPU:9, one launch (start us, length us, event | category | flops | bytes accessed | tf_op | source)
XLA Modules:
  0.0 270.8 jit_solution(17188650786396683326)
XLA Ops:
  6.5 2.7 %copy.13 = f32[6,4,16,1024]{3,2,0,1:T(8,128)} copy(f32[6,4,16,1024]{3,2,1,0:T(8,128)} %bitcast.33) | data formatting | bytes 3145728 | tf_op jit(solution)/shard_map/reshape | solution.py:289
  9.3 4.9 %all-to-all-start = ((f32[4,6,16,1024]{3,2,1,0:T(8,128)}), f32[4,6,16,1024]{3,2,1,0:T(8,128)S(1)}, u32[]{:S(2)}, u32[]{:S(2)}) async-start(f32[4,6,16,1024]{3,2,1,0:T(8,128)} %bitcast.31), calls=%async_computation | async-start | bytes 3145728 | tf_op jit(solution)/shard_map/all_to_all | solution.py:290
  14.2 0.0 all-gather.3.cloned.1.call-start
  14.2 0.0 copy-done.2
  14.2 0.1 copy.10
  14.3 0.1 copy.11
  14.4 0.7 compare_reduce_fusion
  16.4 0.1 pad_add_fusion.2.scal
  16.5 51.6 %all_gather.9.link_ref = f32[4,3,18,1024]{3,2,1,0:T(8,128)S(1)} all-gather(f32[1,3,18,1024]{3,2,1,0:T(8,128)S(1)} %copy.11), channel_id=1, replica_groups=mesh['groups'=2,'tile'=4,'vec'=4] {'tile'}, dimensions={0}, use_global_device_ids=true | all-gather | bytes 1105920 | tf_op jit(solution)/shard_map/all_gather | solution.py:288
  68.0 0.0 all-to-all-done.field_ref
  68.0 26.9 %chebyshev.1 = (f32[4,8,6,16,128]{4,3,2,1,0:T(8,128)S(1)}, f32[2,8,18,128]{3,2,1,0:T(8,128)S(1)}) custom-call(s32[4]{0:T(128)S(1)} %pad_add_fusion.2.scal, f32[4,6,16,1024]{3,2,1,0:T(8,128)S(1)} %all-to-all-done.field_ref, f32[4,3,18,1024]{3,2,1,0:T(8,128)S(1)} %all_gather.9.link_ref), custom_call_target="tpu_custom_call" | custom-call | tf_op jit(solution)/shard_map/chebyshev/pallas_call | solution.py:300
  94.9 36.1 %all_to_all.10.own_ref = f32[4,8,6,16,128]{4,3,2,1,0:T(8,128)} all-to-all(f32[4,8,6,16,128]{4,3,2,1,0:T(8,128)S(1)} %get-tuple-element.7), channel_id=1, replica_groups=mesh['groups'=2,'tile'=4,'vec'=4] {'tile'}, dimensions={0} | all-to-all | bytes 3145728 | tf_op jit(solution)/shard_map/all_to_all | solution.py:317
  131.1 0.0 all-gather.3.cloned.1.call-update
  131.1 0.0 reduce-scatter.2.cloned.1.call-start
  131.2 0.6 fusion.91
  132.9 0.6 fusion.90
  137.5 0.1 fusion.28
  137.6 0.1 fusion.88
  137.7 0.1 fusion.89
  137.9 0.1 add_bitcast_fusion.2
  138.0 0.2 and_select_fusion.21
  138.2 0.4 broadcast_select_fusion.9
  138.5 0.1 compare_convert_fusion
  138.7 0.0 copy-done.4
  138.7 0.2 fusion.13
  139.0 41.7 %all-gather.3.cloned.1.call-done = f32[16,8,6,16,128]{4,3,2,1,0:T(8,128)} async-done(((f32[4,8,6,16,128]{4,3,2,1,0:T(8,128)}), f32[16,8,6,16,128]{4,3,2,1,0:T(8,128)}) %all-gather.3.cloned.1.call-update) | async-done | bytes 6291472 | tf_op jit(solution)/shard_map/all_gather | solution.py:318
  180.7 0.0 copy-done
  180.7 38.2 %contract.1 = f32[256,2048]{1,0:T(8,128)S(1)} custom-call(s32[2,17]{1,0:T(2,128)S(1)} %pad_add_fusion.1.scal, f32[4,4,8,6,16,128]{5,4,3,2,1,0:T(8,128)} %bitcast.32, f32[4,8,6,16,128]{4,3,2,1,0:T(8,128)S(1)} %copy-done, f32[8,16,128]{2,1,0:T(8,128)S(1)} %maximum_bitcast_fusion.trig_ref, f32[2,8,18,128]{3,2,1,0:T(8,128)S(1)} %get-tuple-element.8.glink_ref, ...), custom_call_target="tpu_custom_call" | custom-call | tf_op jit(solution)/shard_map/contract/pallas_call | solution.py:352
  219.0 1.3 copy-done.1
  220.3 0.0 reduce-scatter.2.cloned.1.call-update
  220.3 41.2 %reduce-scatter.2.cloned.1.call-done = f32[64,2048]{1,0:T(8,128)} async-done(((f32[256,2048]{1,0:T(8,128)}), f32[64,2048]{1,0:T(8,128)}) %reduce-scatter.2.cloned.1.call-update) | async-done | bytes 524304 | tf_op jit(solution)/shard_map/reduce_scatter | solution.py:375
  261.6 2.4 reshape.2004
  (17 shorter events, 0.1 us)
Async XLA Ops:
  9.3 4.9 %copy-start.2 = (f32[3,2,3,3,1024]{4,1,3,2,0:T(2,128)S(1)}, f32[3,2,3,3,1024]{4,1,3,2,0:T(2,128)}, u32[]{:S(2)}) copy-start(f32[3,2,3,3,1024]{4,1,3,2,0:T(2,128)} %param.5) | copy-start | bytes 663556
  9.3 5.2 %copy-start.3 = (s32[2]{0:T(128)S(1)}, s32[2]{0:T(128)}, u32[]{:S(2)}) copy-start(s32[2]{0:T(128)} %param.7) | copy-start | bytes 28
  9.3 58.7 %all-to-all-start = ((f32[4,6,16,1024]{3,2,1,0:T(8,128)}), f32[4,6,16,1024]{3,2,1,0:T(8,128)S(1)}, u32[]{:S(2)}, u32[]{:S(2)}) async-start(f32[4,6,16,1024]{3,2,1,0:T(8,128)} %bitcast.31), calls=%async_computation | async-start | bytes 3145728 | tf_op jit(solution)/shard_map/all_to_all | solution.py:290
  14.2 166.6 %all-gather.3.cloned.1.call-start = ((), (), s32[]{:S(2)}) async-start(), calls=%async_computation.4 | async-start | bytes 7864320 | tf_op jit(solution)/shard_map/all_gather | solution.py:318
  131.1 7.6 %copy-start.4 = (s32[8,3]{0,1:T(4,128)S(1)}, s32[8,3]{0,1:T(4,128)}, u32[]{:S(2)}) copy-start(s32[8,3]{0,1:T(4,128)} %param.6) | copy-start | bytes 292
  131.1 49.6 %copy-start = (f32[4,8,6,16,128]{4,3,2,1,0:T(8,128)S(1)}, f32[4,8,6,16,128]{4,3,2,1,0:T(8,128)}, u32[]{:S(2)}) copy-start(f32[4,8,6,16,128]{4,3,2,1,0:T(8,128)} %all_to_all.10.own_ref) | copy-start | bytes 4718596
  131.1 130.4 %reduce-scatter.2.cloned.1.call-start = ((), (), s32[]{:S(2)}) async-start(), calls=%async_computation.3 | async-start | bytes 2621440 | tf_op jit(solution)/shard_map/reduce_scatter | solution.py:375
  219.0 1.3 copy-start.1
Sparse Core Ops, SparseCore 0:
  131.2 49.4 all-gather.2
  220.5 41.0 reduce-scatter.1

commit v2 on v1

v2 whole, which is shorter than its diff:
```python
import functools
import math

import jax
import jax.numpy as jnp
from jax import lax
from jax.experimental import pallas as pl
from jax.experimental.pallas import tpu as pltpu
from jax.sharding import PartitionSpec as P

LY = 16
LZ = 32
ITERS = 4
LANES = 128
PLANE = LY * LZ
QP = PLANE // LANES
YLO = LANES // LZ

hop_scale = 0.125


def piece_coords(mode, tile, tiles, k, lane):
    wy = (LY // tiles) * LZ
    bz = LZ // tiles
    if mode == 0:
        site = k * LANES + lane
        return site // PLANE, site % PLANE // LZ, site % LZ
    if mode == 1:
        flat = k * LANES + lane
        return flat // wy, tile * (LY // tiles) + flat % wy // LZ, lane % LZ
    slot = k * tiles + (lane % LZ) // bz
    return slot // QP, YLO * (slot % QP) + lane // LZ, tile * bz + lane % bz


def piece_index(mode, tile, tiles, x, y, z):
    wy = (LY // tiles) * LZ
    bz = LZ // tiles
    if mode == 0:
        site = x * PLANE + y * LZ + z
        return site // LANES, site % LANES
    if mode == 1:
        flat = x * wy + (y - tile * (LY // tiles)) * LZ + z
        return flat // LANES, flat % LANES
    slot = x * QP + y // YLO
    return slot // tiles, (y % YLO) * LZ + (slot % tiles) * bz + (z - tile * bz)


def pack_piece(mode, tiles, tile, read, write, kt):
    lane = lax.broadcasted_iota(jnp.int32, (1, LANES), 1)
    wy = (LY // tiles) * LZ
    bz = LZ // tiles

    def joined(indices, shifts, owner):
        out = None
        for j, (index, shift) in enumerate(zip(indices, shifts)):
            part = pltpu.roll(read(index), lax.rem(shift + 2 * LANES, LANES), 1)
            out = part if out is None else jnp.where(owner == j, part, out)
        return out

    def one(k, carry):
        if mode == 0:
            value = read(tile * kt + k)
        elif mode == 1 and wy >= LANES:
            per = wy // LANES
            value = read((k // per) * QP + tile * per + k % per)
        elif mode == 1:
            nx = LANES // wy
            first = k * nx * QP + (tile * wy) // LANES
            off = (tile * wy) % LANES
            value = joined([first + j * QP for j in range(nx)], [wy * j - off for j in range(nx)], lane // wy)
        else:
            shifts = [(j - tile) * bz for j in range(tiles)]
            value = joined([k * tiles + j for j in range(tiles)], shifts, (lane % LZ) // bz)
        write(k, value)
        return carry

    lax.fori_loop(0, kt, one, 0, unroll=tiles <= 4)


def filter_kernel(tiles, kt, rows, with_links, *refs):
    scal, slab_refs, refs = refs[0], refs[1 : 1 + tiles], refs[1 + tiles :]
    if with_links:
        piece_refs, (glink_ref, l_ref, a_ref, b_ref) = refs[:tiles], refs[tiles:]
    else:
        l_ref, piece_refs, (a_ref, b_ref) = refs[0], refs[1 : 1 + tiles], refs[1 + tiles :]
    mine = scal[1]
    comps = 6
    nt = tiles * kt
    lx = nt // QP
    lane = lax.broadcasted_iota(jnp.int32, (1, LANES), 1)
    depth = lane % LZ

    def at(x, q):
        return x * QP + q

    def moved(get, n, axis, step):
        x, q = n // QP, lax.rem(n, QP)
        if axis == 0:
            return get(at(lax.rem(x + step + lx, lx), q))
        if axis == 1:
            here, there = get(n), get(at(x, lax.rem(q + step + QP, QP)))
            if step > 0:
                return rolled(jnp.where(lane < LZ, there, here), LANES - LZ)
            return rolled(jnp.where(lane >= LANES - LZ, there, here), LZ)
        here = get(n)
        if step > 0:
            return jnp.where(depth == LZ - 1, rolled(here, LZ - 1), rolled(here, LANES - 1))
        return jnp.where(depth == 0, rolled(here, LANES - LZ + 1), rolled(here, 1))

    def rolled(value, shift):
        return pltpu.roll(value, shift, value.ndim - 1)

    for s in range(tiles):
        t = lax.rem(mine - s + tiles, tiles)
        for k in range(kt):
            lanes = slice(k * LANES, (k + 1) * LANES)
            for c in range(comps):
                a_ref[t * kt + k, c] = slab_refs[s][c * rows : (c + 1) * rows, lanes]
            if with_links:
                for m in range(3):
                    first = comps * rows + 18 * m
                    l_ref[m, t * kt + k] = slab_refs[s][first : first + 18, lanes]

    if with_links:

        def shift_links(n, carry):
            for m in range(3):
                l_ref[3 + m, n] = moved(lambda i: l_ref[m, i], n, m, -1)
            return carry

        lax.fori_loop(0, nt, shift_links, 0)

    def hop(src, n):
        acc = [None] * comps
        for m in range(3):
            for side in (0, 1):
                near = [moved(lambda i: src[i, c], n, m, 1 - 2 * side) for c in range(comps)]
                for i in range(3):
                    for j in range(3):
                        row = i * 3 + j if side == 0 else j * 3 + i
                        lr = l_ref[3 * side + m, n, row : row + 1, :]
                        li = l_ref[3 * side + m, n, 9 + row : 10 + row, :]
                        fr, fi = near[j], near[3 + j]
                        if side == 0:
                            re = lr * fr - li * fi
                            im = lr * fi + li * fr
                        else:
                            re = lr * fr + li * fi
                            im = lr * fi - li * fr
                        acc[i] = re if acc[i] is None else acc[i] + re
                        acc[3 + i] = im if acc[3 + i] is None else acc[3 + i] + im
        return acc

    src, dst = a_ref, b_ref
    for order in range(ITERS):

        def body(n, carry, src=src, dst=dst, order=order):
            acc = hop(src, n)
            for c in range(comps):
                if order == 0:
                    dst[n, c] = hop_scale * acc[c]
                else:
                    dst[n, c] = (2.0 * hop_scale) * acc[c] - dst[n, c]
            return carry

        lax.fori_loop(0, nt, body, 0)
        src, dst = dst, src

    for mode in range(3):

        @pl.when(scal[0] == mode)
        def _():
            for s in range(tiles):
                for c in range(comps):

                    def write(k, value, s=s, c=c):
                        piece_refs[s][k, c] = value

                    pack_piece(mode, tiles, lax.rem(mine + s, tiles), lambda n, c=c: src[n, c], write, kt)
            if with_links:
                for slot in range(glink_ref.shape[0]):

                    def write(k, value, slot=slot):
                        glink_ref[slot, k] = value

                    pack_piece(mode, tiles, mine, lambda n, slot=slot: l_ref[scal[2 + slot], n], write, kt)


def contract_kernel(chunks, slots, moms, norm, scal, left_ref, *refs):
    own_refs = refs[:chunks]
    trig_ref, glink_ref, index_ref, out_ref, side, disp, whole, dhi, dlo, acc_ref = refs[chunks:]
    k = pl.program_id(0)
    vecs, tiles, nvc = left_ref.shape[0], left_ref.shape[1], left_ref.shape[4]
    rows = vecs * tiles * nvc
    cols = tiles * nvc * chunks
    comps = 6
    kt = pl.num_programs(0)
    depth = comps * LANES
    group = dhi.shape[1]
    per = group // cols
    half = 3 * LANES

    mine = scal[slots, 0]

    def split(value):
        high = value.astype(jnp.bfloat16)
        return high, (value - high.astype(jnp.float32)).astype(jnp.bfloat16)

    def place(s, outer, count):
        if nvc % 8:
            return (outer * tiles + s) * count
        return pl.multiple_of((outer * tiles + lax.rem(mine - s + tiles, tiles)) * count, 8)

    @pl.when(k == 0)
    def _():
        acc_ref[...] = jnp.zeros_like(acc_ref)

    for v in range(vecs):
        for t in range(tiles):
            at = pl.ds(place(t, v, nvc), nvc)
            for c in range(comps):
                side[at, c * LANES : (c + 1) * LANES] = left_ref[v, t, 0, c]
    for c in range(3):
        rh, rl = split(side[:, c * LANES : (c + 1) * LANES])
        ih, il = split(side[:, half + c * LANES : half + (c + 1) * LANES])
        for third, re, im in ((0, rh, ih), (1, rl, il), (2, rh, ih)):
            first = third * depth + c * LANES
            whole[0:rows, first : first + LANES] = re
            whole[0:rows, first + half : first + half + LANES] = im
            whole[rows : 2 * rows, first : first + LANES] = -im
            whole[rows : 2 * rows, first + half : first + half + LANES] = re

    for slot in range(slots):
        ka, kb = scal[slot, k], scal[slot, kt + k]
        forward = scal[slot, 2 * kt] > 0
        sign = jnp.where(forward, 1.0, -1.0)
        lanes = jnp.broadcast_to(index_ref[slot, k, 0:1, :], (nvc, LANES))
        take_b = jnp.broadcast_to(index_ref[slot, k, 1:2, :], (nvc, LANES)) > 0
        link = []
        for i in range(3):
            for j in range(3):
                row = jnp.where(forward, i * 3 + j, j * 3 + i)
                link.append((glink_ref[slot, k, pl.ds(row, 1), :], sign * glink_ref[slot, k, pl.ds(9 + row, 1), :]))
        for t in range(tiles):
            for part in range(chunks):
                near = []
                for c in range(comps):
                    first = jnp.take_along_axis(own_refs[part][t, ka, c], lanes, axis=1)
                    second = jnp.take_along_axis(own_refs[part][t, kb, c], lanes, axis=1)
                    near.append(jnp.where(take_b, second, first))
                at = pl.ds(place(t, 0, chunks * nvc) + part * nvc, nvc)
                for i in range(3):
                    dr, di = 0.0, 0.0
                    for j in range(3):
                        lr, li = link[i * 3 + j]
                        dr = dr + lr * near[j] - li * near[3 + j]
                        di = di + lr * near[3 + j] + li * near[j]
                    disp[slot, i, at, :] = dr
                    disp[slot, 3 + i, at, :] = di

    for g in range(slots * moms // per):
        for r in range(per):
            slot, p = divmod(g * per + r, moms)
            co = trig_ref[k, p : p + 1, :]
            si = trig_ref[k, moms + p : moms + p + 1, :]
            for i in range(3):
                dr, di = disp[slot, i], disp[slot, 3 + i]
                for part, value in ((0, co * dr + si * di), (1, co * di - si * dr)):
                    high, low = split(value)
                    first = part * half + i * LANES
                    dhi[g, r * cols : (r + 1) * cols, first : first + LANES] = high
                    dlo[g, r * cols : (r + 1) * cols, first : first + LANES] = low
        high, low = dhi[g], dlo[g]
        acc_ref[g * group : (g + 1) * group, :] += lax.dot_general(
            jnp.concatenate([high, high, low], axis=1),
            whole[...],
            (((1,), (1,)), ((), ())),
            preferred_element_type=jnp.float32,
        )

    @pl.when(k == kt - 1)
    def _():
        span = moms * cols
        for slot in range(slots):
            for part in range(2):
                block = acc_ref[slot * span : (slot + 1) * span, part * rows : (part + 1) * rows]
                first = (slot * 2 + part) * span
                out_ref[:, first : first + span] = norm * block.T


def along_tiles(value, steps):
    if steps == 0:
        return value
    count = lax.axis_size("tile")
    return lax.ppermute(value, "tile", [(i, (i + steps) % count) for i in range(count)])


def local(vectors, links, momenta, directions):
    nv = vectors.shape[1]
    sites = vectors.shape[3]
    tiles = lax.axis_size("tile")
    vecs = lax.axis_size("vec")
    tile = lax.axis_index("tile")
    slots = directions.shape[0]
    moms = momenta.shape[0]
    nvt = nv // tiles
    chunks = 2 if nvt % 16 == 0 else 1
    nvc = nvt // chunks
    kt = sites // LANES
    nt = kt * tiles
    extent_x = sites * tiles // PLANE
    norm = 1.0 / math.sqrt(3.0 * sites * tiles)
    f32 = jnp.float32
    smem = pl.BlockSpec(memory_space=pltpu.SMEM)
    vmem = pl.BlockSpec(memory_space=pltpu.VMEM)

    heading = directions % 3
    uses_y = jnp.any(heading == 1)
    uses_x = jnp.any(heading == 0)
    mode = jnp.where(uses_y, jnp.where(uses_x, 2, 0), 1).astype(jnp.int32)
    scal = jnp.concatenate([jnp.stack([mode, tile.astype(jnp.int32)]), directions.astype(jnp.int32)])

    parts = jnp.transpose(vectors, (0, 2, 1, 3)).reshape(6, tiles, chunks, nvc, sites)
    parts = jnp.transpose(parts, (2, 1, 0, 3, 4)).reshape(chunks, tiles, 6 * nvc, sites)
    flat_links = links.reshape(54, sites)
    fields = []
    for c in range(chunks):
        sent = [lax.dynamic_index_in_dim(parts[c], lax.rem(tile + s, tiles), 0, keepdims=False) for s in range(tiles)]
        if c == 0:
            sent = [jnp.concatenate([block, flat_links]) for block in sent]
        else:
            fields[c - 1], sent = lax.optimization_barrier((fields[c - 1], sent))
        fields.append([along_tiles(block, s) for s, block in enumerate(sent)])

    piece_shapes = (jax.ShapeDtypeStruct((kt, 6, nvc, LANES), f32),) * tiles
    link_shape = (6, nt, 18, LANES)
    owns, lefts = [], []
    for c in range(chunks):
        scratch = [pltpu.VMEM((nt, 6, nvc, LANES), f32)] * 2
        call = functools.partial(
            pl.pallas_call,
            functools.partial(filter_kernel, tiles, kt, nvc, c == 0),
            scratch_shapes=scratch,
            compiler_params=pltpu.CompilerParams(vmem_limit_bytes=48 << 20),
            cost_estimate=pl.CostEstimate(
                flops=250 * ITERS * 432 * nvc * nt * LANES, bytes_accessed=48 * nvc * nt * LANES, transcendentals=0
            ),
            name="chebyshev",
        )
        if c == 0:
            *pieces, glink, turned = call(
                out_shape=(
                    *piece_shapes,
                    jax.ShapeDtypeStruct((slots, kt, 18, LANES), f32),
                    jax.ShapeDtypeStruct(link_shape, f32),
                ),
                in_specs=[smem] + [vmem] * tiles,
                out_specs=(vmem,) * (tiles + 2),
            )(scal, *fields[c])
        else:
            pieces = call(out_shape=piece_shapes, in_specs=[smem] + [vmem] * (tiles + 1), out_specs=(vmem,) * tiles)(
                scal, *fields[c], turned
            )
        if c + 1 < chunks:
            fields[c + 1], pieces = lax.optimization_barrier((fields[c + 1], pieces))
        if c > 0:
            own, pieces = lax.optimization_barrier((own, pieces))
            owns[c - 1] = jnp.stack(own)
        own = [along_tiles(pieces[s], s) for s in range(tiles)]
        owns.append(jnp.stack(own))
    for c in range(chunks):
        if nvc % 8:
            owns[c] = owns[c][jnp.mod(tile - jnp.arange(tiles, dtype=jnp.int32), tiles)]
        lefts.append(lax.all_gather(owns[c], "vec", axis=0))

    k = jnp.arange(kt, dtype=jnp.int32)[:, None]
    lane = jnp.arange(LANES, dtype=jnp.int32)[None]

    def pick(options):
        return jnp.where(mode == 0, options[0], jnp.where(mode == 1, options[1], options[2]))

    coords = [piece_coords(m, tile, tiles, k, lane) for m in range(3)]
    x, y, z = (pick([jnp.broadcast_to(c[axis], (kt, LANES)) for c in coords]) for axis in range(3))
    start_x = jnp.where(mode == 0, tile * (sites // PLANE), 0)

    def part(axis, coord, extent):
        return jnp.mod(momenta[:, axis, None, None] * coord[None], extent).astype(f32) / extent

    angle = 2.0 * math.pi * (part(0, x + start_x, extent_x) + part(1, y, LY) + part(2, z, LZ))
    trig = jnp.transpose(jnp.concatenate([jnp.cos(angle), jnp.sin(angle)]), (1, 0, 2))

    index, spots = [], []
    for slot in range(slots):
        d = directions[slot]
        step = jnp.where(d < 3, 1, -1)
        xs = jnp.mod(x + jnp.where(heading[slot] == 0, step, 0), extent_x)
        ys = jnp.mod(y + jnp.where(heading[slot] == 1, step, 0), LY)
        zs = jnp.mod(z + jnp.where(heading[slot] == 2, step, 0), LZ)
        found = [piece_index(m, tile, tiles, xs, ys, zs) for m in range(3)]
        ks, ls = (pick([f[i] for f in found]) for i in range(2))
        ka, kb = jnp.min(ks, axis=1), jnp.max(ks, axis=1)
        index.append(jnp.stack([ls, (ks == kb[:, None]).astype(jnp.int32)], axis=1))
        spots.append(jnp.concatenate([ka, kb, (d < 3).astype(jnp.int32)[None]]))
    spots.append(jnp.broadcast_to(tile.astype(jnp.int32), spots[0].shape))
    index, spots = jnp.stack(index), jnp.stack(spots).astype(jnp.int32)

    rows, cols = vecs * tiles * nvc, nv
    depth = 6 * LANES
    group = cols * max(1, min(moms, 256 // cols))
    groups = slots * moms * cols // group
    bf16 = jnp.bfloat16
    mine = []
    for c in range(chunks):
        partial_rows = pl.pallas_call(
            functools.partial(contract_kernel, chunks, slots, moms, norm),
            grid=(kt,),
            out_shape=jax.ShapeDtypeStruct((rows, slots * 2 * moms * cols), f32),
            in_specs=[smem, pl.BlockSpec((vecs, tiles, 1, 6, nvc, LANES), lambda i: (0, 0, i, 0, 0, 0))]
            + [vmem] * (chunks + 3),
            out_specs=vmem,
            scratch_shapes=[
                pltpu.VMEM((rows, depth), f32),
                pltpu.VMEM((slots, 6, cols, LANES), f32),
                pltpu.VMEM((2 * rows, 3 * depth), bf16),
                pltpu.VMEM((groups, group, depth), bf16),
                pltpu.VMEM((groups, group, depth), bf16),
                pltpu.VMEM((slots * moms * cols, 2 * rows), f32),
            ],
            compiler_params=pltpu.CompilerParams(vmem_limit_bytes=48 << 20),
            cost_estimate=pl.CostEstimate(
                flops=24 * rows * slots * moms * cols * 6 * sites, bytes_accessed=32 * rows * sites, transcendentals=0
            ),
            name="contract",
        )(spots, lefts[c], *owns, trig, glink, index)
        mine.append(lax.psum_scatter(partial_rows, "tile", scatter_dimension=0, tiled=True))
    mine = [m.reshape(-1, nvc, slots * 2 * moms * cols) for m in mine]
    return jnp.stack(mine, axis=1).reshape(nv * vecs // tiles, slots, 2, moms, cols)


def solution(mesh):
    return jax.shard_map(
        local,
        mesh=mesh,
        in_specs=(
            P(None, "vec", None, ("groups", "tile")),
            P(None, None, None, None, ("groups", "tile")),
            P(),
            P(),
        ),
        out_specs=P(("groups", "tile"), None, None, None, "vec"),
        check_vma=False,
    )
```

time: 274 us -> 223 us (0.81)
  blocking collectives: 87.7 us -> 0 us
  starting transfers between devices: 4.93 us -> 17.3 us
  Pallas kernels: 65.1 us -> 73.6 us
  waiting for transfers between devices: 83 us -> 91 us
  other arithmetic: 2.21 us -> 6.26 us
    all_gather x1 -> x0, blocking collectives: 51.6 us -> none  [local(): gauge = lax.all_gather(links.reshape(3, 18, sites), 'tile', axis=0)]
    ppermute x0 -> x12, waiting for transfers between devices: none -> 41.5 us  [along_tiles(): lax.ppermute(value, 'tile', [(i, (i + steps) % count) for i in range(coun...]
    all_to_all x1 -> x0, blocking collectives: 36.1 us -> none  [local(): own = lax.all_to_all(piece, 'tile', 0, 0)]
    all_gather x1 -> x2, waiting for transfers between devices: 41.7 us -> 14.9 us  [local(): lefts.append(lax.all_gather(owns[c], 'vec', axis=0))]
    ppermute x0 -> x12, starting transfers between devices: none -> 17.2 us  [along_tiles(): lax.ppermute(value, 'tile', [(i, (i + steps) % count) for i in range(coun...]
    pallas_call x2 -> x4, Pallas kernels: 65.1 us -> 73.6 us  [the longest x2 37.4 us: local(): pl.pallas_call(functools.partial(contract_kernel, chunks, slots, moms, no...]
    reduce_scatter x1 -> x2, waiting for transfers between devices: 41.2 us -> 34.6 us  [local(): lax.psum_scatter(partial_rows, 'tile', scatter_dimension=0, tiled=True)]
    all_to_all x1 -> x0, starting transfers between devices: 4.89 us -> none  [local(): field = lax.all_to_all(jnp.transpose(field, (1, 0, 2, 3)), 'tile', 0, 0)]
  transfers between devices with their start and end apart: 3 -> 16, of which waited for: 2 -> 10; matrix products, arithmetic and copies ran while one was open for 1% -> 2% of each run, Pallas kernels for 0% -> 34%
where the time goes in v2:
time: 223 us; the launch traced here: 219 us
  waiting for transfers between devices  91 us (41%)
  Pallas kernels  73.6 us (33%)
  between operations  19.8 us (9%)
  starting transfers between devices  17.3 us (8%)
  local copies, waits for them, and re-layouts  10.6 us (5%)
  other arithmetic  6.26 us (3%)
    ppermute x12, waiting for transfers between devices, along_tiles(): lax.ppermute(value, 'tile', [(i, (i + steps) % count) for i in range(coun...  41.5 us
    pallas_call x2, Pallas kernels, local(): pl.pallas_call(functools.partial(contract_kernel, chunks, slots, moms, no...  37.4 us
    reduce_scatter x2, waiting for transfers between devices, local(): lax.psum_scatter(partial_rows, 'tile', scatter_dimension=0, tiled=True)  34.6 us
    pallas_call x1, Pallas kernels, local(): call(out_shape=(*piece_shapes, jax.ShapeDtypeStruct((slots, kt, 18, LANES...  19.5 us
    ppermute x12, starting transfers between devices, along_tiles(): lax.ppermute(value, 'tile', [(i, (i + steps) % count) for i in range(coun...  17.2 us
    pallas_call x1, Pallas kernels, local(): call(out_shape=piece_shapes, in_specs=[smem] + [vmem] * (tiles + 1), out_...  16.7 us
    all_gather x2, waiting for transfers between devices, local(): lefts.append(lax.all_gather(owns[c], 'vec', axis=0))  14.9 us
    unnamed x15, local copies, waits for them, and re-layouts  5.98 us
  transfers between devices with their start and end apart: 16, of which 10 were waited for; matrix products, arithmetic and copies ran while one was open for 2% of the time, Pallas kernels for 34%

profile of v2, /device:TPU:9, one launch (start us, length us, event | category | flops | bytes accessed | tf_op | source)
XLA Modules:
  0.0 218.6 jit_solution(17819942481479348163)
XLA Ops:
  6.5 1.1 copy.14
  7.7 1.5 fusion.90
  9.5 0.9 pad_maximum_fusion.2
  10.4 1.5 collective-permute-start
  11.8 4.1 %collective-permute-start.1 = (f32[102,1024]{1,0:T(8,128)S(1)}, f32[102,1024]{1,0:T(8,128)S(1)}, u32[]{:S(2)}, u32[]{:S(2)}) collective-permute-start(f32[102,1024]{1,0:T(8,128)S(1)} %get-tuple-element.102), channel_id=1, source_target_pairs={{0,8},{4,12},{8,0},{12,4},{1,9},{5,13},{9,1},{13,5},{2,10},{6,14},... | collective-permute-start | bytes 1253384 | tf_op jit(solution)/shard_map/ppermute | solution.py:295
  16.0 0.7 compare_reduce_fusion
  18.1 3.2 %collective-permute-done.2.refs_4_ = f32[102,1024]{1,0:T(8,128)S(1)} collective-permute-done((f32[102,1024]{1,0:T(8,128)}, f32[102,1024]{1,0:T(8,128)S(1)}, u32[]{:S(2)}, u32[]{:S(2)}) %collective-permute-start.2) | collective-permute-done | bytes 417824 | tf_op jit(solution)/shard_map/ppermute | solution.py:295
  21.3 11.2 %collective-permute-done.refs_2_ = f32[102,1024]{1,0:T(8,128)S(1)} collective-permute-done((f32[102,1024]{1,0:T(8,128)S(1)}, f32[102,1024]{1,0:T(8,128)S(1)}, u32[]{:S(2)}, u32[]{:S(2)}) %collective-permute-start) | collective-permute-done | bytes 417824 | tf_op jit(solution)/shard_map/ppermute | solution.py:295
  32.5 14.9 %collective-permute-done.1.refs_3_ = f32[102,1024]{1,0:T(8,128)S(1)} collective-permute-done((f32[102,1024]{1,0:T(8,128)S(1)}, f32[102,1024]{1,0:T(8,128)S(1)}, u32[]{:S(2)}, u32[]{:S(2)}) %collective-permute-start.1) | collective-permute-done | bytes 417824 | tf_op jit(solution)/shard_map/ppermute | solution.py:295
  47.9 4.0 %collective-permute-start.4 = (f32[48,1024]{1,0:T(8,128)S(1)}, f32[48,1024]{1,0:T(8,128)S(1)}, u32[]{:S(2)}, u32[]{:S(2)}) collective-permute-start(f32[48,1024]{1,0:T(8,128)S(1)} %get-tuple-element.41), channel_id=1, source_target_pairs={{0,8},{4,12},{8,0},{12,4},{1,9},{5,13},{9,1},{13,5},{2,10},{6,14},... | collective-permute-start | bytes 589832 | tf_op jit(solution)/shard_map/ppermute | solution.py:295
  52.0 19.5 %chebyshev.2 = (f32[8,6,8,128]{3,2,1,0:T(8,128)S(1)}, f32[8,6,8,128]{3,2,1,0:T(8,128)S(1)}, f32[8,6,8,128]{3,2,1,0:T(8,128)S(1)}, f32[8,6,8,128]{3,2,1,0:T(8,128...) custom-call(s32[4]{0:T(128)S(1)} %pad_add_fusion.1.refs_0_, ...), custom_call_target="tpu_custom_call" | custom-call | flops 14155776000 | bytes 1572864 | tf_op jit(solution)/shard_map/chebyshev/pallas_call | solution.py:351
  71.5 1.5 collective-permute-start.6
  73.0 1.8 collective-permute-start.7
  74.8 16.7 %chebyshev.3 = (f32[8,6,8,128]{3,2,1,0:T(8,128)S(1)}, f32[8,6,8,128]{3,2,1,0:T(8,128)S(1)}, f32[8,6,8,128]{3,2,1,0:T(8,128)S(1)}, f32[8,6,8,128]{3,2,1,0:T(8,128)S(1)}) custom-call(s32[4]{0:T(128)S(1)} %pad_add_fusion.1.refs_0_, f32[48,1024]{1,0:T(8,128)S(1)} %get-tuple-element.55.refs_1_, f32[48,1024]{1,0:T(8,128)S(1)} %collective-permute-done.3.refs_2_, ...), custom_call_target="tpu_custom_call" | custom-call | flops 14155776000 | bytes 1572864 | tf_op jit(solution)/shard_map/chebyshev/pallas_call | solution.py:361
  91.6 1.0 pad_maximum_fusion.refs_0_
  92.7 0.6 fusion.92
  94.7 1.4 collective-permute-start.9
  96.1 2.4 %collective-permute-start.10 = (f32[8,6,8,128]{3,2,1,0:T(8,128)S(1)}, f32[8,6,8,128]{3,2,1,0:T(8,128)S(1)}, u32[]{:S(2)}, u32[]{:S(2)}) collective-permute-start(f32[8,6,8,128]{3,2,1,0:T(8,128)S(1)} %get-tuple-element.70), channel_id=1, source_target_pairs={{0,8},{4,12},{8,0},{12,4},{1,9},{5,13},{9,1},{13,5},{2,10},{6,14},... | collective-permute-start | bytes 589832 | tf_op jit(solution)/shard_map/ppermute | solution.py:295
  103.0 8.3 %collective-permute-done.10 = f32[8,6,8,128]{3,2,1,0:T(8,128)S(1)} collective-permute-done((f32[8,6,8,128]{3,2,1,0:T(8,128)S(1)}, f32[8,6,8,128]{3,2,1,0:T(8,128)S(1)}, u32[]{:S(2)}, u32[]{:S(2)}) %collective-permute-start.10) | collective-permute-done | bytes 196640 | tf_op jit(solution)/shard_map/ppermute | solution.py:295
  111.3 3.7 %collective-permute-done.11 = f32[8,6,8,128]{3,2,1,0:T(8,128)S(1)} collective-permute-done((f32[8,6,8,128]{3,2,1,0:T(8,128)S(1)}, f32[8,6,8,128]{3,2,1,0:T(8,128)S(1)}, u32[]{:S(2)}, u32[]{:S(2)}) %collective-permute-start.11) | collective-permute-done | bytes 196640 | tf_op jit(solution)/shard_map/ppermute | solution.py:295
  115.0 0.9 pad_maximum_fusion.1.refs_1_
  117.7 6.6 %all-gather.5.cloned.1.call-done = f32[16,8,6,8,128]{4,3,2,1,0:T(8,128)} async-done(((f32[4,8,6,8,128]{4,3,2,1,0:T(8,128)}), f32[16,8,6,8,128]{4,3,2,1,0:T(8,128)}) %all-gather.5.cloned.1.call-update) | async-done | bytes 3145744 | tf_op jit(solution)/shard_map/all_gather | solution.py:374
  124.3 1.1 copy-done.1
  125.5 1.9 copy-done.3
  127.3 18.7 %contract.2 = f32[128,2048]{1,0:T(8,128)} custom-call(s32[3,17]{1,0:T(4,128)S(1)} %add_add_fusion.8.scal, f32[4,4,8,6,8,128]{5,4,3,2,1,0:T(8,128)S(1)} %bitcast.66, f32[4,8,6,8,128]{4,3,2,1,0:T(8,128)S(1)} %copy-done, f32[4,8,6,8,128]{4,3,2,1,0:T(8,128)S(1)} %copy-done.1, f32[8,16,128]{2,1,0:T(8,128)S(1)} %maximum_bitcast_fusion.refs_2_, ...), custom_call_target="tpu_custom_call" | custom-call | flops 19327352832 | bytes 4194304 | tf_op jit(solution)/shard_map/contract/pallas_call | solution.py:414
  146.2 8.3 %all-gather.7.cloned.1.call-done = f32[16,8,6,8,128]{4,3,2,1,0:T(8,128)} async-done(((f32[4,8,6,8,128]{4,3,2,1,0:T(8,128)}), f32[16,8,6,8,128]{4,3,2,1,0:T(8,128)}) %all-gather.7.cloned.1.call-update) | async-done | bytes 3145744 | tf_op jit(solution)/shard_map/all_gather | solution.py:374
  154.5 1.9 copy-done.4
  156.3 18.7 %contract.3 = f32[128,2048]{1,0:T(8,128)} custom-call(s32[3,17]{1,0:T(4,128)S(1)} %add_add_fusion.8.scal, f32[4,4,8,6,8,128]{5,4,3,2,1,0:T(8,128)S(1)} %bitcast.67, f32[4,8,6,8,128]{4,3,2,1,0:T(8,128)S(1)} %copy-done, f32[4,8,6,8,128]{4,3,2,1,0:T(8,128)S(1)} %copy-done.2, f32[8,16,128]{2,1,0:T(8,128)S(1)} %maximum_bitcast_fusion.refs_2_, ...), custom_call_target="tpu_custom_call" | custom-call | flops 19327352832 | bytes 4194304 | tf_op jit(solution)/shard_map/contract/pallas_call | solution.py:414
  175.0 6.5 %reduce-scatter.3.cloned.1.call-done = f32[32,2048]{1,0:T(8,128)} async-done(((f32[128,2048]{1,0:T(8,128)}), f32[32,2048]{1,0:T(8,128)}) %reduce-scatter.3.cloned.1.call-update) | async-done | bytes 262160 | tf_op jit(solution)/shard_map/reduce_scatter | solution.py:435
  181.5 28.1 %reduce-scatter.5.cloned.1.call-done = f32[32,2048]{1,0:T(8,128)} async-done(((f32[128,2048]{1,0:T(8,128)}), f32[32,2048]{1,0:T(8,128)}) %reduce-scatter.5.cloned.1.call-update) | async-done | bytes 262160 | tf_op jit(solution)/shard_map/reduce_scatter | solution.py:435
  209.6 1.1 pad_maximum_fusion.6
  210.7 1.4 reshape.2013
  (58 shorter events, 3.7 us)
Async XLA Ops:
  6.5 117.8 %all-gather.5.cloned.1.call-start = ((), (), s32[]{:S(2)}) async-start(), calls=%async_computation.4 | async-start | bytes 3932160 | tf_op jit(solution)/shard_map/all_gather | solution.py:374
  9.4 6.6 %copy-start.5 = (s32[2]{0:T(128)S(1)}, s32[2]{0:T(128)}, u32[]{:S(2)}) copy-start(s32[2]{0:T(128)} %param.7) | copy-start | bytes 28
  10.4 10.9 %collective-permute-start.2 = (f32[102,1024]{1,0:T(8,128)}, f32[102,1024]{1,0:T(8,128)S(1)}, u32[]{:S(2)}, u32[]{:S(2)}) collective-permute-start(f32[102,1024]{1,0:T(8,128)} %get-tuple-element.100), channel_id=1, source_target_pairs={{0,12},{4,0},{8,4},{12,8},{1,13},{5,1},{9,5},{13,9},{2,14},{6,2},{... | collective-permute-start | bytes 1253384 | tf_op jit(solution)/shard_map/ppermute | solution.py:295
  10.4 22.1 %collective-permute-start = (f32[102,1024]{1,0:T(8,128)S(1)}, f32[102,1024]{1,0:T(8,128)S(1)}, u32[]{:S(2)}, u32[]{:S(2)}) collective-permute-start(f32[102,1024]{1,0:T(8,128)S(1)} %get-tuple-element.101), channel_id=1, source_target_pairs={{0,4},{4,8},{8,12},{12,0},{1,5},{5,9},{9,13},{13,1},{2,6},{6,10},{... | collective-permute-start | bytes 1253384 | tf_op jit(solution)/shard_map/ppermute | solution.py:295
  11.8 35.6 %collective-permute-start.1 = (f32[102,1024]{1,0:T(8,128)S(1)}, f32[102,1024]{1,0:T(8,128)S(1)}, u32[]{:S(2)}, u32[]{:S(2)}) collective-permute-start(f32[102,1024]{1,0:T(8,128)S(1)} %get-tuple-element.102), channel_id=1, source_target_pairs={{0,8},{4,12},{8,0},{12,4},{1,9},{5,13},{9,1},{13,5},{2,10},{6,14},... | collective-permute-start | bytes 1253384 | tf_op jit(solution)/shard_map/ppermute | solution.py:295
  47.4 24.1 %collective-permute-start.3 = (f32[48,1024]{1,0:T(8,128)S(1)}, f32[48,1024]{1,0:T(8,128)S(1)}, u32[]{:S(2)}, u32[]{:S(2)}) collective-permute-start(f32[48,1024]{1,0:T(8,128)S(1)} %get-tuple-element.40), channel_id=1, source_target_pairs={{0,4},{4,8},{8,12},{12,0},{1,5},{5,9},{9,13},{13,1},{2,6},{6,10},{... | collective-permute-start | bytes 589832 | tf_op jit(solution)/shard_map/ppermute | solution.py:295
  47.9 23.6 %collective-permute-start.4 = (f32[48,1024]{1,0:T(8,128)S(1)}, f32[48,1024]{1,0:T(8,128)S(1)}, u32[]{:S(2)}, u32[]{:S(2)}) collective-permute-start(f32[48,1024]{1,0:T(8,128)S(1)} %get-tuple-element.41), channel_id=1, source_target_pairs={{0,8},{4,12},{8,0},{12,4},{1,9},{5,13},{9,1},{13,5},{2,10},{6,14},... | collective-permute-start | bytes 589832 | tf_op jit(solution)/shard_map/ppermute | solution.py:295
  51.9 19.6 %collective-permute-start.5 = (f32[48,1024]{1,0:T(8,128)S(1)}, f32[48,1024]{1,0:T(8,128)S(1)}, u32[]{:S(2)}, u32[]{:S(2)}) collective-permute-start(f32[48,1024]{1,0:T(8,128)S(1)} %get-tuple-element.42), channel_id=1, source_target_pairs={{0,12},{4,0},{8,4},{12,8},{1,13},{5,1},{9,5},{13,9},{2,14},{6,2},{... | collective-permute-start | bytes 589832 | tf_op jit(solution)/shard_map/ppermute | solution.py:295
  71.5 20.0 %collective-permute-start.6 = (f32[8,6,8,128]{3,2,1,0:T(8,128)S(1)}, f32[8,6,8,128]{3,2,1,0:T(8,128)S(1)}, u32[]{:S(2)}, u32[]{:S(2)}) collective-permute-start(f32[8,6,8,128]{3,2,1,0:T(8,128)S(1)} %get-tuple-element.52), channel_id=1, source_target_pairs={{0,4},{4,8},{8,12},{12,0},{1,5},{5,9},{9,13},{13,1},{2,6},{6,10},{... | collective-permute-start | bytes 589832 | tf_op jit(solution)/shard_map/ppermute | solution.py:295
  73.0 18.5 %collective-permute-start.7 = (f32[8,6,8,128]{3,2,1,0:T(8,128)S(1)}, f32[8,6,8,128]{3,2,1,0:T(8,128)S(1)}, u32[]{:S(2)}, u32[]{:S(2)}) collective-permute-start(f32[8,6,8,128]{3,2,1,0:T(8,128)S(1)} %get-tuple-element.53), channel_id=1, source_target_pairs={{0,8},{4,12},{8,0},{12,4},{1,9},{5,13},{9,1},{13,5},{2,10},{6,14},... | collective-permute-start | bytes 589832 | tf_op jit(solution)/shard_map/ppermute | solution.py:295
  74.8 16.8 %collective-permute-start.8 = (f32[8,6,8,128]{3,2,1,0:T(8,128)S(1)}, f32[8,6,8,128]{3,2,1,0:T(8,128)S(1)}, u32[]{:S(2)}, u32[]{:S(2)}) collective-permute-start(f32[8,6,8,128]{3,2,1,0:T(8,128)S(1)} %get-tuple-element.54), channel_id=1, source_target_pairs={{0,12},{4,0},{8,4},{12,8},{1,13},{5,1},{9,5},{13,9},{2,14},{6,2},{... | collective-permute-start | bytes 589832 | tf_op jit(solution)/shard_map/ppermute | solution.py:295
  91.6 25.7 %copy-start.6 = (s32[8,3]{0,1:T(4,128)S(1)}, s32[8,3]{0,1:T(4,128)}, u32[]{:S(2)}) copy-start(s32[8,3]{0,1:T(4,128)} %param.6) | copy-start | bytes 292
  92.6 31.7 %copy-start = (f32[4,8,6,8,128]{4,3,2,1,0:T(8,128)S(1)}, f32[4,8,6,8,128]{4,3,2,1,0:T(8,128)}, u32[]{:S(2)}) copy-start(f32[4,8,6,8,128]{4,3,2,1,0:T(8,128)} %pad_maximum_fusion.refs_0_) | copy-start | bytes 2359300
  92.6 61.8 %all-gather.7.cloned.1.call-start = ((), (), s32[]{:S(2)}) async-start(), calls=%async_computation.5 | async-start | bytes 3932160 | tf_op jit(solution)/shard_map/all_gather | solution.py:374
  94.7 8.3 %collective-permute-start.9 = (f32[8,6,8,128]{3,2,1,0:T(8,128)S(1)}, f32[8,6,8,128]{3,2,1,0:T(8,128)S(1)}, u32[]{:S(2)}, u32[]{:S(2)}) collective-permute-start(f32[8,6,8,128]{3,2,1,0:T(8,128)S(1)} %get-tuple-element.69), channel_id=1, source_target_pairs={{0,4},{4,8},{8,12},{12,0},{1,5},{5,9},{9,13},{13,1},{2,6},{6,10},{... | collective-permute-start | bytes 589832 | tf_op jit(solution)/shard_map/ppermute | solution.py:295
  96.1 15.2 %collective-permute-start.10 = (f32[8,6,8,128]{3,2,1,0:T(8,128)S(1)}, f32[8,6,8,128]{3,2,1,0:T(8,128)S(1)}, u32[]{:S(2)}, u32[]{:S(2)}) collective-permute-start(f32[8,6,8,128]{3,2,1,0:T(8,128)S(1)} %get-tuple-element.70), channel_id=1, source_target_pairs={{0,8},{4,12},{8,0},{12,4},{1,9},{5,13},{9,1},{13,5},{2,10},{6,14},... | collective-permute-start | bytes 589832 | tf_op jit(solution)/shard_map/ppermute | solution.py:295
  98.5 16.5 %collective-permute-start.11 = (f32[8,6,8,128]{3,2,1,0:T(8,128)S(1)}, f32[8,6,8,128]{3,2,1,0:T(8,128)S(1)}, u32[]{:S(2)}, u32[]{:S(2)}) collective-permute-start(f32[8,6,8,128]{3,2,1,0:T(8,128)S(1)} %get-tuple-element.71), channel_id=1, source_target_pairs={{0,12},{4,0},{8,4},{12,8},{1,13},{5,1},{9,5},{13,9},{2,14},{6,2},{... | collective-permute-start | bytes 589832 | tf_op jit(solution)/shard_map/ppermute | solution.py:295
  115.9 65.6 %reduce-scatter.3.cloned.1.call-start = ((), (), s32[]{:S(2)}) async-start(), calls=%async_computation.2 | async-start | bytes 1310720 | tf_op jit(solution)/shard_map/reduce_scatter | solution.py:435
  124.3 1.1 copy-start.1
  125.5 1.9 copy-start.3
  127.3 27.1 %copy-start.2 = (f32[4,8,6,8,128]{4,3,2,1,0:T(8,128)S(1)}, f32[4,8,6,8,128]{4,3,2,1,0:T(8,128)}, u32[]{:S(2)}) copy-start(f32[4,8,6,8,128]{4,3,2,1,0:T(8,128)} %pad_maximum_fusion.1.refs_1_) | copy-start | bytes 2359300
  146.1 63.5 %reduce-scatter.5.cloned.1.call-start = ((), (), s32[]{:S(2)}) async-start(), calls=%async_computation.3 | async-start | bytes 1310720 | tf_op jit(solution)/shard_map/reduce_scatter | solution.py:435
  154.5 1.9 copy-start.4
Sparse Core Ops, SparseCore 0:
  92.7 31.5 all-gather.4
  125.9 28.5 all-gather.6
  156.7 24.7 reduce-scatter.2
  183.8 25.7 reduce-scatter.4

commit v3 on v2

--- a/solution.py
+++ b/solution.py
@@ -80,7 +80,7 @@
 def filter_kernel(tiles, kt, rows, with_links, *refs):
     scal, slab_refs, refs = refs[0], refs[1 : 1 + tiles], refs[1 + tiles :]
     if with_links:
-        piece_refs, (glink_ref, l_ref, a_ref, b_ref) = refs[:tiles], refs[tiles:]
+        link_ref, piece_refs, (glink_ref, l_ref, a_ref, b_ref) = refs[0], refs[1 : 1 + tiles], refs[1 + tiles :]
     else:
         l_ref, piece_refs, (a_ref, b_ref) = refs[0], refs[1 : 1 + tiles], refs[1 + tiles :]
     mine = scal[1]
@@ -117,9 +117,10 @@
             for c in range(comps):
                 a_ref[t * kt + k, c] = slab_refs[s][c * rows : (c + 1) * rows, lanes]
             if with_links:
+                share = link_ref.shape[3] // LANES
+                lanes = slice(k % share * LANES, (k % share + 1) * LANES)
                 for m in range(3):
-                    first = comps * rows + 18 * m
-                    l_ref[m, t * kt + k] = slab_refs[s][first : first + 18, lanes]
+                    l_ref[m, t * kt + k] = link_ref[k // share, s, 18 * m : 18 * m + 18, lanes]
 
     if with_links:
 
@@ -186,11 +187,12 @@
                     pack_piece(mode, tiles, mine, lambda n, slot=slot: l_ref[scal[2 + slot], n], write, kt)
 
 
-def contract_kernel(chunks, slots, moms, norm, scal, left_ref, *refs):
-    own_refs = refs[:chunks]
-    trig_ref, glink_ref, index_ref, out_ref, side, disp, whole, dhi, dlo, acc_ref = refs[chunks:]
+def contract_kernel(vecs, chunks, slots, moms, norm, scal, *refs):
+    left_refs, own_refs, refs = refs[:vecs], refs[vecs : vecs + chunks], refs[vecs + chunks :]
+    tiles, nvc = own_refs[0].shape[0], own_refs[0].shape[3]
+    (trig_ref, glink_ref, index_ref), out_refs, refs = refs[:3], refs[3 : 3 + tiles], refs[3 + tiles :]
+    side, disp, whole, dhi, dlo, acc_ref, turned = refs
     k = pl.program_id(0)
-    vecs, tiles, nvc = left_ref.shape[0], left_ref.shape[1], left_ref.shape[4]
     rows = vecs * tiles * nvc
     cols = tiles * nvc * chunks
     comps = 6
@@ -217,9 +219,9 @@
 
     for v in range(vecs):
         for t in range(tiles):
-            at = pl.ds(place(t, v, nvc), nvc)
+            at = pl.ds(place(t, v if nvc % 8 else scal[slots + 1, v], nvc), nvc)
             for c in range(comps):
-                side[at, c * LANES : (c + 1) * LANES] = left_ref[v, t, 0, c]
+                side[at, c * LANES : (c + 1) * LANES] = left_refs[v][t, 0, c]
     for c in range(3):
         rh, rl = split(side[:, c * LANES : (c + 1) * LANES])
         ih, il = split(side[:, half + c * LANES : half + (c + 1) * LANES])
@@ -285,7 +287,10 @@
             for part in range(2):
                 block = acc_ref[slot * span : (slot + 1) * span, part * rows : (part + 1) * rows]
                 first = (slot * 2 + part) * span
-                out_ref[:, first : first + span] = norm * block.T
+                turned[:, first : first + span] = norm * block.T
+        part = rows // tiles
+        for s in range(tiles):
+            out_refs[s][...] = turned[pl.ds(pl.multiple_of(lax.rem(mine + s, tiles) * part, 8), part), :]
 
 
 def along_tiles(value, steps):
@@ -293,6 +298,33 @@
         return value
     count = lax.axis_size("tile")
     return lax.ppermute(value, "tile", [(i, (i + steps) % count) for i in range(count)])
+
+
+def vec_cores():
+    return 2 if lax.axis_size("vec") % 2 == 0 else 1
+
+
+def over_chips(value):
+    count = lax.axis_size("vec")
+    blocks = [value]
+    for step in range(vec_cores(), count, vec_cores()):
+        blocks.append(lax.ppermute(value, "vec", [(i, (i + step) % count) for i in range(count)]))
+    return blocks
+
+
+def over_cores(blocks):
+    if vec_cores() == 1:
+        return []
+    count = lax.axis_size("vec")
+    return [lax.ppermute(block, "vec", [(i, i ^ 1) for i in range(count)]) for block in blocks]
+
+
+def block_owners():
+    count, here = lax.axis_size("vec"), lax.axis_index("vec")
+    owner = [lax.rem(here - step + count, count) for step in range(0, count, vec_cores())]
+    if vec_cores() == 2:
+        owner += [other + 1 - 2 * (here % 2) for other in owner]
+    return jnp.stack(owner).astype(jnp.int32)
 
 
 def local(vectors, links, momenta, directions):
@@ -322,13 +354,13 @@
 
     parts = jnp.transpose(vectors, (0, 2, 1, 3)).reshape(6, tiles, chunks, nvc, sites)
     parts = jnp.transpose(parts, (2, 1, 0, 3, 4)).reshape(chunks, tiles, 6 * nvc, sites)
-    flat_links = links.reshape(54, sites)
+    share = sites // vecs
+    link_share = lax.dynamic_slice_in_dim(links.reshape(54, sites), lax.axis_index("vec") * share, share, 1)
+    gauge = lax.all_gather(jnp.stack([along_tiles(link_share, s) for s in range(tiles)]), "vec", axis=0)
     fields = []
     for c in range(chunks):
         sent = [lax.dynamic_index_in_dim(parts[c], lax.rem(tile + s, tiles), 0, keepdims=False) for s in range(tiles)]
-        if c == 0:
-            sent = [jnp.concatenate([block, flat_links]) for block in sent]
-        else:
+        if c > 0:
             fields[c - 1], sent = lax.optimization_barrier((fields[c - 1], sent))
         fields.append([along_tiles(block, s) for s, block in enumerate(sent)])
 
@@ -354,9 +386,9 @@
                     jax.ShapeDtypeStruct((slots, kt, 18, LANES), f32),
                     jax.ShapeDtypeStruct(link_shape, f32),
                 ),
-                in_specs=[smem] + [vmem] * tiles,
+                in_specs=[smem] + [vmem] * (tiles + 1),
                 out_specs=(vmem,) * (tiles + 2),
-            )(scal, *fields[c])
+            )(scal, *fields[c], gauge)
         else:
             pieces = call(out_shape=piece_shapes, in_specs=[smem] + [vmem] * (tiles + 1), out_specs=(vmem,) * tiles)(
                 scal, *fields[c], turned
@@ -371,7 +403,11 @@
     for c in range(chunks):
         if nvc % 8:
             owns[c] = owns[c][jnp.mod(tile - jnp.arange(tiles, dtype=jnp.int32), tiles)]
-        lefts.append(lax.all_gather(owns[c], "vec", axis=0))
+        lefts.append(over_chips(owns[c]))
+        if c == 1:
+            lefts[0][1:], owns[1] = lax.optimization_barrier((lefts[0][1:], owns[1]))
+            lefts[1][0] = owns[1]
+    owner = block_owners()
 
     k = jnp.arange(kt, dtype=jnp.int32)[:, None]
     lane = jnp.arange(LANES, dtype=jnp.int32)[None]
@@ -402,6 +438,7 @@
         index.append(jnp.stack([ls, (ks == kb[:, None]).astype(jnp.int32)], axis=1))
         spots.append(jnp.concatenate([ka, kb, (d < 3).astype(jnp.int32)[None]]))
     spots.append(jnp.broadcast_to(tile.astype(jnp.int32), spots[0].shape))
+    spots.append(jnp.pad(owner, (0, 2 * kt + 1 - vecs)))
     index, spots = jnp.stack(index), jnp.stack(spots).astype(jnp.int32)
 
     rows, cols = vecs * tiles * nvc, nv
@@ -411,13 +448,23 @@
     bf16 = jnp.bfloat16
     mine = []
     for c in range(chunks):
+        near, far = lefts[c][:1], lefts[c][1:]
+        twins = over_cores(near)
+        if c > 0:
+            far, partial_rows = lax.optimization_barrier((far, partial_rows))
+        left = near + far + twins + over_cores(far)
+        if nvc % 8:
+            left = list(jnp.stack(left)[jnp.argsort(owner)])
+        if c > 0:
+            mine.append(functools.reduce(jnp.add, [along_tiles(partial_rows[s], s) for s in range(tiles)]))
         partial_rows = pl.pallas_call(
-            functools.partial(contract_kernel, chunks, slots, moms, norm),
+            functools.partial(contract_kernel, vecs, chunks, slots, moms, norm),
             grid=(kt,),
-            out_shape=jax.ShapeDtypeStruct((rows, slots * 2 * moms * cols), f32),
-            in_specs=[smem, pl.BlockSpec((vecs, tiles, 1, 6, nvc, LANES), lambda i: (0, 0, i, 0, 0, 0))]
+            out_shape=(jax.ShapeDtypeStruct((rows // tiles, slots * 2 * moms * cols), f32),) * tiles,
+            in_specs=[smem]
+            + [pl.BlockSpec((tiles, 1, 6, nvc, LANES), lambda i: (0, i, 0, 0, 0))] * vecs
             + [vmem] * (chunks + 3),
-            out_specs=vmem,
+            out_specs=(vmem,) * tiles,
             scratch_shapes=[
                 pltpu.VMEM((rows, depth), f32),
                 pltpu.VMEM((slots, 6, cols, LANES), f32),
@@ -425,14 +472,15 @@
                 pltpu.VMEM((groups, group, depth), bf16),
                 pltpu.VMEM((groups, group, depth), bf16),
                 pltpu.VMEM((slots * moms * cols, 2 * rows), f32),
+                pltpu.VMEM((rows, slots * 2 * moms * cols), f32),
             ],
             compiler_params=pltpu.CompilerParams(vmem_limit_bytes=48 << 20),
             cost_estimate=pl.CostEstimate(
                 flops=24 * rows * slots * moms * cols * 6 * sites, bytes_accessed=32 * rows * sites, transcendentals=0
             ),
             name="contract",
-        )(spots, lefts[c], *owns, trig, glink, index)
-        mine.append(lax.psum_scatter(partial_rows, "tile", scatter_dimension=0, tiled=True))
+        )(spots, *left, *owns, trig, glink, index)
+    mine.append(functools.reduce(jnp.add, [along_tiles(partial_rows[s], s) for s in range(tiles)]))
     mine = [m.reshape(-1, nvc, slots * 2 * moms * cols) for m in mine]
     return jnp.stack(mine, axis=1).reshape(nv * vecs // tiles, slots, 2, moms, cols)
 

time: 223 us -> 163 us (0.73); the launches traced: 219 us -> 163 us
  waiting for transfers between devices: 91 us -> 39.5 us
  between operations: 19.8 us -> 6.39 us
  blocking collectives: 0 us -> 11.2 us
  starting transfers between devices: 17.3 us -> 27.8 us
  local copies, waits for them, and re-layouts: 10.6 us -> 5.69 us
  Pallas kernels: 73.6 us -> 69.6 us
  other arithmetic: 6.26 us -> 2.62 us
    reduce_scatter x2 -> x0, waiting for transfers between devices: 34.6 us -> none  [local(): lax.psum_scatter(partial_rows, 'tile', scatter_dimension=0, tiled=True)]
    all_gather x2 -> x0, waiting for transfers between devices: 14.9 us -> none  [local(): lefts.append(lax.all_gather(owns[c], 'vec', axis=0))]
    all_gather x0 -> x1, blocking collectives: none -> 11.2 us  [local(): lax.all_gather(jnp.stack([along_tiles(link_share, s) for s in range(tiles...]
    ppermute x0 -> x6, starting transfers between devices: none -> 5.86 us  [the longest x4 4.31 us: over_cores(): lax.ppermute(block, 'vec', [(i, i ^ 1) for i in range(count)])]
    unnamed x15 -> x5, local copies, waits for them, and re-layouts: 5.98 us -> 1.06 us
    ppermute x12 -> x21, starting transfers between devices: 17.2 us -> 21.9 us  [along_tiles(): lax.ppermute(value, 'tile', [(i, (i + steps) % count) for i in range(coun...]
    ppermute x12 -> x21, waiting for transfers between devices: 41.5 us -> 39.5 us  [along_tiles(): lax.ppermute(value, 'tile', [(i, (i + steps) % count) for i in range(coun...]
  transfers between devices with their start and end apart: 16 -> 27, of which waited for: 10 -> 8; matrix products, arithmetic and copies ran while one was open for 2% -> 3% of each run, Pallas kernels for 34% -> 43%
where the time goes in v3:
time: 163 us
  Pallas kernels  69.6 us (43%)
  waiting for transfers between devices  39.5 us (24%)
  starting transfers between devices  27.8 us (17%)
  blocking collectives  11.2 us (7%)
  between operations  6.39 us (4%)
  local copies, waits for them, and re-layouts  5.69 us (3%)
  other arithmetic  2.62 us (2%)
    ppermute x21, waiting for transfers between devices, along_tiles(): lax.ppermute(value, 'tile', [(i, (i + steps) % count) for i in range(coun...  39.5 us
    pallas_call x2, Pallas kernels, local(): pl.pallas_call(functools.partial(contract_kernel, vecs, chunks, slots, mo...  35.2 us
    ppermute x21, starting transfers between devices, along_tiles(): lax.ppermute(value, 'tile', [(i, (i + steps) % count) for i in range(coun...  21.9 us
    pallas_call x1, Pallas kernels, local(): call(out_shape=(*piece_shapes, jax.ShapeDtypeStruct((slots, kt, 18, LANES...  18.5 us
    pallas_call x1, Pallas kernels, local(): call(out_shape=piece_shapes, in_specs=[smem] + [vmem] * (tiles + 1), out_...  15.9 us
    all_gather x1, blocking collectives, local(): lax.all_gather(jnp.stack([along_tiles(link_share, s) for s in range(tiles...  11.2 us
    ppermute x4, starting transfers between devices, over_cores(): lax.ppermute(block, 'vec', [(i, i ^ 1) for i in range(count)])  4.31 us
  transfers between devices with their start and end apart: 27, of which 8 were waited for; matrix products, arithmetic and copies ran while one was open for 3% of the time, Pallas kernels for 43%

profile of v3, /device:TPU:9, one launch (start us, length us, event | category | flops | bytes accessed | tf_op | source)
XLA Modules:
  0.0 162.8 jit_solution(18240612587102171239)
XLA Ops:
  0.0 1.1 copy.14
  1.2 1.3 collective-permute-start.6
  2.5 1.1 collective-permute-start.7
  3.6 1.4 collective-permute-start.8
  5.0 1.5 fusion.90
  6.9 3.1 %collective-permute-start.1 = (f32[48,1024]{1,0:T(8,128)S(1)}, f32[48,1024]{1,0:T(8,128)S(1)}, u32[]{:S(2)}, u32[]{:S(2)}) collective-permute-start(f32[48,1024]{1,0:T(8,128)S(1)} %get-tuple-element.127), channel_id=1, source_target_pairs={{0,8},{4,12},{8,0},{12,4},{1,9},{5,13},{9,1},{13,5},{2,10},{6,14},... | collective-permute-start | bytes 589832 | tf_op jit(solution)/shard_map/ppermute | solution.py:300
  10.0 0.7 compare_reduce_fusion
  19.4 11.2 %all-gather = f32[16,54,256]{2,1,0:T(8,128)S(1)} all-gather(f32[4,54,256]{2,1,0:T(8,128)S(1)} %pad_maximum_fusion.3), channel_id=2, replica_groups=mesh['groups'=2,'tile'=4,'vec'=4] {'vec'}, dimensions={0}, use_global_device_ids=true | all-gather | bytes 1105920 | tf_op jit(solution)/shard_map/all_gather | solution.py:359
  30.6 1.8 %collective-permute-start.3 = (f32[48,1024]{1,0:T(8,128)S(1)}, f32[48,1024]{1,0:T(8,128)S(1)}, u32[]{:S(2)}, u32[]{:S(2)}) collective-permute-start(f32[48,1024]{1,0:T(8,128)S(1)} %get-tuple-element.55), channel_id=1, source_target_pairs={{0,4},{4,8},{8,12},{12,0},{1,5},{5,9},{9,13},{13,1},{2,6},{6,10},{... | collective-permute-start | bytes 589832 | tf_op jit(solution)/shard_map/ppermute | solution.py:300
  32.4 1.5 collective-permute-start.4
  34.0 18.5 %chebyshev.2 = (f32[8,6,8,128]{3,2,1,0:T(8,128)S(1)}, f32[8,6,8,128]{3,2,1,0:T(8,128)S(1)}, f32[8,6,8,128]{3,2,1,0:T(8,128)S(1)}, f32[8,6,8,128]{3,2,1,0:T(8,128...) custom-call(s32[4]{0:T(128)S(1)} %pad_add_fusion.2.refs_0_, ...), custom_call_target="tpu_custom_call" | custom-call | flops 14155776000 | bytes 1572864 | tf_op jit(solution)/shard_map/chebyshev/pallas_call | solution.py:383
  52.5 0.9 collective-permute-start.10
  53.4 1.8 %collective-permute-start.11 = (f32[8,6,8,128]{3,2,1,0:T(8,128)S(1)}, f32[8,6,8,128]{3,2,1,0:T(8,128)S(1)}, u32[]{:S(2)}, u32[]{:S(2)}) collective-permute-start(f32[8,6,8,128]{3,2,1,0:T(8,128)S(1)} %get-tuple-element.69), channel_id=1, source_target_pairs={{0,12},{4,0},{8,4},{12,8},{1,13},{5,1},{9,5},{13,9},{2,14},{6,2},{... | collective-permute-start | bytes 589832 | tf_op jit(solution)/shard_map/ppermute | solution.py:300
  55.8 15.9 %chebyshev.3 = (f32[8,6,8,128]{3,2,1,0:T(8,128)S(1)}, f32[8,6,8,128]{3,2,1,0:T(8,128)S(1)}, f32[8,6,8,128]{3,2,1,0:T(8,128)S(1)}, f32[8,6,8,128]{3,2,1,0:T(8,128)S(1)}) custom-call(s32[4]{0:T(128)S(1)} %pad_add_fusion.2.refs_0_, f32[48,1024]{1,0:T(8,128)S(1)} %get-tuple-element.70.refs_1_, f32[48,1024]{1,0:T(8,128)S(1)} %collective-permute-done.3.refs_2_, ...), custom_call_target="tpu_custom_call" | custom-call | flops 14155776000 | bytes 1572864 | tf_op jit(solution)/shard_map/chebyshev/pallas_call | solution.py:393
  71.7 1.3 collective-permute-done.11
  73.8 1.5 collective-permute-start.13
  75.3 0.9 collective-permute-start.14
  76.2 2.7 %collective-permute-start.17 = (f32[4,8,6,8,128]{4,3,2,1,0:T(8,128)S(1)}, f32[4,8,6,8,128]{4,3,2,1,0:T(8,128)S(1)}, u32[]{:S(2)}, u32[]{:S(2)}) collective-permute-start(f32[4,8,6,8,128]{4,3,2,1,0:T(8,128)S(1)} %pad_maximum_fusion.1.refs_0_.refs_4_), channel_id=1, source_target_pairs={{0,1},{1,0},{2,3},{3,2},{4,5},{5,4},{6,7},{7,6},{8,9},{9,8},{10,11... | collective-permute-start | bytes 2359304 | tf_op jit(solution)/shard_map/ppermute | solution.py:319
  79.3 9.1 %collective-permute-done.13 = f32[8,6,8,128]{3,2,1,0:T(8,128)S(1)} collective-permute-done((f32[8,6,8,128]{3,2,1,0:T(8,128)S(1)}, f32[8,6,8,128]{3,2,1,0:T(8,128)S(1)}, u32[]{:S(2)}, u32[]{:S(2)}) %collective-permute-start.13) | collective-permute-done | bytes 196640 | tf_op jit(solution)/shard_map/ppermute | solution.py:300
  88.3 5.0 %collective-permute-done.14 = f32[8,6,8,128]{3,2,1,0:T(8,128)S(1)} collective-permute-done((f32[8,6,8,128]{3,2,1,0:T(8,128)S(1)}, f32[8,6,8,128]{3,2,1,0:T(8,128)S(1)}, u32[]{:S(2)}, u32[]{:S(2)}) %collective-permute-start.14) | collective-permute-done | bytes 196640 | tf_op jit(solution)/shard_map/ppermute | solution.py:300
  94.3 1.2 collective-permute-start.15
  95.8 17.6 %contract.2 = (f32[32,2048]{1,0:T(8,128)S(1)}, f32[32,2048]{1,0:T(8,128)S(1)}, f32[32,2048]{1,0:T(8,128)S(1)}, f32[32,2048]{1,0:T(8,128)S(1)}) custom-call(s32[4,17]{1,0:T(4,128)S(1)} %pad_add_fusion.1.scal, f32[4,8,6,8,128]{4,3,2,1,0:T(8,128)S(1)} %pad_maximum_fusion.1.refs_0_.refs_4_, f32[4,8,6,8,128]{4,3,2,1,0:T(8,128)S(1)} %collective-permute-done.16.refs_1_, ...), custom_call_target="tpu_custom_call" | custom-call | flops 19327352832 | bytes 4194304 | tf_op jit(solution)/shard_map/contract/pallas_call | solution.py:460
  113.5 0.8 collective-permute-start.23
  114.2 0.9 collective-permute-start.20
  115.1 1.4 collective-permute-start.21
  116.5 17.6 %contract.3 = (f32[32,2048]{1,0:T(8,128)S(1)}, f32[32,2048]{1,0:T(8,128)S(1)}, f32[32,2048]{1,0:T(8,128)S(1)}, f32[32,2048]{1,0:T(8,128)S(1)}) custom-call(s32[4,17]{1,0:T(4,128)S(1)} %pad_add_fusion.1.scal, f32[4,8,6,8,128]{4,3,2,1,0:T(8,128)S(1)} %pad_maximum_fusion.refs_5_.refs_0_, f32[4,8,6,8,128]{4,3,2,1,0:T(8,128)S(1)} %collective-permute-done.15.refs_1_, ...), custom_call_target="tpu_custom_call" | custom-call | flops 19327352832 | bytes 4194304 | tf_op jit(solution)/shard_map/contract/pallas_call | solution.py:460
  134.6 2.9 %collective-permute-start.25 = (f32[32,2048]{1,0:T(8,128)S(1)}, f32[32,2048]{1,0:T(8,128)S(1)}, u32[]{:S(2)}, u32[]{:S(2)}) collective-permute-start(f32[32,2048]{1,0:T(8,128)S(1)} %get-tuple-element.101), channel_id=1, source_target_pairs={{0,8},{4,12},{8,0},{12,4},{1,9},{5,13},{9,1},{13,5},{2,10},{6,14},... | collective-permute-start | bytes 786440 | tf_op jit(solution)/shard_map/ppermute | solution.py:300
  137.6 1.2 collective-permute-done.21
  138.8 15.1 %collective-permute-done.24 = f32[32,2048]{1,0:T(8,128)S(1)} collective-permute-done((f32[32,2048]{1,0:T(8,128)S(1)}, f32[32,2048]{1,0:T(8,128)S(1)}, u32[]{:S(2)}, u32[]{:S(2)}) %collective-permute-start.24) | collective-permute-done | bytes 262176 | tf_op jit(solution)/shard_map/ppermute | solution.py:300
  153.9 5.6 %collective-permute-done.25 = f32[32,2048]{1,0:T(8,128)S(1)} collective-permute-done((f32[32,2048]{1,0:T(8,128)S(1)}, f32[32,2048]{1,0:T(8,128)S(1)}, u32[]{:S(2)}, u32[]{:S(2)}) %collective-permute-start.25) | collective-permute-done | bytes 262176 | tf_op jit(solution)/shard_map/ppermute | solution.py:300
  159.5 1.8 %collective-permute-done.26 = f32[32,2048]{1,0:T(8,128)S(1)} collective-permute-done((f32[32,2048]{1,0:T(8,128)S(1)}, f32[32,2048]{1,0:T(8,128)S(1)}, u32[]{:S(2)}, u32[]{:S(2)}) %collective-permute-start.26) | collective-permute-done | bytes 262176 | tf_op jit(solution)/shard_map/ppermute | solution.py:300
  161.4 1.4 reshape.2013
  (73 shorter events, 6.7 us)
Async XLA Ops:
  1.2 18.1 %collective-permute-start.6 = (f32[54,256]{1,0:T(8,128)S(1)}, f32[54,256]{1,0:T(8,128)S(1)}, u32[]{:S(2)}, u32[]{:S(2)}) collective-permute-start(f32[54,256]{1,0:T(8,128)S(1)} %constant_dynamic-slice_fusion), channel_id=1, source_target_pairs={{0,4},{4,8},{8,12},{12,0},{1,5},{5,9},{9,13},{13,1},{2,6},{6,10},{... | collective-permute-start | bytes 165896 | tf_op jit(solution)/shard_map/ppermute | solution.py:300
  2.5 16.8 %collective-permute-start.7 = (f32[54,256]{1,0:T(8,128)S(1)}, f32[54,256]{1,0:T(8,128)S(1)}, u32[]{:S(2)}, u32[]{:S(2)}) collective-permute-start(f32[54,256]{1,0:T(8,128)S(1)} %constant_dynamic-slice_fusion), channel_id=1, source_target_pairs={{0,8},{4,12},{8,0},{12,4},{1,9},{5,13},{9,1},{13,5},{2,10},{6,14},... | collective-permute-start | bytes 165896 | tf_op jit(solution)/shard_map/ppermute | solution.py:300
  3.6 15.7 %collective-permute-start.8 = (f32[54,256]{1,0:T(8,128)S(1)}, f32[54,256]{1,0:T(8,128)S(1)}, u32[]{:S(2)}, u32[]{:S(2)}) collective-permute-start(f32[54,256]{1,0:T(8,128)S(1)} %constant_dynamic-slice_fusion), channel_id=1, source_target_pairs={{0,12},{4,0},{8,4},{12,8},{1,13},{5,1},{9,5},{13,9},{2,14},{6,2},{... | collective-permute-start | bytes 165896 | tf_op jit(solution)/shard_map/ppermute | solution.py:300
  6.7 3.3 %copy-start = (s32[2]{0:T(128)S(1)}, s32[2]{0:T(128)}, u32[]{:S(2)}) copy-start(s32[2]{0:T(128)} %param.7) | copy-start | bytes 28
  6.8 23.8 %collective-permute-start = (f32[48,1024]{1,0:T(8,128)S(1)}, f32[48,1024]{1,0:T(8,128)S(1)}, u32[]{:S(2)}, u32[]{:S(2)}) collective-permute-start(f32[48,1024]{1,0:T(8,128)S(1)} %get-tuple-element.128), channel_id=1, source_target_pairs={{0,4},{4,8},{8,12},{12,0},{1,5},{5,9},{9,13},{13,1},{2,6},{6,10},{... | collective-permute-start | bytes 589832 | tf_op jit(solution)/shard_map/ppermute | solution.py:300
  6.9 23.7 %collective-permute-start.1 = (f32[48,1024]{1,0:T(8,128)S(1)}, f32[48,1024]{1,0:T(8,128)S(1)}, u32[]{:S(2)}, u32[]{:S(2)}) collective-permute-start(f32[48,1024]{1,0:T(8,128)S(1)} %get-tuple-element.127), channel_id=1, source_target_pairs={{0,8},{4,12},{8,0},{12,4},{1,9},{5,13},{9,1},{13,5},{2,10},{6,14},... | collective-permute-start | bytes 589832 | tf_op jit(solution)/shard_map/ppermute | solution.py:300
  19.3 11.3 %collective-permute-start.2 = (f32[48,1024]{1,0:T(8,128)S(1)}, f32[48,1024]{1,0:T(8,128)S(1)}, u32[]{:S(2)}, u32[]{:S(2)}) collective-permute-start(f32[48,1024]{1,0:T(8,128)S(1)} %get-tuple-element.126), channel_id=1, source_target_pairs={{0,12},{4,0},{8,4},{12,8},{1,13},{5,1},{9,5},{13,9},{2,14},{6,2},{... | collective-permute-start | bytes 589832 | tf_op jit(solution)/shard_map/ppermute | solution.py:300
  30.6 21.9 %collective-permute-start.3 = (f32[48,1024]{1,0:T(8,128)S(1)}, f32[48,1024]{1,0:T(8,128)S(1)}, u32[]{:S(2)}, u32[]{:S(2)}) collective-permute-start(f32[48,1024]{1,0:T(8,128)S(1)} %get-tuple-element.55), channel_id=1, source_target_pairs={{0,4},{4,8},{8,12},{12,0},{1,5},{5,9},{9,13},{13,1},{2,6},{6,10},{... | collective-permute-start | bytes 589832 | tf_op jit(solution)/shard_map/ppermute | solution.py:300
  32.4 20.1 %collective-permute-start.4 = (f32[48,1024]{1,0:T(8,128)S(1)}, f32[48,1024]{1,0:T(8,128)S(1)}, u32[]{:S(2)}, u32[]{:S(2)}) collective-permute-start(f32[48,1024]{1,0:T(8,128)S(1)} %get-tuple-element.56), channel_id=1, source_target_pairs={{0,8},{4,12},{8,0},{12,4},{1,9},{5,13},{9,1},{13,5},{2,10},{6,14},... | collective-permute-start | bytes 589832 | tf_op jit(solution)/shard_map/ppermute | solution.py:300
  33.9 18.6 %collective-permute-start.5 = (f32[48,1024]{1,0:T(8,128)S(1)}, f32[48,1024]{1,0:T(8,128)S(1)}, u32[]{:S(2)}, u32[]{:S(2)}) collective-permute-start(f32[48,1024]{1,0:T(8,128)S(1)} %get-tuple-element.57), channel_id=1, source_target_pairs={{0,12},{4,0},{8,4},{12,8},{1,13},{5,1},{9,5},{13,9},{2,14},{6,2},{... | collective-permute-start | bytes 589832 | tf_op jit(solution)/shard_map/ppermute | solution.py:300
  52.5 19.1 %collective-permute-start.10 = (f32[8,6,8,128]{3,2,1,0:T(8,128)S(1)}, f32[8,6,8,128]{3,2,1,0:T(8,128)S(1)}, u32[]{:S(2)}, u32[]{:S(2)}) collective-permute-start(f32[8,6,8,128]{3,2,1,0:T(8,128)S(1)} %get-tuple-element.68), channel_id=1, source_target_pairs={{0,8},{4,12},{8,0},{12,4},{1,9},{5,13},{9,1},{13,5},{2,10},{6,14},... | collective-permute-start | bytes 589832 | tf_op jit(solution)/shard_map/ppermute | solution.py:300
  53.4 19.6 %collective-permute-start.11 = (f32[8,6,8,128]{3,2,1,0:T(8,128)S(1)}, f32[8,6,8,128]{3,2,1,0:T(8,128)S(1)}, u32[]{:S(2)}, u32[]{:S(2)}) collective-permute-start(f32[8,6,8,128]{3,2,1,0:T(8,128)S(1)} %get-tuple-element.69), channel_id=1, source_target_pairs={{0,12},{4,0},{8,4},{12,8},{1,13},{5,1},{9,5},{13,9},{2,14},{6,2},{... | collective-permute-start | bytes 589832 | tf_op jit(solution)/shard_map/ppermute | solution.py:300
  55.2 17.8 %collective-permute-start.9 = (f32[8,6,8,128]{3,2,1,0:T(8,128)S(1)}, f32[8,6,8,128]{3,2,1,0:T(8,128)S(1)}, u32[]{:S(2)}, u32[]{:S(2)}) collective-permute-start(f32[8,6,8,128]{3,2,1,0:T(8,128)S(1)} %get-tuple-element.67), channel_id=1, source_target_pairs={{0,4},{4,8},{8,12},{12,0},{1,5},{5,9},{9,13},{13,1},{2,6},{6,10},{... | collective-permute-start | bytes 589832 | tf_op jit(solution)/shard_map/ppermute | solution.py:300
  73.0 20.9 %copy-start.1 = (s32[8,3]{0,1:T(4,128)S(1)}, s32[8,3]{0,1:T(4,128)}, u32[]{:S(2)}) copy-start(s32[8,3]{0,1:T(4,128)} %param.6) | copy-start | bytes 292
  73.1 20.3 %collective-permute-start.16 = (f32[4,8,6,8,128]{4,3,2,1,0:T(8,128)S(1)}, f32[4,8,6,8,128]{4,3,2,1,0:T(8,128)S(1)}, u32[]{:S(2)}, u32[]{:S(2)}) collective-permute-start(f32[4,8,6,8,128]{4,3,2,1,0:T(8,128)S(1)} %pad_maximum_fusion.1.refs_0_.refs_4_), channel_id=1, source_target_pairs={{0,2},{1,3},{2,0},{3,1},{4,6},{5,7},{6,4},{7,5},{8,10},{9,11},{10,... | collective-permute-start | bytes 2359304 | tf_op jit(solution)/shard_map/ppermute | solution.py:311
  73.5 5.7 %collective-permute-start.12 = (f32[8,6,8,128]{3,2,1,0:T(8,128)S(1)}, f32[8,6,8,128]{3,2,1,0:T(8,128)S(1)}, u32[]{:S(2)}, u32[]{:S(2)}) collective-permute-start(f32[8,6,8,128]{3,2,1,0:T(8,128)S(1)} %get-tuple-element.80), channel_id=1, source_target_pairs={{0,4},{4,8},{8,12},{12,0},{1,5},{5,9},{9,13},{13,1},{2,6},{6,10},{... | collective-permute-start | bytes 589832 | tf_op jit(solution)/shard_map/ppermute | solution.py:300
  73.8 14.6 %collective-permute-start.13 = (f32[8,6,8,128]{3,2,1,0:T(8,128)S(1)}, f32[8,6,8,128]{3,2,1,0:T(8,128)S(1)}, u32[]{:S(2)}, u32[]{:S(2)}) collective-permute-start(f32[8,6,8,128]{3,2,1,0:T(8,128)S(1)} %get-tuple-element.81), channel_id=1, source_target_pairs={{0,8},{4,12},{8,0},{12,4},{1,9},{5,13},{9,1},{13,5},{2,10},{6,14},... | collective-permute-start | bytes 589832 | tf_op jit(solution)/shard_map/ppermute | solution.py:300
  75.3 18.0 %collective-permute-start.14 = (f32[8,6,8,128]{3,2,1,0:T(8,128)S(1)}, f32[8,6,8,128]{3,2,1,0:T(8,128)S(1)}, u32[]{:S(2)}, u32[]{:S(2)}) collective-permute-start(f32[8,6,8,128]{3,2,1,0:T(8,128)S(1)} %get-tuple-element.82), channel_id=1, source_target_pairs={{0,12},{4,0},{8,4},{12,8},{1,13},{5,1},{9,5},{13,9},{2,14},{6,2},{... | collective-permute-start | bytes 589832 | tf_op jit(solution)/shard_map/ppermute | solution.py:300
  76.2 19.6 %collective-permute-start.17 = (f32[4,8,6,8,128]{4,3,2,1,0:T(8,128)S(1)}, f32[4,8,6,8,128]{4,3,2,1,0:T(8,128)S(1)}, u32[]{:S(2)}, u32[]{:S(2)}) collective-permute-start(f32[4,8,6,8,128]{4,3,2,1,0:T(8,128)S(1)} %pad_maximum_fusion.1.refs_0_.refs_4_), channel_id=1, source_target_pairs={{0,1},{1,0},{2,3},{3,2},{4,5},{5,4},{6,7},{7,6},{8,9},{9,8},{10,11... | collective-permute-start | bytes 2359304 | tf_op jit(solution)/shard_map/ppermute | solution.py:319
  93.4 2.5 %collective-permute-start.18 = (f32[4,8,6,8,128]{4,3,2,1,0:T(8,128)S(1)}, f32[4,8,6,8,128]{4,3,2,1,0:T(8,128)S(1)}, u32[]{:S(2)}, u32[]{:S(2)}) collective-permute-start(f32[4,8,6,8,128]{4,3,2,1,0:T(8,128)S(1)} %collective-permute-done.16.refs_1_), channel_id=1, source_target_pairs={{0,1},{1,0},{2,3},{3,2},{4,5},{5,4},{6,7},{7,6},{8,9},{9,8},{10,11... | collective-permute-start | bytes 2359304 | tf_op jit(solution)/shard_map/ppermute | solution.py:319
  94.3 19.2 %collective-permute-start.15 = (f32[4,8,6,8,128]{4,3,2,1,0:T(8,128)S(1)}, f32[4,8,6,8,128]{4,3,2,1,0:T(8,128)S(1)}, u32[]{:S(2)}, u32[]{:S(2)}) collective-permute-start(f32[4,8,6,8,128]{4,3,2,1,0:T(8,128)S(1)} %pad_maximum_fusion.refs_5_.refs_0_), channel_id=1, source_target_pairs={{0,2},{1,3},{2,0},{3,1},{4,6},{5,7},{6,4},{7,5},{8,10},{9,11},{10,... | collective-permute-start | bytes 2359304 | tf_op jit(solution)/shard_map/ppermute | solution.py:311
  95.5 21.0 %collective-permute-start.22 = (f32[4,8,6,8,128]{4,3,2,1,0:T(8,128)S(1)}, f32[4,8,6,8,128]{4,3,2,1,0:T(8,128)S(1)}, u32[]{:S(2)}, u32[]{:S(2)}) collective-permute-start(f32[4,8,6,8,128]{4,3,2,1,0:T(8,128)S(1)} %pad_maximum_fusion.refs_5_.refs_0_), channel_id=1, source_target_pairs={{0,1},{1,0},{2,3},{3,2},{4,5},{5,4},{6,7},{7,6},{8,9},{9,8},{10,11... | collective-permute-start | bytes 2359304 | tf_op jit(solution)/shard_map/ppermute | solution.py:319
  113.5 3.1 %collective-permute-start.23 = (f32[4,8,6,8,128]{4,3,2,1,0:T(8,128)S(1)}, f32[4,8,6,8,128]{4,3,2,1,0:T(8,128)S(1)}, u32[]{:S(2)}, u32[]{:S(2)}) collective-permute-start(f32[4,8,6,8,128]{4,3,2,1,0:T(8,128)S(1)} %collective-permute-done.15.refs_1_), channel_id=1, source_target_pairs={{0,1},{1,0},{2,3},{3,2},{4,5},{5,4},{6,7},{7,6},{8,9},{9,8},{10,11... | collective-permute-start | bytes 2359304 | tf_op jit(solution)/shard_map/ppermute | solution.py:319
  114.2 23.3 %collective-permute-start.19 = (f32[32,2048]{1,0:T(8,128)S(1)}, f32[32,2048]{1,0:T(8,128)S(1)}, u32[]{:S(2)}, u32[]{:S(2)}) collective-permute-start(f32[32,2048]{1,0:T(8,128)S(1)} %get-tuple-element.95), channel_id=1, source_target_pairs={{0,4},{4,8},{8,12},{12,0},{1,5},{5,9},{9,13},{13,1},{2,6},{6,10},{... | collective-permute-start | bytes 786440 | tf_op jit(solution)/shard_map/ppermute | solution.py:300
  114.2 23.3 %collective-permute-start.20 = (f32[32,2048]{1,0:T(8,128)S(1)}, f32[32,2048]{1,0:T(8,128)S(1)}, u32[]{:S(2)}, u32[]{:S(2)}) collective-permute-start(f32[32,2048]{1,0:T(8,128)S(1)} %get-tuple-element.96), channel_id=1, source_target_pairs={{0,8},{4,12},{8,0},{12,4},{1,9},{5,13},{9,1},{13,5},{2,10},{6,14},... | collective-permute-start | bytes 786440 | tf_op jit(solution)/shard_map/ppermute | solution.py:300
  115.1 23.7 %collective-permute-start.21 = (f32[32,2048]{1,0:T(8,128)S(1)}, f32[32,2048]{1,0:T(8,128)S(1)}, u32[]{:S(2)}, u32[]{:S(2)}) collective-permute-start(f32[32,2048]{1,0:T(8,128)S(1)} %get-tuple-element.97), channel_id=1, source_target_pairs={{0,12},{4,0},{8,4},{12,8},{1,13},{5,1},{9,5},{13,9},{2,14},{6,2},{... | collective-permute-start | bytes 786440 | tf_op jit(solution)/shard_map/ppermute | solution.py:300
  134.2 19.7 %collective-permute-start.24 = (f32[32,2048]{1,0:T(8,128)S(1)}, f32[32,2048]{1,0:T(8,128)S(1)}, u32[]{:S(2)}, u32[]{:S(2)}) collective-permute-start(f32[32,2048]{1,0:T(8,128)S(1)} %get-tuple-element.100), channel_id=1, source_target_pairs={{0,4},{4,8},{8,12},{12,0},{1,5},{5,9},{9,13},{13,1},{2,6},{6,10},{... | collective-permute-start | bytes 786440 | tf_op jit(solution)/shard_map/ppermute | solution.py:300
  134.6 24.9 %collective-permute-start.25 = (f32[32,2048]{1,0:T(8,128)S(1)}, f32[32,2048]{1,0:T(8,128)S(1)}, u32[]{:S(2)}, u32[]{:S(2)}) collective-permute-start(f32[32,2048]{1,0:T(8,128)S(1)} %get-tuple-element.101), channel_id=1, source_target_pairs={{0,8},{4,12},{8,0},{12,4},{1,9},{5,13},{9,1},{13,5},{2,10},{6,14},... | collective-permute-start | bytes 786440 | tf_op jit(solution)/shard_map/ppermute | solution.py:300
  137.5 23.7 %collective-permute-start.26 = (f32[32,2048]{1,0:T(8,128)S(1)}, f32[32,2048]{1,0:T(8,128)S(1)}, u32[]{:S(2)}, u32[]{:S(2)}) collective-permute-start(f32[32,2048]{1,0:T(8,128)S(1)} %get-tuple-element.102), channel_id=1, source_target_pairs={{0,12},{4,0},{8,4},{12,8},{1,13},{5,1},{9,5},{13,9},{2,14},{6,2},{... | collective-permute-start | bytes 786440 | tf_op jit(solution)/shard_map/ppermute | solution.py:300

commit v4 on v3

--- a/solution.py
+++ b/solution.py
@@ -93,12 +93,12 @@
     def at(x, q):
         return x * QP + q
 
-    def moved(get, n, axis, step):
-        x, q = n // QP, lax.rem(n, QP)
+    def moved(get, x, q, axis, step):
+        n = at(x, q)
         if axis == 0:
             return get(at(lax.rem(x + step + lx, lx), q))
         if axis == 1:
-            here, there = get(n), get(at(x, lax.rem(q + step + QP, QP)))
+            here, there = get(n), get(at(x, (q + step) % QP))
             if step > 0:
                 return rolled(jnp.where(lane < LZ, there, here), LANES - LZ)
             return rolled(jnp.where(lane >= LANES - LZ, there, here), LZ)
@@ -120,22 +120,24 @@
                 share = link_ref.shape[3] // LANES
                 lanes = slice(k % share * LANES, (k % share + 1) * LANES)
                 for m in range(3):
-                    l_ref[m, t * kt + k] = link_ref[k // share, s, 18 * m : 18 * m + 18, lanes]
+                    l_ref[m, s * kt + k] = link_ref[k // share, s, 18 * m : 18 * m + 18, lanes]
 
     if with_links:
 
-        def shift_links(n, carry):
-            for m in range(3):
-                l_ref[3 + m, n] = moved(lambda i: l_ref[m, i], n, m, -1)
+        def shift_links(x, carry):
+            for q in range(QP):
+                for m in range(3):
+                    l_ref[3 + m, at(x, q)] = moved(lambda i: l_ref[m, i], x, q, m, -1)
             return carry
 
-        lax.fori_loop(0, nt, shift_links, 0)
-
-    def hop(src, n):
+        lax.fori_loop(0, lx, shift_links, 0)
+
+    def hop(src, x, q):
+        n = at(x, q)
         acc = [None] * comps
         for m in range(3):
             for side in (0, 1):
-                near = [moved(lambda i: src[i, c], n, m, 1 - 2 * side) for c in range(comps)]
+                near = [moved(lambda i: src[i, c], x, q, m, 1 - 2 * side) for c in range(comps)]
                 for i in range(3):
                     for j in range(3):
                         row = i * 3 + j if side == 0 else j * 3 + i
@@ -155,16 +157,18 @@
     src, dst = a_ref, b_ref
     for order in range(ITERS):
 
-        def body(n, carry, src=src, dst=dst, order=order):
-            acc = hop(src, n)
-            for c in range(comps):
-                if order == 0:
-                    dst[n, c] = hop_scale * acc[c]
-                else:
-                    dst[n, c] = (2.0 * hop_scale) * acc[c] - dst[n, c]
+        def body(x, carry, src=src, dst=dst, order=order):
+            for q in range(QP):
+                n = x * QP + q
+                acc = hop(src, x, q)
+                for c in range(comps):
+                    if order == 0:
+                        dst[n, c] = hop_scale * acc[c]
+                    else:
+                        dst[n, c] = (2.0 * hop_scale) * acc[c] - dst[n, c]
             return carry
 
-        lax.fori_loop(0, nt, body, 0)
+        lax.fori_loop(0, lx, body, 0)
         src, dst = dst, src
 
     for mode in range(3):
@@ -356,12 +360,13 @@
     parts = jnp.transpose(parts, (2, 1, 0, 3, 4)).reshape(chunks, tiles, 6 * nvc, sites)
     share = sites // vecs
     link_share = lax.dynamic_slice_in_dim(links.reshape(54, sites), lax.axis_index("vec") * share, share, 1)
-    gauge = lax.all_gather(jnp.stack([along_tiles(link_share, s) for s in range(tiles)]), "vec", axis=0)
+    gauge = lax.all_gather(link_share, ("vec", "tile"), axis=0).reshape(vecs, tiles, 54, share)
     fields = []
     for c in range(chunks):
         sent = [lax.dynamic_index_in_dim(parts[c], lax.rem(tile + s, tiles), 0, keepdims=False) for s in range(tiles)]
         if c > 0:
-            fields[c - 1], sent = lax.optimization_barrier((fields[c - 1], sent))
+            for s in range(1, tiles):
+                fields[c - 1][s], sent[s] = lax.optimization_barrier((fields[c - 1][s], sent[s]))
         fields.append([along_tiles(block, s) for s, block in enumerate(sent)])
 
     piece_shapes = (jax.ShapeDtypeStruct((kt, 6, nvc, LANES), f32),) * tiles

time: 163 us -> 187 us (1.15)
  blocking collectives: 11.2 us -> 41 us
  Pallas kernels: 69.6 us -> 55.7 us
  waiting for transfers between devices: 39.5 us -> 48.5 us
    all_gather x1, blocking collectives: 11.2 us -> 41 us  [local(): lax.all_gather(link_share, ('vec', 'tile'), axis=0)]
    ppermute x21 -> x18, waiting for transfers between devices: 39.5 us -> 48.4 us  [along_tiles(): lax.ppermute(value, 'tile', [(i, (i + steps) % count) for i in range(coun...]
    pallas_call x1, Pallas kernels: 18.5 us -> 10.7 us  [local(): call(out_shape=(*piece_shapes, jax.ShapeDtypeStruct((slots, kt, 18, LANES...]
    pallas_call x1, Pallas kernels: 15.9 us -> 9.77 us  [local(): call(out_shape=piece_shapes, in_specs=[smem] + [vmem] * (tiles + 1), out_...]
    ppermute x21 -> x18, starting transfers between devices: 21.9 us -> 21 us  [along_tiles(): lax.ppermute(value, 'tile', [(i, (i + steps) % count) for i in range(coun...]
  transfers between devices with their start and end apart: 27 -> 24, of which waited for: 8 -> 9; matrix products, arithmetic and copies ran while one was open for 3% -> 2% of each run, Pallas kernels for 43% -> 30%
where the time goes in v4:
time: 187 us; the launch traced here: 186 us
  Pallas kernels  55.7 us (30%)
  waiting for transfers between devices  48.5 us (26%)
  blocking collectives  41 us (22%)
  starting transfers between devices  27.1 us (14%)
  between operations  6.54 us (3%)
  local copies, waits for them, and re-layouts  4.8 us (3%)
  other arithmetic  2.64 us (1%)
    ppermute x18, waiting for transfers between devices, along_tiles(): lax.ppermute(value, 'tile', [(i, (i + steps) % count) for i in range(coun...  48.4 us
    all_gather x1, blocking collectives, local(): lax.all_gather(link_share, ('vec', 'tile'), axis=0)  41 us
    pallas_call x2, Pallas kernels, local(): pl.pallas_call(functools.partial(contract_kernel, vecs, chunks, slots, mo...  35.2 us
    ppermute x18, starting transfers between devices, along_tiles(): lax.ppermute(value, 'tile', [(i, (i + steps) % count) for i in range(coun...  21 us
    pallas_call x1, Pallas kernels, local(): call(out_shape=(*piece_shapes, jax.ShapeDtypeStruct((slots, kt, 18, LANES...  10.7 us
    pallas_call x1, Pallas kernels, local(): call(out_shape=piece_shapes, in_specs=[smem] + [vmem] * (tiles + 1), out_...  9.77 us
    ppermute x4, starting transfers between devices, over_cores(): lax.ppermute(block, 'vec', [(i, i ^ 1) for i in range(count)])  4.68 us
  transfers between devices with their start and end apart: 24, of which 9 were waited for; matrix products, arithmetic and copies ran while one was open for 2% of the time, Pallas kernels for 30%

profile of v4, /device:TPU:9, one launch (start us, length us, event | category | flops | bytes accessed | tf_op | source)
XLA Modules:
  0.0 186.4 jit_solution(3438105840772472790)
XLA Ops:
  0.0 1.5 fusion.90
  1.8 2.5 %collective-permute-start.2 = (f32[48,1024]{1,0:T(8,128)S(1)}, f32[48,1024]{1,0:T(8,128)S(1)}, u32[]{:S(2)}, u32[]{:S(2)}) collective-permute-start(f32[48,1024]{1,0:T(8,128)S(1)} %get-tuple-element.120), channel_id=1, source_target_pairs={{0,8},{4,12},{8,0},{12,4},{1,9},{5,13},{9,1},{13,5},{2,10},{6,14},... | collective-permute-start | bytes 589832 | tf_op jit(solution)/shard_map/ppermute | solution.py:304
  4.3 2.2 %collective-permute-start = (f32[48,1024]{1,0:T(8,128)S(1)}, f32[48,1024]{1,0:T(8,128)S(1)}, u32[]{:S(2)}, u32[]{:S(2)}) collective-permute-start(f32[48,1024]{1,0:T(8,128)S(1)} %get-tuple-element.121), channel_id=1, source_target_pairs={{0,4},{4,8},{8,12},{12,0},{1,5},{5,9},{9,13},{13,1},{2,6},{6,10},{... | collective-permute-start | bytes 589832 | tf_op jit(solution)/shard_map/ppermute | solution.py:304
  6.5 0.7 compare_reduce_fusion
  9.2 0.7 fusion.91
  15.0 41.0 %all-gather.1 = f32[16,54,256]{2,1,0:T(8,128)S(1)} all-gather(f32[1,54,256]{2,1,0:T(8,128)S(1)} %dynamic-slice_bitcast_fusion.8), channel_id=2, replica_groups=mesh['groups'=2,'tile'=4,'vec'=4] {'vec','tile'}, dimensions={0}, use_global_device_ids=true | all-gather | bytes 940032 | tf_op jit(solution)/shard_map/all_gather | solution.py:363
  57.4 0.8 collective-permute-start.5
  58.2 1.8 collective-permute-start.3
  60.0 2.3 %collective-permute-start.1 = (f32[48,1024]{1,0:T(8,128)S(1)}, f32[48,1024]{1,0:T(8,128)S(1)}, u32[]{:S(2)}, u32[]{:S(2)}) collective-permute-start(f32[48,1024]{1,0:T(8,128)S(1)} %get-tuple-element.52), channel_id=1, source_target_pairs={{0,4},{4,8},{8,12},{12,0},{1,5},{5,9},{9,13},{13,1},{2,6},{6,10},{... | collective-permute-start | bytes 589832 | tf_op jit(solution)/shard_map/ppermute | solution.py:304
  62.2 10.7 %chebyshev.2 = (f32[8,6,8,128]{3,2,1,0:T(8,128)S(1)}, f32[8,6,8,128]{3,2,1,0:T(8,128)S(1)}, f32[8,6,8,128]{3,2,1,0:T(8,128)S(1)}, f32[8,6,8,128]{3,2,1,0:T(8,128...) custom-call(s32[4]{0:T(128)S(1)} %pad_add_fusion.2.refs_0_, ...), custom_call_target="tpu_custom_call" | custom-call | flops 14155776000 | bytes 1572864 | tf_op jit(solution)/shard_map/chebyshev/pallas_call | solution.py:388
  73.0 3.5 %collective-permute-done.1.refs_2_ = f32[48,1024]{1,0:T(8,128)S(1)} collective-permute-done((f32[48,1024]{1,0:T(8,128)S(1)}, f32[48,1024]{1,0:T(8,128)S(1)}, u32[]{:S(2)}, u32[]{:S(2)}) %collective-permute-start.1) | collective-permute-done | bytes 196640 | tf_op jit(solution)/shard_map/ppermute | solution.py:304
  76.4 2.2 %collective-permute-start.6 = (f32[8,6,8,128]{3,2,1,0:T(8,128)S(1)}, f32[8,6,8,128]{3,2,1,0:T(8,128)S(1)}, u32[]{:S(2)}, u32[]{:S(2)}) collective-permute-start(f32[8,6,8,128]{3,2,1,0:T(8,128)S(1)} %get-tuple-element.63), channel_id=1, source_target_pairs={{0,4},{4,8},{8,12},{12,0},{1,5},{5,9},{9,13},{13,1},{2,6},{6,10},{... | collective-permute-start | bytes 589832 | tf_op jit(solution)/shard_map/ppermute | solution.py:304
  78.6 0.8 collective-permute-start.7
  79.8 9.8 %chebyshev.3 = (f32[8,6,8,128]{3,2,1,0:T(8,128)S(1)}, f32[8,6,8,128]{3,2,1,0:T(8,128)S(1)}, f32[8,6,8,128]{3,2,1,0:T(8,128)S(1)}, f32[8,6,8,128]{3,2,1,0:T(8,128)S(1)}) custom-call(s32[4]{0:T(128)S(1)} %pad_add_fusion.2.refs_0_, f32[48,1024]{1,0:T(8,128)S(1)} %get-tuple-element.66.refs_1_, f32[48,1024]{1,0:T(8,128)S(1)} %collective-permute-done.1.refs_2_, ...), custom_call_target="tpu_custom_call" | custom-call | flops 14155776000 | bytes 1572864 | tf_op jit(solution)/shard_map/chebyshev/pallas_call | solution.py:398
  89.6 4.7 %collective-permute-done.7 = f32[8,6,8,128]{3,2,1,0:T(8,128)S(1)} collective-permute-done((f32[8,6,8,128]{3,2,1,0:T(8,128)S(1)}, f32[8,6,8,128]{3,2,1,0:T(8,128)S(1)}, u32[]{:S(2)}, u32[]{:S(2)}) %collective-permute-start.7) | collective-permute-done | bytes 196640 | tf_op jit(solution)/shard_map/ppermute | solution.py:304
  94.4 2.3 %collective-permute-done.8 = f32[8,6,8,128]{3,2,1,0:T(8,128)S(1)} collective-permute-done((f32[8,6,8,128]{3,2,1,0:T(8,128)S(1)}, f32[8,6,8,128]{3,2,1,0:T(8,128)S(1)}, u32[]{:S(2)}, u32[]{:S(2)}) %collective-permute-start.8) | collective-permute-done | bytes 196640 | tf_op jit(solution)/shard_map/ppermute | solution.py:304
  97.4 0.9 collective-permute-start.10
  98.3 1.4 collective-permute-start.11
  99.7 3.0 %collective-permute-start.14 = (f32[4,8,6,8,128]{4,3,2,1,0:T(8,128)S(1)}, f32[4,8,6,8,128]{4,3,2,1,0:T(8,128)S(1)}, u32[]{:S(2)}, u32[]{:S(2)}) collective-permute-start(f32[4,8,6,8,128]{4,3,2,1,0:T(8,128)S(1)} %pad_maximum_fusion.1.refs_0_.refs_4_), channel_id=1, source_target_pairs={{0,1},{1,0},{2,3},{3,2},{4,5},{5,4},{6,7},{7,6},{8,9},{9,8},{10,11... | collective-permute-start | bytes 2359304 | tf_op jit(solution)/shard_map/ppermute | solution.py:323
  102.7 10.7 %collective-permute-done.10 = f32[8,6,8,128]{3,2,1,0:T(8,128)S(1)} collective-permute-done((f32[8,6,8,128]{3,2,1,0:T(8,128)S(1)}, f32[8,6,8,128]{3,2,1,0:T(8,128)S(1)}, u32[]{:S(2)}, u32[]{:S(2)}) %collective-permute-start.10) | collective-permute-done | bytes 196640 | tf_op jit(solution)/shard_map/ppermute | solution.py:304
  113.4 2.8 %collective-permute-done.11 = f32[8,6,8,128]{3,2,1,0:T(8,128)S(1)} collective-permute-done((f32[8,6,8,128]{3,2,1,0:T(8,128)S(1)}, f32[8,6,8,128]{3,2,1,0:T(8,128)S(1)}, u32[]{:S(2)}, u32[]{:S(2)}) %collective-permute-start.11) | collective-permute-done | bytes 196640 | tf_op jit(solution)/shard_map/ppermute | solution.py:304
  117.2 1.1 collective-permute-start.12
  118.7 17.6 %contract.2 = (f32[32,2048]{1,0:T(8,128)S(1)}, f32[32,2048]{1,0:T(8,128)S(1)}, f32[32,2048]{1,0:T(8,128)S(1)}, f32[32,2048]{1,0:T(8,128)S(1)}) custom-call(s32[4,17]{1,0:T(4,128)S(1)} %pad_add_fusion.1.scal, f32[4,8,6,8,128]{4,3,2,1,0:T(8,128)S(1)} %pad_maximum_fusion.1.refs_0_.refs_4_, f32[4,8,6,8,128]{4,3,2,1,0:T(8,128)S(1)} %collective-permute-done.13.refs_1_, ...), custom_call_target="tpu_custom_call" | custom-call | flops 19327352832 | bytes 4194304 | tf_op jit(solution)/shard_map/contract/pallas_call | solution.py:465
  136.4 0.8 collective-permute-start.20
  137.1 1.6 collective-permute-start.17
  138.7 1.5 collective-permute-start.18
  140.2 17.6 %contract.3 = (f32[32,2048]{1,0:T(8,128)S(1)}, f32[32,2048]{1,0:T(8,128)S(1)}, f32[32,2048]{1,0:T(8,128)S(1)}, f32[32,2048]{1,0:T(8,128)S(1)}) custom-call(s32[4,17]{1,0:T(4,128)S(1)} %pad_add_fusion.1.scal, f32[4,8,6,8,128]{4,3,2,1,0:T(8,128)S(1)} %pad_maximum_fusion.refs_5_.refs_0_, f32[4,8,6,8,128]{4,3,2,1,0:T(8,128)S(1)} %collective-permute-done.12.refs_1_, ...), custom_call_target="tpu_custom_call" | custom-call | flops 19327352832 | bytes 4194304 | tf_op jit(solution)/shard_map/contract/pallas_call | solution.py:465
  157.9 2.6 %collective-permute-start.22 = (f32[32,2048]{1,0:T(8,128)S(1)}, f32[32,2048]{1,0:T(8,128)S(1)}, u32[]{:S(2)}, u32[]{:S(2)}) collective-permute-start(f32[32,2048]{1,0:T(8,128)S(1)} %get-tuple-element.97), channel_id=1, source_target_pairs={{0,8},{4,12},{8,0},{12,4},{1,9},{5,13},{9,1},{13,5},{2,10},{6,14},... | collective-permute-start | bytes 786440 | tf_op jit(solution)/shard_map/ppermute | solution.py:304
  160.5 12.7 %collective-permute-done.18 = f32[32,2048]{1,0:T(8,128)S(1)} collective-permute-done((f32[32,2048]{1,0:T(8,128)S(1)}, f32[32,2048]{1,0:T(8,128)S(1)}, u32[]{:S(2)}, u32[]{:S(2)}) %collective-permute-start.18) | collective-permute-done | bytes 262176 | tf_op jit(solution)/shard_map/ppermute | solution.py:304
  173.3 9.1 %collective-permute-done.22 = f32[32,2048]{1,0:T(8,128)S(1)} collective-permute-done((f32[32,2048]{1,0:T(8,128)S(1)}, f32[32,2048]{1,0:T(8,128)S(1)}, u32[]{:S(2)}, u32[]{:S(2)}) %collective-permute-start.22) | collective-permute-done | bytes 262176 | tf_op jit(solution)/shard_map/ppermute | solution.py:304
  182.4 2.4 %collective-permute-done.23 = f32[32,2048]{1,0:T(8,128)S(1)} collective-permute-done((f32[32,2048]{1,0:T(8,128)S(1)}, f32[32,2048]{1,0:T(8,128)S(1)}, u32[]{:S(2)}, u32[]{:S(2)}) %collective-permute-start.23) | collective-permute-done | bytes 262176 | tf_op jit(solution)/shard_map/ppermute | solution.py:304
  185.0 1.4 reshape.2017
  (67 shorter events, 5.2 us)
Async XLA Ops:
  1.7 4.8 %copy-start.1 = (s32[2]{0:T(128)S(1)}, s32[2]{0:T(128)}, u32[]{:S(2)}) copy-start(s32[2]{0:T(128)} %param.7) | copy-start | bytes 28
  1.7 13.1 %copy-start = (f32[3,2,3,3,1024]{4,1,3,2,0:T(2,128)S(1)}, f32[3,2,3,3,1024]{4,1,3,2,0:T(2,128)}, u32[]{:S(2)}) copy-start(f32[3,2,3,3,1024]{4,1,3,2,0:T(2,128)} %param.5) | copy-start | bytes 663556
  1.8 55.6 %collective-permute-start.4 = (f32[48,1024]{1,0:T(8,128)S(1)}, f32[48,1024]{1,0:T(8,128)S(1)}, u32[]{:S(2)}, u32[]{:S(2)}) collective-permute-start(f32[48,1024]{1,0:T(8,128)S(1)} %get-tuple-element.119), channel_id=1, source_target_pairs={{0,12},{4,0},{8,4},{12,8},{1,13},{5,1},{9,5},{13,9},{2,14},{6,2},{... | collective-permute-start | bytes 589832 | tf_op jit(solution)/shard_map/ppermute | solution.py:304
  1.8 55.5 %collective-permute-start.2 = (f32[48,1024]{1,0:T(8,128)S(1)}, f32[48,1024]{1,0:T(8,128)S(1)}, u32[]{:S(2)}, u32[]{:S(2)}) collective-permute-start(f32[48,1024]{1,0:T(8,128)S(1)} %get-tuple-element.120), channel_id=1, source_target_pairs={{0,8},{4,12},{8,0},{12,4},{1,9},{5,13},{9,1},{13,5},{2,10},{6,14},... | collective-permute-start | bytes 589832 | tf_op jit(solution)/shard_map/ppermute | solution.py:304
  4.3 53.1 %collective-permute-start = (f32[48,1024]{1,0:T(8,128)S(1)}, f32[48,1024]{1,0:T(8,128)S(1)}, u32[]{:S(2)}, u32[]{:S(2)}) collective-permute-start(f32[48,1024]{1,0:T(8,128)S(1)} %get-tuple-element.121), channel_id=1, source_target_pairs={{0,4},{4,8},{8,12},{12,0},{1,5},{5,9},{9,13},{13,1},{2,6},{6,10},{... | collective-permute-start | bytes 589832 | tf_op jit(solution)/shard_map/ppermute | solution.py:304
  57.4 15.6 %collective-permute-start.5 = (f32[48,1024]{1,0:T(8,128)S(1)}, f32[48,1024]{1,0:T(8,128)S(1)}, u32[]{:S(2)}, u32[]{:S(2)}) collective-permute-start(f32[48,1024]{1,0:T(8,128)S(1)} %get-tuple-element.54), channel_id=1, source_target_pairs={{0,12},{4,0},{8,4},{12,8},{1,13},{5,1},{9,5},{13,9},{2,14},{6,2},{... | collective-permute-start | bytes 589832 | tf_op jit(solution)/shard_map/ppermute | solution.py:304
  58.2 14.8 %collective-permute-start.3 = (f32[48,1024]{1,0:T(8,128)S(1)}, f32[48,1024]{1,0:T(8,128)S(1)}, u32[]{:S(2)}, u32[]{:S(2)}) collective-permute-start(f32[48,1024]{1,0:T(8,128)S(1)} %get-tuple-element.53), channel_id=1, source_target_pairs={{0,8},{4,12},{8,0},{12,4},{1,9},{5,13},{9,1},{13,5},{2,10},{6,14},... | collective-permute-start | bytes 589832 | tf_op jit(solution)/shard_map/ppermute | solution.py:304
  60.0 16.5 %collective-permute-start.1 = (f32[48,1024]{1,0:T(8,128)S(1)}, f32[48,1024]{1,0:T(8,128)S(1)}, u32[]{:S(2)}, u32[]{:S(2)}) collective-permute-start(f32[48,1024]{1,0:T(8,128)S(1)} %get-tuple-element.52), channel_id=1, source_target_pairs={{0,4},{4,8},{8,12},{12,0},{1,5},{5,9},{9,13},{13,1},{2,6},{6,10},{... | collective-permute-start | bytes 589832 | tf_op jit(solution)/shard_map/ppermute | solution.py:304
  76.4 13.2 %collective-permute-start.6 = (f32[8,6,8,128]{3,2,1,0:T(8,128)S(1)}, f32[8,6,8,128]{3,2,1,0:T(8,128)S(1)}, u32[]{:S(2)}, u32[]{:S(2)}) collective-permute-start(f32[8,6,8,128]{3,2,1,0:T(8,128)S(1)} %get-tuple-element.63), channel_id=1, source_target_pairs={{0,4},{4,8},{8,12},{12,0},{1,5},{5,9},{9,13},{13,1},{2,6},{6,10},{... | collective-permute-start | bytes 589832 | tf_op jit(solution)/shard_map/ppermute | solution.py:304
  78.6 15.7 %collective-permute-start.7 = (f32[8,6,8,128]{3,2,1,0:T(8,128)S(1)}, f32[8,6,8,128]{3,2,1,0:T(8,128)S(1)}, u32[]{:S(2)}, u32[]{:S(2)}) collective-permute-start(f32[8,6,8,128]{3,2,1,0:T(8,128)S(1)} %get-tuple-element.64), channel_id=1, source_target_pairs={{0,8},{4,12},{8,0},{12,4},{1,9},{5,13},{9,1},{13,5},{2,10},{6,14},... | collective-permute-start | bytes 589832 | tf_op jit(solution)/shard_map/ppermute | solution.py:304
  79.4 17.3 %collective-permute-start.8 = (f32[8,6,8,128]{3,2,1,0:T(8,128)S(1)}, f32[8,6,8,128]{3,2,1,0:T(8,128)S(1)}, u32[]{:S(2)}, u32[]{:S(2)}) collective-permute-start(f32[8,6,8,128]{3,2,1,0:T(8,128)S(1)} %get-tuple-element.65), channel_id=1, source_target_pairs={{0,12},{4,0},{8,4},{12,8},{1,13},{5,1},{9,5},{13,9},{2,14},{6,2},{... | collective-permute-start | bytes 589832 | tf_op jit(solution)/shard_map/ppermute | solution.py:304
  96.7 20.1 %copy-start.2 = (s32[8,3]{0,1:T(4,128)S(1)}, s32[8,3]{0,1:T(4,128)}, u32[]{:S(2)}) copy-start(s32[8,3]{0,1:T(4,128)} %param.6) | copy-start | bytes 292
  96.8 19.5 %collective-permute-start.13 = (f32[4,8,6,8,128]{4,3,2,1,0:T(8,128)S(1)}, f32[4,8,6,8,128]{4,3,2,1,0:T(8,128)S(1)}, u32[]{:S(2)}, u32[]{:S(2)}) collective-permute-start(f32[4,8,6,8,128]{4,3,2,1,0:T(8,128)S(1)} %pad_maximum_fusion.1.refs_0_.refs_4_), channel_id=1, source_target_pairs={{0,2},{1,3},{2,0},{3,1},{4,6},{5,7},{6,4},{7,5},{8,10},{9,11},{10,... | collective-permute-start | bytes 2359304 | tf_op jit(solution)/shard_map/ppermute | solution.py:315
  97.3 5.4 %collective-permute-start.9 = (f32[8,6,8,128]{3,2,1,0:T(8,128)S(1)}, f32[8,6,8,128]{3,2,1,0:T(8,128)S(1)}, u32[]{:S(2)}, u32[]{:S(2)}) collective-permute-start(f32[8,6,8,128]{3,2,1,0:T(8,128)S(1)} %get-tuple-element.76), channel_id=1, source_target_pairs={{0,4},{4,8},{8,12},{12,0},{1,5},{5,9},{9,13},{13,1},{2,6},{6,10},{... | collective-permute-start | bytes 589832 | tf_op jit(solution)/shard_map/ppermute | solution.py:304
  97.4 16.0 %collective-permute-start.10 = (f32[8,6,8,128]{3,2,1,0:T(8,128)S(1)}, f32[8,6,8,128]{3,2,1,0:T(8,128)S(1)}, u32[]{:S(2)}, u32[]{:S(2)}) collective-permute-start(f32[8,6,8,128]{3,2,1,0:T(8,128)S(1)} %get-tuple-element.77), channel_id=1, source_target_pairs={{0,8},{4,12},{8,0},{12,4},{1,9},{5,13},{9,1},{13,5},{2,10},{6,14},... | collective-permute-start | bytes 589832 | tf_op jit(solution)/shard_map/ppermute | solution.py:304
  98.3 17.9 %collective-permute-start.11 = (f32[8,6,8,128]{3,2,1,0:T(8,128)S(1)}, f32[8,6,8,128]{3,2,1,0:T(8,128)S(1)}, u32[]{:S(2)}, u32[]{:S(2)}) collective-permute-start(f32[8,6,8,128]{3,2,1,0:T(8,128)S(1)} %get-tuple-element.78), channel_id=1, source_target_pairs={{0,12},{4,0},{8,4},{12,8},{1,13},{5,1},{9,5},{13,9},{2,14},{6,2},{... | collective-permute-start | bytes 589832 | tf_op jit(solution)/shard_map/ppermute | solution.py:304
  99.7 18.9 %collective-permute-start.14 = (f32[4,8,6,8,128]{4,3,2,1,0:T(8,128)S(1)}, f32[4,8,6,8,128]{4,3,2,1,0:T(8,128)S(1)}, u32[]{:S(2)}, u32[]{:S(2)}) collective-permute-start(f32[4,8,6,8,128]{4,3,2,1,0:T(8,128)S(1)} %pad_maximum_fusion.1.refs_0_.refs_4_), channel_id=1, source_target_pairs={{0,1},{1,0},{2,3},{3,2},{4,5},{5,4},{6,7},{7,6},{8,9},{9,8},{10,11... | collective-permute-start | bytes 2359304 | tf_op jit(solution)/shard_map/ppermute | solution.py:323
  116.3 2.5 %collective-permute-start.15 = (f32[4,8,6,8,128]{4,3,2,1,0:T(8,128)S(1)}, f32[4,8,6,8,128]{4,3,2,1,0:T(8,128)S(1)}, u32[]{:S(2)}, u32[]{:S(2)}) collective-permute-start(f32[4,8,6,8,128]{4,3,2,1,0:T(8,128)S(1)} %collective-permute-done.13.refs_1_), channel_id=1, source_target_pairs={{0,1},{1,0},{2,3},{3,2},{4,5},{5,4},{6,7},{7,6},{8,9},{9,8},{10,11... | collective-permute-start | bytes 2359304 | tf_op jit(solution)/shard_map/ppermute | solution.py:323
  117.2 19.2 %collective-permute-start.12 = (f32[4,8,6,8,128]{4,3,2,1,0:T(8,128)S(1)}, f32[4,8,6,8,128]{4,3,2,1,0:T(8,128)S(1)}, u32[]{:S(2)}, u32[]{:S(2)}) collective-permute-start(f32[4,8,6,8,128]{4,3,2,1,0:T(8,128)S(1)} %pad_maximum_fusion.refs_5_.refs_0_), channel_id=1, source_target_pairs={{0,2},{1,3},{2,0},{3,1},{4,6},{5,7},{6,4},{7,5},{8,10},{9,11},{10,... | collective-permute-start | bytes 2359304 | tf_op jit(solution)/shard_map/ppermute | solution.py:315
  118.3 21.9 %collective-permute-start.19 = (f32[4,8,6,8,128]{4,3,2,1,0:T(8,128)S(1)}, f32[4,8,6,8,128]{4,3,2,1,0:T(8,128)S(1)}, u32[]{:S(2)}, u32[]{:S(2)}) collective-permute-start(f32[4,8,6,8,128]{4,3,2,1,0:T(8,128)S(1)} %pad_maximum_fusion.refs_5_.refs_0_), channel_id=1, source_target_pairs={{0,1},{1,0},{2,3},{3,2},{4,5},{5,4},{6,7},{7,6},{8,9},{9,8},{10,11... | collective-permute-start | bytes 2359304 | tf_op jit(solution)/shard_map/ppermute | solution.py:323
  136.4 3.8 %collective-permute-start.20 = (f32[4,8,6,8,128]{4,3,2,1,0:T(8,128)S(1)}, f32[4,8,6,8,128]{4,3,2,1,0:T(8,128)S(1)}, u32[]{:S(2)}, u32[]{:S(2)}) collective-permute-start(f32[4,8,6,8,128]{4,3,2,1,0:T(8,128)S(1)} %collective-permute-done.12.refs_1_), channel_id=1, source_target_pairs={{0,1},{1,0},{2,3},{3,2},{4,5},{5,4},{6,7},{7,6},{8,9},{9,8},{10,11... | collective-permute-start | bytes 2359304 | tf_op jit(solution)/shard_map/ppermute | solution.py:323
  137.1 23.3 %collective-permute-start.16 = (f32[32,2048]{1,0:T(8,128)S(1)}, f32[32,2048]{1,0:T(8,128)S(1)}, u32[]{:S(2)}, u32[]{:S(2)}) collective-permute-start(f32[32,2048]{1,0:T(8,128)S(1)} %get-tuple-element.91), channel_id=1, source_target_pairs={{0,4},{4,8},{8,12},{12,0},{1,5},{5,9},{9,13},{13,1},{2,6},{6,10},{... | collective-permute-start | bytes 786440 | tf_op jit(solution)/shard_map/ppermute | solution.py:304
  137.1 23.3 %collective-permute-start.17 = (f32[32,2048]{1,0:T(8,128)S(1)}, f32[32,2048]{1,0:T(8,128)S(1)}, u32[]{:S(2)}, u32[]{:S(2)}) collective-permute-start(f32[32,2048]{1,0:T(8,128)S(1)} %get-tuple-element.92), channel_id=1, source_target_pairs={{0,8},{4,12},{8,0},{12,4},{1,9},{5,13},{9,1},{13,5},{2,10},{6,14},... | collective-permute-start | bytes 786440 | tf_op jit(solution)/shard_map/ppermute | solution.py:304
  138.7 34.5 %collective-permute-start.18 = (f32[32,2048]{1,0:T(8,128)S(1)}, f32[32,2048]{1,0:T(8,128)S(1)}, u32[]{:S(2)}, u32[]{:S(2)}) collective-permute-start(f32[32,2048]{1,0:T(8,128)S(1)} %get-tuple-element.93), channel_id=1, source_target_pairs={{0,12},{4,0},{8,4},{12,8},{1,13},{5,1},{9,5},{13,9},{2,14},{6,2},{... | collective-permute-start | bytes 786440 | tf_op jit(solution)/shard_map/ppermute | solution.py:304
  157.8 15.5 %collective-permute-start.21 = (f32[32,2048]{1,0:T(8,128)S(1)}, f32[32,2048]{1,0:T(8,128)S(1)}, u32[]{:S(2)}, u32[]{:S(2)}) collective-permute-start(f32[32,2048]{1,0:T(8,128)S(1)} %get-tuple-element.96), channel_id=1, source_target_pairs={{0,4},{4,8},{8,12},{12,0},{1,5},{5,9},{9,13},{13,1},{2,6},{6,10},{... | collective-permute-start | bytes 786440 | tf_op jit(solution)/shard_map/ppermute | solution.py:304
  157.9 24.6 %collective-permute-start.22 = (f32[32,2048]{1,0:T(8,128)S(1)}, f32[32,2048]{1,0:T(8,128)S(1)}, u32[]{:S(2)}, u32[]{:S(2)}) collective-permute-start(f32[32,2048]{1,0:T(8,128)S(1)} %get-tuple-element.97), channel_id=1, source_target_pairs={{0,8},{4,12},{8,0},{12,4},{1,9},{5,13},{9,1},{13,5},{2,10},{6,14},... | collective-permute-start | bytes 786440 | tf_op jit(solution)/shard_map/ppermute | solution.py:304
  160.5 24.4 %collective-permute-start.23 = (f32[32,2048]{1,0:T(8,128)S(1)}, f32[32,2048]{1,0:T(8,128)S(1)}, u32[]{:S(2)}, u32[]{:S(2)}) collective-permute-start(f32[32,2048]{1,0:T(8,128)S(1)} %get-tuple-element.98), channel_id=1, source_target_pairs={{0,12},{4,0},{8,4},{12,8},{1,13},{5,1},{9,5},{13,9},{2,14},{6,2},{... | collective-permute-start | bytes 786440 | tf_op jit(solution)/shard_map/ppermute | solution.py:304

commit v5 on v4

--- a/solution.py
+++ b/solution.py
@@ -120,7 +120,7 @@
                 share = link_ref.shape[3] // LANES
                 lanes = slice(k % share * LANES, (k % share + 1) * LANES)
                 for m in range(3):
-                    l_ref[m, s * kt + k] = link_ref[k // share, s, 18 * m : 18 * m + 18, lanes]
+                    l_ref[m, t * kt + k] = link_ref[k // share, s, 18 * m : 18 * m + 18, lanes]
 
     if with_links:
 
@@ -264,7 +264,7 @@
                     disp[slot, i, at, :] = dr
                     disp[slot, 3 + i, at, :] = di
 
-    for g in range(slots * moms // per):
+    def twist(g):
         for r in range(per):
             slot, p = divmod(g * per + r, moms)
             co = trig_ref[k, p : p + 1, :]
@@ -276,6 +276,8 @@
                     first = part * half + i * LANES
                     dhi[g, r * cols : (r + 1) * cols, first : first + LANES] = high
                     dlo[g, r * cols : (r + 1) * cols, first : first + LANES] = low
+
+    def multiply(g):
         high, low = dhi[g], dlo[g]
         acc_ref[g * group : (g + 1) * group, :] += lax.dot_general(
             jnp.concatenate([high, high, low], axis=1),
@@ -283,6 +285,13 @@
             (((1,), (1,)), ((), ())),
             preferred_element_type=jnp.float32,
         )
+
+    groups = dhi.shape[0]
+    twist(0)
+    for g in range(groups):
+        if g + 1 < groups:
+            twist(g + 1)
+        multiply(g)
 
     @pl.when(k == kt - 1)
     def _():
@@ -360,7 +369,7 @@
     parts = jnp.transpose(parts, (2, 1, 0, 3, 4)).reshape(chunks, tiles, 6 * nvc, sites)
     share = sites // vecs
     link_share = lax.dynamic_slice_in_dim(links.reshape(54, sites), lax.axis_index("vec") * share, share, 1)
-    gauge = lax.all_gather(link_share, ("vec", "tile"), axis=0).reshape(vecs, tiles, 54, share)
+    gauge = lax.all_gather(jnp.stack([along_tiles(link_share, s) for s in range(tiles)]), "vec", axis=0)
     fields = []
     for c in range(chunks):
         sent = [lax.dynamic_index_in_dim(parts[c], lax.rem(tile + s, tiles), 0, keepdims=False) for s in range(tiles)]
@@ -394,6 +403,8 @@
                 in_specs=[smem] + [vmem] * (tiles + 1),
                 out_specs=(vmem,) * (tiles + 2),
             )(scal, *fields[c], gauge)
+            glink, momenta, directions = lax.optimization_barrier((glink, momenta, directions))
+            heading = directions % 3
         else:
             pieces = call(out_shape=piece_shapes, in_specs=[smem] + [vmem] * (tiles + 1), out_specs=(vmem,) * tiles)(
                 scal, *fields[c], turned

time: 187 us -> 173 us (0.925)
  blocking collectives: 41 us -> 11.5 us
  waiting for transfers between devices: 48.5 us -> 63.9 us
  starting transfers between devices: 27.1 us -> 24.8 us
    all_gather x1, blocking collectives: 41 us -> 11.5 us  [local(): lax.all_gather(jnp.stack([along_tiles(link_share, s) for s in range(tiles...]
    ppermute x18 -> x21, waiting for transfers between devices: 48.4 us -> 62.4 us  [along_tiles(): lax.ppermute(value, 'tile', [(i, (i + steps) % count) for i in range(coun...]
    ppermute x18 -> x21, starting transfers between devices: 21 us -> 20.3 us  [along_tiles(): lax.ppermute(value, 'tile', [(i, (i + steps) % count) for i in range(coun...]
  transfers between devices with their start and end apart: 24 -> 27, of which waited for: 9 -> 13; matrix products, arithmetic and copies ran while one was open for 2% -> 2% of each run, Pallas kernels for 30% -> 26%
where the time goes in v5:
time: 173 us; the launch traced here: 172 us
  waiting for transfers between devices  63.9 us (37%)
  Pallas kernels  56.7 us (33%)
  starting transfers between devices  24.8 us (14%)
  blocking collectives  11.5 us (7%)
  between operations  6.61 us (4%)
  local copies, waits for them, and re-layouts  6.16 us (4%)
  other arithmetic  2.6 us (2%)
    ppermute x21, waiting for transfers between devices, along_tiles(): lax.ppermute(value, 'tile', [(i, (i + steps) % count) for i in range(coun...  62.4 us
    pallas_call x2, Pallas kernels, local(): pl.pallas_call(functools.partial(contract_kernel, vecs, chunks, slots, mo...  35.4 us
    ppermute x21, starting transfers between devices, along_tiles(): lax.ppermute(value, 'tile', [(i, (i + steps) % count) for i in range(coun...  20.3 us
    all_gather x1, blocking collectives, local(): lax.all_gather(jnp.stack([along_tiles(link_share, s) for s in range(tiles...  11.5 us
    pallas_call x1, Pallas kernels, local(): call(out_shape=(*piece_shapes, jax.ShapeDtypeStruct((slots, kt, 18, LANES...  11.1 us
    pallas_call x1, Pallas kernels, local(): call(out_shape=piece_shapes, in_specs=[smem] + [vmem] * (tiles + 1), out_...  10.2 us
    ppermute x4, starting transfers between devices, over_cores(): lax.ppermute(block, 'vec', [(i, i ^ 1) for i in range(count)])  3.65 us
  transfers between devices with their start and end apart: 27, of which 13 were waited for; matrix products, arithmetic and copies ran while one was open for 2% of the time, Pallas kernels for 26%

profile of v5, /device:TPU:9, one launch (start us, length us, event | category | flops | bytes accessed | tf_op | source)
XLA Modules:
  0.0 172.3 jit_solution(16095963645425875062)
XLA Ops:
  0.0 1.1 copy.14
  1.2 1.3 collective-permute-start.6
  2.5 1.1 collective-permute-start.7
  3.6 1.4 collective-permute-start.8
  5.0 1.5 fusion.90
  6.7 1.1 collective-permute-start.4
  10.8 1.2 collective-permute-start
  12.0 11.5 %all-gather = f32[16,54,256]{2,1,0:T(8,128)S(1)} all-gather(f32[4,54,256]{2,1,0:T(8,128)S(1)} %pad_maximum_fusion.3), channel_id=2, replica_groups=mesh['groups'=2,'tile'=4,'vec'=4] {'vec'}, dimensions={0}, use_global_device_ids=true | all-gather | bytes 1105920 | tf_op jit(solution)/shard_map/all_gather | solution.py:372
  23.5 1.9 %collective-permute-done.refs_2_ = f32[48,1024]{1,0:T(8,128)S(1)} collective-permute-done((f32[48,1024]{1,0:T(8,128)S(1)}, f32[48,1024]{1,0:T(8,128)S(1)}, u32[]{:S(2)}, u32[]{:S(2)}) %collective-permute-start) | collective-permute-done | bytes 196640 | tf_op jit(solution)/shard_map/ppermute | solution.py:313
  25.4 11.1 %chebyshev.2 = (f32[8,6,8,128]{3,2,1,0:T(8,128)S(1)}, f32[8,6,8,128]{3,2,1,0:T(8,128)S(1)}, f32[8,6,8,128]{3,2,1,0:T(8,128)S(1)}, f32[8,6,8,128]{3,2,1,0:T(8,128...) custom-call(s32[4]{0:T(128)S(1)} %pad_add_fusion.2.refs_0_, ...), custom_call_target="tpu_custom_call" | custom-call | flops 14155776000 | bytes 1572864 | tf_op jit(solution)/shard_map/chebyshev/pallas_call | solution.py:397
  44.0 2.8 %collective-permute-start.3 = (f32[48,1024]{1,0:T(8,128)S(1)}, f32[48,1024]{1,0:T(8,128)S(1)}, u32[]{:S(2)}, u32[]{:S(2)}) collective-permute-start(f32[48,1024]{1,0:T(8,128)S(1)} %get-tuple-element.56), channel_id=1, source_target_pairs={{0,8},{4,12},{8,0},{12,4},{1,9},{5,13},{9,1},{13,5},{2,10},{6,14},... | collective-permute-start | bytes 589832 | tf_op jit(solution)/shard_map/ppermute | solution.py:313
  47.2 3.3 %collective-permute-done.5.refs_4_ = f32[48,1024]{1,0:T(8,128)S(1)} collective-permute-done((f32[48,1024]{1,0:T(8,128)S(1)}, f32[48,1024]{1,0:T(8,128)S(1)}, u32[]{:S(2)}, u32[]{:S(2)}) %collective-permute-start.5) | collective-permute-done | bytes 196640 | tf_op jit(solution)/shard_map/ppermute | solution.py:313
  50.5 7.4 %collective-permute-done.3.refs_3_ = f32[48,1024]{1,0:T(8,128)S(1)} collective-permute-done((f32[48,1024]{1,0:T(8,128)S(1)}, f32[48,1024]{1,0:T(8,128)S(1)}, u32[]{:S(2)}, u32[]{:S(2)}) %collective-permute-start.3) | collective-permute-done | bytes 196640 | tf_op jit(solution)/shard_map/ppermute | solution.py:313
  57.9 4.2 %collective-permute-done.1.refs_2_ = f32[48,1024]{1,0:T(8,128)S(1)} collective-permute-done((f32[48,1024]{1,0:T(8,128)S(1)}, f32[48,1024]{1,0:T(8,128)S(1)}, u32[]{:S(2)}, u32[]{:S(2)}) %collective-permute-start.1) | collective-permute-done | bytes 196640 | tf_op jit(solution)/shard_map/ppermute | solution.py:313
  62.1 3.4 %collective-permute-start.11 = (f32[8,6,8,128]{3,2,1,0:T(8,128)S(1)}, f32[8,6,8,128]{3,2,1,0:T(8,128)S(1)}, u32[]{:S(2)}, u32[]{:S(2)}) collective-permute-start(f32[8,6,8,128]{3,2,1,0:T(8,128)S(1)} %get-tuple-element.68), channel_id=1, source_target_pairs={{0,12},{4,0},{8,4},{12,8},{1,13},{5,1},{9,5},{13,9},{2,14},{6,2},{... | collective-permute-start | bytes 589832 | tf_op jit(solution)/shard_map/ppermute | solution.py:313
  65.5 10.2 %chebyshev.3 = (f32[8,6,8,128]{3,2,1,0:T(8,128)S(1)}, f32[8,6,8,128]{3,2,1,0:T(8,128)S(1)}, f32[8,6,8,128]{3,2,1,0:T(8,128)S(1)}, f32[8,6,8,128]{3,2,1,0:T(8,128)S(1)}) custom-call(s32[4]{0:T(128)S(1)} %pad_add_fusion.2.refs_0_, f32[48,1024]{1,0:T(8,128)S(1)} %get-tuple-element.69.refs_1_, f32[48,1024]{1,0:T(8,128)S(1)} %collective-permute-done.1.refs_2_, ...), custom_call_target="tpu_custom_call" | custom-call | flops 14155776000 | bytes 1572864 | tf_op jit(solution)/shard_map/chebyshev/pallas_call | solution.py:409
  75.7 6.8 %collective-permute-done.11 = f32[8,6,8,128]{3,2,1,0:T(8,128)S(1)} collective-permute-done((f32[8,6,8,128]{3,2,1,0:T(8,128)S(1)}, f32[8,6,8,128]{3,2,1,0:T(8,128)S(1)}, u32[]{:S(2)}, u32[]{:S(2)}) %collective-permute-start.11) | collective-permute-done | bytes 196640 | tf_op jit(solution)/shard_map/ppermute | solution.py:313
  83.3 1.4 collective-permute-start.14
  84.8 1.3 collective-permute-start.17
  86.1 2.8 %collective-permute-done.12 = f32[8,6,8,128]{3,2,1,0:T(8,128)S(1)} collective-permute-done((f32[8,6,8,128]{3,2,1,0:T(8,128)S(1)}, f32[8,6,8,128]{3,2,1,0:T(8,128)S(1)}, u32[]{:S(2)}, u32[]{:S(2)}) %collective-permute-start.12) | collective-permute-done | bytes 196640 | tf_op jit(solution)/shard_map/ppermute | solution.py:313
  88.9 10.8 %collective-permute-done.13 = f32[8,6,8,128]{3,2,1,0:T(8,128)S(1)} collective-permute-done((f32[8,6,8,128]{3,2,1,0:T(8,128)S(1)}, f32[8,6,8,128]{3,2,1,0:T(8,128)S(1)}, u32[]{:S(2)}, u32[]{:S(2)}) %collective-permute-start.13) | collective-permute-done | bytes 196640 | tf_op jit(solution)/shard_map/ppermute | solution.py:313
  99.7 1.0 collective-permute-done.14
  101.3 1.3 collective-permute-start.18
  104.5 17.7 %contract.2 = (f32[32,2048]{1,0:T(8,128)S(1)}, f32[32,2048]{1,0:T(8,128)S(1)}, f32[32,2048]{1,0:T(8,128)S(1)}, f32[32,2048]{1,0:T(8,128)S(1)}) custom-call(s32[4,17]{1,0:T(4,128)S(1)} %pad_add_fusion.1.scal, f32[4,8,6,8,128]{4,3,2,1,0:T(8,128)S(1)} %pad_maximum_fusion.1.refs_0_.refs_4_, f32[4,8,6,8,128]{4,3,2,1,0:T(8,128)S(1)} %collective-permute-done.16.refs_1_, ...), custom_call_target="tpu_custom_call" | custom-call | flops 19327352832 | bytes 4194304 | tf_op jit(solution)/shard_map/contract/pallas_call | solution.py:476
  122.9 1.6 collective-permute-start.20
  124.6 1.5 collective-permute-start.21
  126.0 17.7 %contract.3 = (f32[32,2048]{1,0:T(8,128)S(1)}, f32[32,2048]{1,0:T(8,128)S(1)}, f32[32,2048]{1,0:T(8,128)S(1)}, f32[32,2048]{1,0:T(8,128)S(1)}) custom-call(s32[4,17]{1,0:T(4,128)S(1)} %pad_add_fusion.1.scal, f32[4,8,6,8,128]{4,3,2,1,0:T(8,128)S(1)} %pad_maximum_fusion.refs_5_.refs_0_, f32[4,8,6,8,128]{4,3,2,1,0:T(8,128)S(1)} %collective-permute-done.15.refs_1_, ...), custom_call_target="tpu_custom_call" | custom-call | flops 19327352832 | bytes 4194304 | tf_op jit(solution)/shard_map/contract/pallas_call | solution.py:476
  143.8 2.5 %collective-permute-start.25 = (f32[32,2048]{1,0:T(8,128)S(1)}, f32[32,2048]{1,0:T(8,128)S(1)}, u32[]{:S(2)}, u32[]{:S(2)}) collective-permute-start(f32[32,2048]{1,0:T(8,128)S(1)} %get-tuple-element.103), channel_id=1, source_target_pairs={{0,8},{4,12},{8,0},{12,4},{1,9},{5,13},{9,1},{13,5},{2,10},{6,14},... | collective-permute-start | bytes 786440 | tf_op jit(solution)/shard_map/ppermute | solution.py:313
  146.3 12.7 %collective-permute-done.21 = f32[32,2048]{1,0:T(8,128)S(1)} collective-permute-done((f32[32,2048]{1,0:T(8,128)S(1)}, f32[32,2048]{1,0:T(8,128)S(1)}, u32[]{:S(2)}, u32[]{:S(2)}) %collective-permute-start.21) | collective-permute-done | bytes 262176 | tf_op jit(solution)/shard_map/ppermute | solution.py:313
  159.1 9.1 %collective-permute-done.25 = f32[32,2048]{1,0:T(8,128)S(1)} collective-permute-done((f32[32,2048]{1,0:T(8,128)S(1)}, f32[32,2048]{1,0:T(8,128)S(1)}, u32[]{:S(2)}, u32[]{:S(2)}) %collective-permute-start.25) | collective-permute-done | bytes 262176 | tf_op jit(solution)/shard_map/ppermute | solution.py:313
  168.2 2.5 %collective-permute-done.26 = f32[32,2048]{1,0:T(8,128)S(1)} collective-permute-done((f32[32,2048]{1,0:T(8,128)S(1)}, f32[32,2048]{1,0:T(8,128)S(1)}, u32[]{:S(2)}, u32[]{:S(2)}) %collective-permute-start.26) | collective-permute-done | bytes 262176 | tf_op jit(solution)/shard_map/ppermute | solution.py:313
  170.9 1.4 reshape.2013
  (75 shorter events, 9.2 us)
Async XLA Ops:
  1.2 9.6 %collective-permute-start.6 = (f32[54,256]{1,0:T(8,128)S(1)}, f32[54,256]{1,0:T(8,128)S(1)}, u32[]{:S(2)}, u32[]{:S(2)}) collective-permute-start(f32[54,256]{1,0:T(8,128)S(1)} %constant_dynamic-slice_fusion), channel_id=1, source_target_pairs={{0,4},{4,8},{8,12},{12,0},{1,5},{5,9},{9,13},{13,1},{2,6},{6,10},{... | collective-permute-start | bytes 165896 | tf_op jit(solution)/shard_map/ppermute | solution.py:313
  2.5 9.5 %collective-permute-start.7 = (f32[54,256]{1,0:T(8,128)S(1)}, f32[54,256]{1,0:T(8,128)S(1)}, u32[]{:S(2)}, u32[]{:S(2)}) collective-permute-start(f32[54,256]{1,0:T(8,128)S(1)} %constant_dynamic-slice_fusion), channel_id=1, source_target_pairs={{0,8},{4,12},{8,0},{12,4},{1,9},{5,13},{9,1},{13,5},{2,10},{6,14},... | collective-permute-start | bytes 165896 | tf_op jit(solution)/shard_map/ppermute | solution.py:313
  3.6 8.4 %collective-permute-start.8 = (f32[54,256]{1,0:T(8,128)S(1)}, f32[54,256]{1,0:T(8,128)S(1)}, u32[]{:S(2)}, u32[]{:S(2)}) collective-permute-start(f32[54,256]{1,0:T(8,128)S(1)} %constant_dynamic-slice_fusion), channel_id=1, source_target_pairs={{0,12},{4,0},{8,4},{12,8},{1,13},{5,1},{9,5},{13,9},{2,14},{6,2},{... | collective-permute-start | bytes 165896 | tf_op jit(solution)/shard_map/ppermute | solution.py:313
  6.7 16.9 %collective-permute-start.4 = (f32[48,1024]{1,0:T(8,128)S(1)}, f32[48,1024]{1,0:T(8,128)S(1)}, u32[]{:S(2)}, u32[]{:S(2)}) collective-permute-start(f32[48,1024]{1,0:T(8,128)S(1)} %get-tuple-element.127), channel_id=1, source_target_pairs={{0,12},{4,0},{8,4},{12,8},{1,13},{5,1},{9,5},{13,9},{2,14},{6,2},{... | collective-permute-start | bytes 589832 | tf_op jit(solution)/shard_map/ppermute | solution.py:313
  7.8 15.7 %collective-permute-start.2 = (f32[48,1024]{1,0:T(8,128)S(1)}, f32[48,1024]{1,0:T(8,128)S(1)}, u32[]{:S(2)}, u32[]{:S(2)}) collective-permute-start(f32[48,1024]{1,0:T(8,128)S(1)} %get-tuple-element.129), channel_id=1, source_target_pairs={{0,8},{4,12},{8,0},{12,4},{1,9},{5,13},{9,1},{13,5},{2,10},{6,14},... | collective-permute-start | bytes 589832 | tf_op jit(solution)/shard_map/ppermute | solution.py:313
  8.1 0.7 copy-start
  10.8 14.6 %collective-permute-start = (f32[48,1024]{1,0:T(8,128)S(1)}, f32[48,1024]{1,0:T(8,128)S(1)}, u32[]{:S(2)}, u32[]{:S(2)}) collective-permute-start(f32[48,1024]{1,0:T(8,128)S(1)} %get-tuple-element.130), channel_id=1, source_target_pairs={{0,4},{4,8},{8,12},{12,0},{1,5},{5,9},{9,13},{13,1},{2,6},{6,10},{... | collective-permute-start | bytes 589832 | tf_op jit(solution)/shard_map/ppermute | solution.py:313
  43.4 7.1 %collective-permute-start.5 = (f32[48,1024]{1,0:T(8,128)S(1)}, f32[48,1024]{1,0:T(8,128)S(1)}, u32[]{:S(2)}, u32[]{:S(2)}) collective-permute-start(f32[48,1024]{1,0:T(8,128)S(1)} %get-tuple-element.57), channel_id=1, source_target_pairs={{0,12},{4,0},{8,4},{12,8},{1,13},{5,1},{9,5},{13,9},{2,14},{6,2},{... | collective-permute-start | bytes 589832 | tf_op jit(solution)/shard_map/ppermute | solution.py:313
  44.0 13.9 %collective-permute-start.3 = (f32[48,1024]{1,0:T(8,128)S(1)}, f32[48,1024]{1,0:T(8,128)S(1)}, u32[]{:S(2)}, u32[]{:S(2)}) collective-permute-start(f32[48,1024]{1,0:T(8,128)S(1)} %get-tuple-element.56), channel_id=1, source_target_pairs={{0,8},{4,12},{8,0},{12,4},{1,9},{5,13},{9,1},{13,5},{2,10},{6,14},... | collective-permute-start | bytes 589832 | tf_op jit(solution)/shard_map/ppermute | solution.py:313
  46.9 15.3 %collective-permute-start.1 = (f32[48,1024]{1,0:T(8,128)S(1)}, f32[48,1024]{1,0:T(8,128)S(1)}, u32[]{:S(2)}, u32[]{:S(2)}) collective-permute-start(f32[48,1024]{1,0:T(8,128)S(1)} %get-tuple-element.55), channel_id=1, source_target_pairs={{0,4},{4,8},{8,12},{12,0},{1,5},{5,9},{9,13},{13,1},{2,6},{6,10},{... | collective-permute-start | bytes 589832 | tf_op jit(solution)/shard_map/ppermute | solution.py:313
  62.1 13.6 %collective-permute-start.10 = (f32[8,6,8,128]{3,2,1,0:T(8,128)S(1)}, f32[8,6,8,128]{3,2,1,0:T(8,128)S(1)}, u32[]{:S(2)}, u32[]{:S(2)}) collective-permute-start(f32[8,6,8,128]{3,2,1,0:T(8,128)S(1)} %get-tuple-element.67), channel_id=1, source_target_pairs={{0,8},{4,12},{8,0},{12,4},{1,9},{5,13},{9,1},{13,5},{2,10},{6,14},... | collective-permute-start | bytes 589832 | tf_op jit(solution)/shard_map/ppermute | solution.py:313
  62.1 20.4 %collective-permute-start.11 = (f32[8,6,8,128]{3,2,1,0:T(8,128)S(1)}, f32[8,6,8,128]{3,2,1,0:T(8,128)S(1)}, u32[]{:S(2)}, u32[]{:S(2)}) collective-permute-start(f32[8,6,8,128]{3,2,1,0:T(8,128)S(1)} %get-tuple-element.68), channel_id=1, source_target_pairs={{0,12},{4,0},{8,4},{12,8},{1,13},{5,1},{9,5},{13,9},{2,14},{6,2},{... | collective-permute-start | bytes 589832 | tf_op jit(solution)/shard_map/ppermute | solution.py:313
  65.5 17.0 %collective-permute-start.9 = (f32[8,6,8,128]{3,2,1,0:T(8,128)S(1)}, f32[8,6,8,128]{3,2,1,0:T(8,128)S(1)}, u32[]{:S(2)}, u32[]{:S(2)}) collective-permute-start(f32[8,6,8,128]{3,2,1,0:T(8,128)S(1)} %get-tuple-element.66), channel_id=1, source_target_pairs={{0,4},{4,8},{8,12},{12,0},{1,5},{5,9},{9,13},{13,1},{2,6},{6,10},{... | collective-permute-start | bytes 589832 | tf_op jit(solution)/shard_map/ppermute | solution.py:313
  82.5 20.1 %copy-start.1 = (s32[8,3]{0,1:T(4,128)S(1)}, s32[8,3]{0,1:T(4,128)}, u32[]{:S(2)}) copy-start(s32[8,3]{0,1:T(4,128)} %param.6) | copy-start | bytes 292
  82.6 18.7 %collective-permute-start.16 = (f32[4,8,6,8,128]{4,3,2,1,0:T(8,128)S(1)}, f32[4,8,6,8,128]{4,3,2,1,0:T(8,128)S(1)}, u32[]{:S(2)}, u32[]{:S(2)}) collective-permute-start(f32[4,8,6,8,128]{4,3,2,1,0:T(8,128)S(1)} %pad_maximum_fusion.1.refs_0_.refs_4_), channel_id=1, source_target_pairs={{0,2},{1,3},{2,0},{3,1},{4,6},{5,7},{6,4},{7,5},{8,10},{9,11},{10,... | collective-permute-start | bytes 2359304 | tf_op jit(solution)/shard_map/ppermute | solution.py:324
  83.2 5.7 %collective-permute-start.12 = (f32[8,6,8,128]{3,2,1,0:T(8,128)S(1)}, f32[8,6,8,128]{3,2,1,0:T(8,128)S(1)}, u32[]{:S(2)}, u32[]{:S(2)}) collective-permute-start(f32[8,6,8,128]{3,2,1,0:T(8,128)S(1)} %get-tuple-element.79), channel_id=1, source_target_pairs={{0,4},{4,8},{8,12},{12,0},{1,5},{5,9},{9,13},{13,1},{2,6},{6,10},{... | collective-permute-start | bytes 589832 | tf_op jit(solution)/shard_map/ppermute | solution.py:313
  83.2 16.4 %collective-permute-start.13 = (f32[8,6,8,128]{3,2,1,0:T(8,128)S(1)}, f32[8,6,8,128]{3,2,1,0:T(8,128)S(1)}, u32[]{:S(2)}, u32[]{:S(2)}) collective-permute-start(f32[8,6,8,128]{3,2,1,0:T(8,128)S(1)} %get-tuple-element.80), channel_id=1, source_target_pairs={{0,8},{4,12},{8,0},{12,4},{1,9},{5,13},{9,1},{13,5},{2,10},{6,14},... | collective-permute-start | bytes 589832 | tf_op jit(solution)/shard_map/ppermute | solution.py:313
  83.3 17.3 %collective-permute-start.14 = (f32[8,6,8,128]{3,2,1,0:T(8,128)S(1)}, f32[8,6,8,128]{3,2,1,0:T(8,128)S(1)}, u32[]{:S(2)}, u32[]{:S(2)}) collective-permute-start(f32[8,6,8,128]{3,2,1,0:T(8,128)S(1)} %get-tuple-element.81), channel_id=1, source_target_pairs={{0,12},{4,0},{8,4},{12,8},{1,13},{5,1},{9,5},{13,9},{2,14},{6,2},{... | collective-permute-start | bytes 589832 | tf_op jit(solution)/shard_map/ppermute | solution.py:313
  84.8 18.8 %collective-permute-start.17 = (f32[4,8,6,8,128]{4,3,2,1,0:T(8,128)S(1)}, f32[4,8,6,8,128]{4,3,2,1,0:T(8,128)S(1)}, u32[]{:S(2)}, u32[]{:S(2)}) collective-permute-start(f32[4,8,6,8,128]{4,3,2,1,0:T(8,128)S(1)} %pad_maximum_fusion.1.refs_0_.refs_4_), channel_id=1, source_target_pairs={{0,1},{1,0},{2,3},{3,2},{4,5},{5,4},{6,7},{7,6},{8,9},{9,8},{10,11... | collective-permute-start | bytes 2359304 | tf_op jit(solution)/shard_map/ppermute | solution.py:332
  101.3 3.3 %collective-permute-start.18 = (f32[4,8,6,8,128]{4,3,2,1,0:T(8,128)S(1)}, f32[4,8,6,8,128]{4,3,2,1,0:T(8,128)S(1)}, u32[]{:S(2)}, u32[]{:S(2)}) collective-permute-start(f32[4,8,6,8,128]{4,3,2,1,0:T(8,128)S(1)} %collective-permute-done.16.refs_1_), channel_id=1, source_target_pairs={{0,1},{1,0},{2,3},{3,2},{4,5},{5,4},{6,7},{7,6},{8,9},{9,8},{10,11... | collective-permute-start | bytes 2359304 | tf_op jit(solution)/shard_map/ppermute | solution.py:332
  103.0 19.3 %collective-permute-start.15 = (f32[4,8,6,8,128]{4,3,2,1,0:T(8,128)S(1)}, f32[4,8,6,8,128]{4,3,2,1,0:T(8,128)S(1)}, u32[]{:S(2)}, u32[]{:S(2)}) collective-permute-start(f32[4,8,6,8,128]{4,3,2,1,0:T(8,128)S(1)} %pad_maximum_fusion.refs_5_.refs_0_), channel_id=1, source_target_pairs={{0,2},{1,3},{2,0},{3,1},{4,6},{5,7},{6,4},{7,5},{8,10},{9,11},{10,... | collective-permute-start | bytes 2359304 | tf_op jit(solution)/shard_map/ppermute | solution.py:324
  103.3 22.7 %collective-permute-start.22 = (f32[4,8,6,8,128]{4,3,2,1,0:T(8,128)S(1)}, f32[4,8,6,8,128]{4,3,2,1,0:T(8,128)S(1)}, u32[]{:S(2)}, u32[]{:S(2)}) collective-permute-start(f32[4,8,6,8,128]{4,3,2,1,0:T(8,128)S(1)} %pad_maximum_fusion.refs_5_.refs_0_), channel_id=1, source_target_pairs={{0,1},{1,0},{2,3},{3,2},{4,5},{5,4},{6,7},{7,6},{8,9},{9,8},{10,11... | collective-permute-start | bytes 2359304 | tf_op jit(solution)/shard_map/ppermute | solution.py:332
  122.2 3.8 %collective-permute-start.23 = (f32[4,8,6,8,128]{4,3,2,1,0:T(8,128)S(1)}, f32[4,8,6,8,128]{4,3,2,1,0:T(8,128)S(1)}, u32[]{:S(2)}, u32[]{:S(2)}) collective-permute-start(f32[4,8,6,8,128]{4,3,2,1,0:T(8,128)S(1)} %collective-permute-done.15.refs_1_), channel_id=1, source_target_pairs={{0,1},{1,0},{2,3},{3,2},{4,5},{5,4},{6,7},{7,6},{8,9},{9,8},{10,11... | collective-permute-start | bytes 2359304 | tf_op jit(solution)/shard_map/ppermute | solution.py:332
  122.9 23.4 %collective-permute-start.19 = (f32[32,2048]{1,0:T(8,128)S(1)}, f32[32,2048]{1,0:T(8,128)S(1)}, u32[]{:S(2)}, u32[]{:S(2)}) collective-permute-start(f32[32,2048]{1,0:T(8,128)S(1)} %get-tuple-element.97), channel_id=1, source_target_pairs={{0,4},{4,8},{8,12},{12,0},{1,5},{5,9},{9,13},{13,1},{2,6},{6,10},{... | collective-permute-start | bytes 786440 | tf_op jit(solution)/shard_map/ppermute | solution.py:313
  122.9 23.4 %collective-permute-start.20 = (f32[32,2048]{1,0:T(8,128)S(1)}, f32[32,2048]{1,0:T(8,128)S(1)}, u32[]{:S(2)}, u32[]{:S(2)}) collective-permute-start(f32[32,2048]{1,0:T(8,128)S(1)} %get-tuple-element.98), channel_id=1, source_target_pairs={{0,8},{4,12},{8,0},{12,4},{1,9},{5,13},{9,1},{13,5},{2,10},{6,14},... | collective-permute-start | bytes 786440 | tf_op jit(solution)/shard_map/ppermute | solution.py:313
  124.6 34.5 %collective-permute-start.21 = (f32[32,2048]{1,0:T(8,128)S(1)}, f32[32,2048]{1,0:T(8,128)S(1)}, u32[]{:S(2)}, u32[]{:S(2)}) collective-permute-start(f32[32,2048]{1,0:T(8,128)S(1)} %get-tuple-element.99), channel_id=1, source_target_pairs={{0,12},{4,0},{8,4},{12,8},{1,13},{5,1},{9,5},{13,9},{2,14},{6,2},{... | collective-permute-start | bytes 786440 | tf_op jit(solution)/shard_map/ppermute | solution.py:313
  143.7 15.4 %collective-permute-start.24 = (f32[32,2048]{1,0:T(8,128)S(1)}, f32[32,2048]{1,0:T(8,128)S(1)}, u32[]{:S(2)}, u32[]{:S(2)}) collective-permute-start(f32[32,2048]{1,0:T(8,128)S(1)} %get-tuple-element.102), channel_id=1, source_target_pairs={{0,4},{4,8},{8,12},{12,0},{1,5},{5,9},{9,13},{13,1},{2,6},{6,10},{... | collective-permute-start | bytes 786440 | tf_op jit(solution)/shard_map/ppermute | solution.py:313
  143.8 24.4 %collective-permute-start.25 = (f32[32,2048]{1,0:T(8,128)S(1)}, f32[32,2048]{1,0:T(8,128)S(1)}, u32[]{:S(2)}, u32[]{:S(2)}) collective-permute-start(f32[32,2048]{1,0:T(8,128)S(1)} %get-tuple-element.103), channel_id=1, source_target_pairs={{0,8},{4,12},{8,0},{12,4},{1,9},{5,13},{9,1},{13,5},{2,10},{6,14},... | collective-permute-start | bytes 786440 | tf_op jit(solution)/shard_map/ppermute | solution.py:313
  146.3 24.4 %collective-permute-start.26 = (f32[32,2048]{1,0:T(8,128)S(1)}, f32[32,2048]{1,0:T(8,128)S(1)}, u32[]{:S(2)}, u32[]{:S(2)}) collective-permute-start(f32[32,2048]{1,0:T(8,128)S(1)} %get-tuple-element.104), channel_id=1, source_target_pairs={{0,12},{4,0},{8,4},{12,8},{1,13},{5,1},{9,5},{13,9},{2,14},{6,2},{... | collective-permute-start | bytes 786440 | tf_op jit(solution)/shard_map/ppermute | solution.py:313

commit v6 on v4

--- a/solution.py
+++ b/solution.py
@@ -120,7 +120,7 @@
                 share = link_ref.shape[3] // LANES
                 lanes = slice(k % share * LANES, (k % share + 1) * LANES)
                 for m in range(3):
-                    l_ref[m, s * kt + k] = link_ref[k // share, s, 18 * m : 18 * m + 18, lanes]
+                    l_ref[m, t * kt + k] = link_ref[k // share, s, 18 * m : 18 * m + 18, lanes]
 
     if with_links:
 
@@ -202,8 +202,6 @@
     comps = 6
     kt = pl.num_programs(0)
     depth = comps * LANES
-    group = dhi.shape[1]
-    per = group // cols
     half = 3 * LANES
 
     mine = scal[slots, 0]
@@ -227,14 +225,14 @@
             for c in range(comps):
                 side[at, c * LANES : (c + 1) * LANES] = left_refs[v][t, 0, c]
     for c in range(3):
-        rh, rl = split(side[:, c * LANES : (c + 1) * LANES])
-        ih, il = split(side[:, half + c * LANES : half + (c + 1) * LANES])
+        rh, rl = split(side[:, c * LANES : (c + 1) * LANES].T)
+        ih, il = split(side[:, half + c * LANES : half + (c + 1) * LANES].T)
         for third, re, im in ((0, rh, ih), (1, rl, il), (2, rh, ih)):
             first = third * depth + c * LANES
-            whole[0:rows, first : first + LANES] = re
-            whole[0:rows, first + half : first + half + LANES] = im
-            whole[rows : 2 * rows, first : first + LANES] = -im
-            whole[rows : 2 * rows, first + half : first + half + LANES] = re
+            whole[first : first + LANES, 0:rows] = re
+            whole[first + half : first + half + LANES, 0:rows] = im
+            whole[first : first + LANES, rows : 2 * rows] = -im
+            whole[first + half : first + half + LANES, rows : 2 * rows] = re
 
     for slot in range(slots):
         ka, kb = scal[slot, k], scal[slot, kt + k]
@@ -264,25 +262,20 @@
                     disp[slot, i, at, :] = dr
                     disp[slot, 3 + i, at, :] = di
 
-    for g in range(slots * moms // per):
-        for r in range(per):
-            slot, p = divmod(g * per + r, moms)
-            co = trig_ref[k, p : p + 1, :]
-            si = trig_ref[k, moms + p : moms + p + 1, :]
-            for i in range(3):
-                dr, di = disp[slot, i], disp[slot, 3 + i]
-                for part, value in ((0, co * dr + si * di), (1, co * di - si * dr)):
-                    high, low = split(value)
-                    first = part * half + i * LANES
-                    dhi[g, r * cols : (r + 1) * cols, first : first + LANES] = high
-                    dlo[g, r * cols : (r + 1) * cols, first : first + LANES] = low
-        high, low = dhi[g], dlo[g]
-        acc_ref[g * group : (g + 1) * group, :] += lax.dot_general(
-            jnp.concatenate([high, high, low], axis=1),
-            whole[...],
-            (((1,), (1,)), ((), ())),
-            preferred_element_type=jnp.float32,
-        )
+    for r in range(slots * moms):
+        slot, p = divmod(r, moms)
+        co = trig_ref[k, p : p + 1, :]
+        si = trig_ref[k, moms + p : moms + p + 1, :]
+        for i in range(3):
+            dr, di = disp[slot, i], disp[slot, 3 + i]
+            for part, value in ((0, co * dr + si * di), (1, co * di - si * dr)):
+                high, low = split(value)
+                first = part * half + i * LANES
+                dhi[r * cols : (r + 1) * cols, first : first + LANES] = high
+                dlo[r * cols : (r + 1) * cols, first : first + LANES] = low
+    acc_ref[...] += jnp.dot(
+        jnp.concatenate([dhi[...], dhi[...], dlo[...]], axis=1), whole[...], preferred_element_type=jnp.float32
+    )
 
     @pl.when(k == kt - 1)
     def _():
@@ -360,14 +353,51 @@
     parts = jnp.transpose(parts, (2, 1, 0, 3, 4)).reshape(chunks, tiles, 6 * nvc, sites)
     share = sites // vecs
     link_share = lax.dynamic_slice_in_dim(links.reshape(54, sites), lax.axis_index("vec") * share, share, 1)
-    gauge = lax.all_gather(link_share, ("vec", "tile"), axis=0).reshape(vecs, tiles, 54, share)
+    shares = [along_tiles(link_share, s) for s in range(tiles)]
+    shares, momenta, directions = lax.optimization_barrier((shares, momenta, directions))
+    heading = directions % 3
+    gauge = lax.all_gather(jnp.stack(shares), "vec", axis=0)
     fields = []
     for c in range(chunks):
         sent = [lax.dynamic_index_in_dim(parts[c], lax.rem(tile + s, tiles), 0, keepdims=False) for s in range(tiles)]
         if c > 0:
-            for s in range(1, tiles):
-                fields[c - 1][s], sent[s] = lax.optimization_barrier((fields[c - 1][s], sent[s]))
+            fields[c - 1], sent = lax.optimization_barrier((fields[c - 1], sent))
         fields.append([along_tiles(block, s) for s, block in enumerate(sent)])
+
+    k = jnp.arange(kt, dtype=jnp.int32)[:, None]
+    lane = jnp.arange(LANES, dtype=jnp.int32)[None]
+
+    def pick(options):
+        return jnp.where(mode == 0, options[0], jnp.where(mode == 1, options[1], options[2]))
+
+    coords = [piece_coords(m, tile, tiles, k, lane) for m in range(3)]
+    x, y, z = (pick([jnp.broadcast_to(c[axis], (kt, LANES)) for c in coords]) for axis in range(3))
+    start_x = jnp.where(mode == 0, tile * (sites // PLANE), 0)
+
+    def part(axis, coord, extent):
+        return jnp.mod(momenta[:, axis, None, None] * coord[None], extent).astype(f32) / extent
+
+    angle = 2.0 * math.pi * (part(0, x + start_x, extent_x) + part(1, y, LY) + part(2, z, LZ))
+    trig = jnp.transpose(jnp.concatenate([jnp.cos(angle), jnp.sin(angle)]), (1, 0, 2))
+
+    index, spots = [], []
+    for slot in range(slots):
+        d = directions[slot]
+        step = jnp.where(d < 3, 1, -1)
+        xs = jnp.mod(x + jnp.where(heading[slot] == 0, step, 0), extent_x)
+        ys = jnp.mod(y + jnp.where(heading[slot] == 1, step, 0), LY)
+        zs = jnp.mod(z + jnp.where(heading[slot] == 2, step, 0), LZ)
+        found = [piece_index(m, tile, tiles, xs, ys, zs) for m in range(3)]
+        ks, ls = (pick([f[i] for f in found]) for i in range(2))
+        ka, kb = jnp.min(ks, axis=1), jnp.max(ks, axis=1)
+        index.append(jnp.stack([ls, (ks == kb[:, None]).astype(jnp.int32)], axis=1))
+        spots.append(jnp.concatenate([ka, kb, (d < 3).astype(jnp.int32)[None]]))
+    owner = block_owners()
+    spots.append(jnp.broadcast_to(tile.astype(jnp.int32), spots[0].shape))
+    spots.append(jnp.pad(owner, (0, 2 * kt + 1 - vecs)))
+    index, spots = jnp.stack(index), jnp.stack(spots).astype(jnp.int32)
+
+    fields[0][0], trig, index, spots = lax.optimization_barrier((fields[0][0], trig, index, spots))
 
     piece_shapes = (jax.ShapeDtypeStruct((kt, 6, nvc, LANES), f32),) * tiles
     link_shape = (6, nt, 18, LANES)
@@ -412,44 +442,9 @@
         if c == 1:
             lefts[0][1:], owns[1] = lax.optimization_barrier((lefts[0][1:], owns[1]))
             lefts[1][0] = owns[1]
-    owner = block_owners()
-
-    k = jnp.arange(kt, dtype=jnp.int32)[:, None]
-    lane = jnp.arange(LANES, dtype=jnp.int32)[None]
-
-    def pick(options):
-        return jnp.where(mode == 0, options[0], jnp.where(mode == 1, options[1], options[2]))
-
-    coords = [piece_coords(m, tile, tiles, k, lane) for m in range(3)]
-    x, y, z = (pick([jnp.broadcast_to(c[axis], (kt, LANES)) for c in coords]) for axis in range(3))
-    start_x = jnp.where(mode == 0, tile * (sites // PLANE), 0)
-
-    def part(axis, coord, extent):
-        return jnp.mod(momenta[:, axis, None, None] * coord[None], extent).astype(f32) / extent
-
-    angle = 2.0 * math.pi * (part(0, x + start_x, extent_x) + part(1, y, LY) + part(2, z, LZ))
-    trig = jnp.transpose(jnp.concatenate([jnp.cos(angle), jnp.sin(angle)]), (1, 0, 2))
-
-    index, spots = [], []
-    for slot in range(slots):
-        d = directions[slot]
-        step = jnp.where(d < 3, 1, -1)
-        xs = jnp.mod(x + jnp.where(heading[slot] == 0, step, 0), extent_x)
-        ys = jnp.mod(y + jnp.where(heading[slot] == 1, step, 0), LY)
-        zs = jnp.mod(z + jnp.where(heading[slot] == 2, step, 0), LZ)
-        found = [piece_index(m, tile, tiles, xs, ys, zs) for m in range(3)]
-        ks, ls = (pick([f[i] for f in found]) for i in range(2))
-        ka, kb = jnp.min(ks, axis=1), jnp.max(ks, axis=1)
-        index.append(jnp.stack([ls, (ks == kb[:, None]).astype(jnp.int32)], axis=1))
-        spots.append(jnp.concatenate([ka, kb, (d < 3).astype(jnp.int32)[None]]))
-    spots.append(jnp.broadcast_to(tile.astype(jnp.int32), spots[0].shape))
-    spots.append(jnp.pad(owner, (0, 2 * kt + 1 - vecs)))
-    index, spots = jnp.stack(index), jnp.stack(spots).astype(jnp.int32)
 
     rows, cols = vecs * tiles * nvc, nv
     depth = 6 * LANES
-    group = cols * max(1, min(moms, 256 // cols))
-    groups = slots * moms * cols // group
     bf16 = jnp.bfloat16
     mine = []
     for c in range(chunks):
@@ -473,9 +468,9 @@
             scratch_shapes=[
                 pltpu.VMEM((rows, depth), f32),
                 pltpu.VMEM((slots, 6, cols, LANES), f32),
-                pltpu.VMEM((2 * rows, 3 * depth), bf16),
-                pltpu.VMEM((groups, group, depth), bf16),
-                pltpu.VMEM((groups, group, depth), bf16),
+                pltpu.VMEM((3 * depth, 2 * rows), bf16),
+                pltpu.VMEM((slots * moms * cols, depth), bf16),
+                pltpu.VMEM((slots * moms * cols, depth), bf16),
                 pltpu.VMEM((slots * moms * cols, 2 * rows), f32),
                 pltpu.VMEM((rows, slots * 2 * moms * cols), f32),
             ],

time: 187 us -> 161 us (0.86)
  blocking collectives: 41 us -> 11.2 us
  Pallas kernels: 55.7 us -> 59 us
    all_gather x1, blocking collectives: 41 us -> 11.2 us  [local(): gauge = lax.all_gather(jnp.stack(shares), 'vec', axis=0)]
    ppermute x18 -> x21, starting transfers between devices: 21 us -> 21.7 us  [along_tiles(): lax.ppermute(value, 'tile', [(i, (i + steps) % count) for i in range(coun...]
    ppermute x18 -> x21, waiting for transfers between devices: 48.4 us -> 47.8 us  [along_tiles(): lax.ppermute(value, 'tile', [(i, (i + steps) % count) for i in range(coun...]
  transfers between devices with their start and end apart: 24 -> 27, of which waited for: 9 -> 12; matrix products, arithmetic and copies ran while one was open for 2% -> 4% of each run, Pallas kernels for 30% -> 37%
where the time goes in v6:
time: 161 us
  Pallas kernels  59 us (37%)
  waiting for transfers between devices  48.2 us (30%)
  starting transfers between devices  26.8 us (17%)
  blocking collectives  11.2 us (7%)
  between operations  6.98 us (4%)
  local copies, waits for them, and re-layouts  5.83 us (4%)
  other arithmetic  2.61 us (2%)
    ppermute x21, waiting for transfers between devices, along_tiles(): lax.ppermute(value, 'tile', [(i, (i + steps) % count) for i in range(coun...  47.8 us
    pallas_call x2, Pallas kernels, local(): pl.pallas_call(functools.partial(contract_kernel, vecs, chunks, slots, mo...  35.9 us
    ppermute x21, starting transfers between devices, along_tiles(): lax.ppermute(value, 'tile', [(i, (i + steps) % count) for i in range(coun...  21.7 us
    pallas_call x1, Pallas kernels, local(): call(out_shape=(*piece_shapes, jax.ShapeDtypeStruct((slots, kt, 18, LANES...  12.1 us
    all_gather x1, blocking collectives, local(): gauge = lax.all_gather(jnp.stack(shares), 'vec', axis=0)  11.2 us
    pallas_call x1, Pallas kernels, local(): call(out_shape=piece_shapes, in_specs=[smem] + [vmem] * (tiles + 1), out_...  11 us
    ppermute x4, starting transfers between devices, over_cores(): lax.ppermute(block, 'vec', [(i, i ^ 1) for i in range(count)])  3.47 us
  transfers between devices with their start and end apart: 27, of which 12 were waited for; matrix products, arithmetic and copies ran while one was open for 4% of the time, Pallas kernels for 37%

profile of v6, /device:TPU:9, one launch (start us, length us, event | category | flops | bytes accessed | tf_op | source)
XLA Modules:
  0.0 160.6 jit_solution(13588977466579061205)
XLA Ops:
  0.0 1.1 copy.14
  1.3 2.5 %collective-permute-start.7 = (f32[54,256]{1,0:T(8,128)S(1)}, f32[54,256]{1,0:T(8,128)S(1)}, u32[]{:S(2)}, u32[]{:S(2)}) collective-permute-start(f32[54,256]{1,0:T(8,128)S(1)} %constant_dynamic-slice_fusion), channel_id=1, source_target_pairs={{0,8},{4,12},{8,0},{12,4},{1,9},{5,13},{9,1},{13,5},{2,10},{6,14},... | collective-permute-start | bytes 165896 | tf_op jit(solution)/shard_map/ppermute | solution.py:297
  3.7 2.2 %collective-permute-start.6 = (f32[54,256]{1,0:T(8,128)S(1)}, f32[54,256]{1,0:T(8,128)S(1)}, u32[]{:S(2)}, u32[]{:S(2)}) collective-permute-start(f32[54,256]{1,0:T(8,128)S(1)} %constant_dynamic-slice_fusion), channel_id=1, source_target_pairs={{0,4},{4,8},{8,12},{12,0},{1,5},{5,9},{9,13},{13,1},{2,6},{6,10},{... | collective-permute-start | bytes 165896 | tf_op jit(solution)/shard_map/ppermute | solution.py:297
  5.9 1.5 fusion.90
  7.8 1.2 collective-permute-start.1
  11.2 2.1 %collective-permute-start = (f32[48,1024]{1,0:T(8,128)S(1)}, f32[48,1024]{1,0:T(8,128)S(1)}, u32[]{:S(2)}, u32[]{:S(2)}) collective-permute-start(f32[48,1024]{1,0:T(8,128)S(1)} %get-tuple-element.147), channel_id=1, source_target_pairs={{0,4},{4,8},{8,12},{12,0},{1,5},{5,9},{9,13},{13,1},{2,6},{6,10},{... | collective-permute-start | bytes 589832 | tf_op jit(solution)/shard_map/ppermute | solution.py:297
  20.7 11.2 %all-gather = f32[16,54,256]{2,1,0:T(8,128)S(1)} all-gather(f32[4,54,256]{2,1,0:T(8,128)S(1)} %pad_maximum_fusion.3), channel_id=2, replica_groups=mesh['groups'=2,'tile'=4,'vec'=4] {'vec'}, dimensions={0}, use_global_device_ids=true | all-gather | bytes 1105920 | tf_op jit(solution)/shard_map/all_gather | solution.py:359
  32.9 1.8 %collective-permute-start.4 = (f32[48,1024]{1,0:T(8,128)S(1)}, f32[48,1024]{1,0:T(8,128)S(1)}, u32[]{:S(2)}, u32[]{:S(2)}) collective-permute-start(f32[48,1024]{1,0:T(8,128)S(1)} %get-tuple-element.66), channel_id=1, source_target_pairs={{0,8},{4,12},{8,0},{12,4},{1,9},{5,13},{9,1},{13,5},{2,10},{6,14},... | collective-permute-start | bytes 589832 | tf_op jit(solution)/shard_map/ppermute | solution.py:297
  34.8 1.4 collective-permute-start.5
  36.1 12.1 %chebyshev.2 = (f32[8,6,8,128]{3,2,1,0:T(8,128)S(1)}, f32[8,6,8,128]{3,2,1,0:T(8,128)S(1)}, f32[8,6,8,128]{3,2,1,0:T(8,128)S(1)}, f32[8,6,8,128]{3,2,1,0:T(8,128...) custom-call(s32[4]{0:T(128)S(1)} %pad_add_fusion.2.refs_0_, ...), custom_call_target="tpu_custom_call" | custom-call | flops 14155776000 | bytes 1572864 | tf_op jit(solution)/shard_map/chebyshev/pallas_call | solution.py:418
  48.3 1.8 %collective-permute-done.4.refs_3_ = f32[48,1024]{1,0:T(8,128)S(1)} collective-permute-done((f32[48,1024]{1,0:T(8,128)S(1)}, f32[48,1024]{1,0:T(8,128)S(1)}, u32[]{:S(2)}, u32[]{:S(2)}) %collective-permute-start.4) | collective-permute-done | bytes 196640 | tf_op jit(solution)/shard_map/ppermute | solution.py:297
  50.0 2.7 %collective-permute-done.5.refs_4_ = f32[48,1024]{1,0:T(8,128)S(1)} collective-permute-done((f32[48,1024]{1,0:T(8,128)S(1)}, f32[48,1024]{1,0:T(8,128)S(1)}, u32[]{:S(2)}, u32[]{:S(2)}) %collective-permute-start.5) | collective-permute-done | bytes 196640 | tf_op jit(solution)/shard_map/ppermute | solution.py:297
  53.1 1.5 collective-permute-start.11
  54.6 11.0 %chebyshev.3 = (f32[8,6,8,128]{3,2,1,0:T(8,128)S(1)}, f32[8,6,8,128]{3,2,1,0:T(8,128)S(1)}, f32[8,6,8,128]{3,2,1,0:T(8,128)S(1)}, f32[8,6,8,128]{3,2,1,0:T(8,128)S(1)}) custom-call(s32[4]{0:T(128)S(1)} %pad_add_fusion.2.refs_0_, f32[48,1024]{1,0:T(8,128)S(1)} %get-tuple-element.87.refs_1_, f32[48,1024]{1,0:T(8,128)S(1)} %collective-permute-done.3.refs_2_, ...), custom_call_target="tpu_custom_call" | custom-call | flops 14155776000 | bytes 1572864 | tf_op jit(solution)/shard_map/chebyshev/pallas_call | solution.py:428
  65.6 3.9 %collective-permute-done.10 = f32[8,6,8,128]{3,2,1,0:T(8,128)S(1)} collective-permute-done((f32[8,6,8,128]{3,2,1,0:T(8,128)S(1)}, f32[8,6,8,128]{3,2,1,0:T(8,128)S(1)}, u32[]{:S(2)}, u32[]{:S(2)}) %collective-permute-start.10) | collective-permute-done | bytes 196640 | tf_op jit(solution)/shard_map/ppermute | solution.py:297
  69.5 1.7 %collective-permute-done.11 = f32[8,6,8,128]{3,2,1,0:T(8,128)S(1)} collective-permute-done((f32[8,6,8,128]{3,2,1,0:T(8,128)S(1)}, f32[8,6,8,128]{3,2,1,0:T(8,128)S(1)}, u32[]{:S(2)}, u32[]{:S(2)}) %collective-permute-start.11) | collective-permute-done | bytes 196640 | tf_op jit(solution)/shard_map/ppermute | solution.py:297
  71.6 1.4 collective-permute-start.13
  73.0 1.5 collective-permute-start.14
  74.4 2.1 %collective-permute-start.17 = (f32[4,8,6,8,128]{4,3,2,1,0:T(8,128)S(1)}, f32[4,8,6,8,128]{4,3,2,1,0:T(8,128)S(1)}, u32[]{:S(2)}, u32[]{:S(2)}) collective-permute-start(f32[4,8,6,8,128]{4,3,2,1,0:T(8,128)S(1)} %pad_maximum_fusion.1.refs_0_.refs_4_), channel_id=1, source_target_pairs={{0,1},{1,0},{2,3},{3,2},{4,5},{5,4},{6,7},{7,6},{8,9},{9,8},{10,11... | collective-permute-start | bytes 2359304 | tf_op jit(solution)/shard_map/ppermute | solution.py:316
  77.2 10.8 %collective-permute-done.13 = f32[8,6,8,128]{3,2,1,0:T(8,128)S(1)} collective-permute-done((f32[8,6,8,128]{3,2,1,0:T(8,128)S(1)}, f32[8,6,8,128]{3,2,1,0:T(8,128)S(1)}, u32[]{:S(2)}, u32[]{:S(2)}) %collective-permute-start.13) | collective-permute-done | bytes 196640 | tf_op jit(solution)/shard_map/ppermute | solution.py:297
  88.0 3.0 %collective-permute-done.14 = f32[8,6,8,128]{3,2,1,0:T(8,128)S(1)} collective-permute-done((f32[8,6,8,128]{3,2,1,0:T(8,128)S(1)}, f32[8,6,8,128]{3,2,1,0:T(8,128)S(1)}, u32[]{:S(2)}, u32[]{:S(2)}) %collective-permute-start.14) | collective-permute-done | bytes 196640 | tf_op jit(solution)/shard_map/ppermute | solution.py:297
  91.6 1.2 collective-permute-start.15
  93.5 18.0 %contract.2 = (f32[32,2048]{1,0:T(8,128)S(1)}, f32[32,2048]{1,0:T(8,128)S(1)}, f32[32,2048]{1,0:T(8,128)S(1)}, f32[32,2048]{1,0:T(8,128)S(1)}) custom-call(s32[4,17]{1,0:T(4,128)S(1)} %pad_add_fusion.1.scal, f32[4,8,6,8,128]{4,3,2,1,0:T(8,128)S(1)} %pad_maximum_fusion.1.refs_0_.refs_4_, f32[4,8,6,8,128]{4,3,2,1,0:T(8,128)S(1)} %collective-permute-done.16.refs_1_, ...), custom_call_target="tpu_custom_call" | custom-call | flops 19327352832 | bytes 4194304 | tf_op jit(solution)/shard_map/contract/pallas_call | solution.py:460
  111.9 1.1 collective-permute-start.20
  113.0 1.5 collective-permute-start.21
  114.5 18.0 %contract.3 = (f32[32,2048]{1,0:T(8,128)S(1)}, f32[32,2048]{1,0:T(8,128)S(1)}, f32[32,2048]{1,0:T(8,128)S(1)}, f32[32,2048]{1,0:T(8,128)S(1)}) custom-call(s32[4,17]{1,0:T(4,128)S(1)} %pad_add_fusion.1.scal, f32[4,8,6,8,128]{4,3,2,1,0:T(8,128)S(1)} %pad_maximum_fusion.refs_5_.refs_0_, f32[4,8,6,8,128]{4,3,2,1,0:T(8,128)S(1)} %collective-permute-done.15.refs_1_, ...), custom_call_target="tpu_custom_call" | custom-call | flops 19327352832 | bytes 4194304 | tf_op jit(solution)/shard_map/contract/pallas_call | solution.py:460
  132.7 2.9 %collective-permute-start.25 = (f32[32,2048]{1,0:T(8,128)S(1)}, f32[32,2048]{1,0:T(8,128)S(1)}, u32[]{:S(2)}, u32[]{:S(2)}) collective-permute-start(f32[32,2048]{1,0:T(8,128)S(1)} %get-tuple-element.121), channel_id=1, source_target_pairs={{0,8},{4,12},{8,0},{12,4},{1,9},{5,13},{9,1},{13,5},{2,10},{6,14},... | collective-permute-start | bytes 786440 | tf_op jit(solution)/shard_map/ppermute | solution.py:297
  135.6 1.1 collective-permute-done.21
  136.8 4.8 %collective-permute-done.24 = f32[32,2048]{1,0:T(8,128)S(1)} collective-permute-done((f32[32,2048]{1,0:T(8,128)S(1)}, f32[32,2048]{1,0:T(8,128)S(1)}, u32[]{:S(2)}, u32[]{:S(2)}) %collective-permute-start.24) | collective-permute-done | bytes 262176 | tf_op jit(solution)/shard_map/ppermute | solution.py:297
  141.6 15.5 %collective-permute-done.25 = f32[32,2048]{1,0:T(8,128)S(1)} collective-permute-done((f32[32,2048]{1,0:T(8,128)S(1)}, f32[32,2048]{1,0:T(8,128)S(1)}, u32[]{:S(2)}, u32[]{:S(2)}) %collective-permute-start.25) | collective-permute-done | bytes 262176 | tf_op jit(solution)/shard_map/ppermute | solution.py:297
  157.1 2.0 %collective-permute-done.26 = f32[32,2048]{1,0:T(8,128)S(1)} collective-permute-done((f32[32,2048]{1,0:T(8,128)S(1)}, f32[32,2048]{1,0:T(8,128)S(1)}, u32[]{:S(2)}, u32[]{:S(2)}) %collective-permute-start.26) | collective-permute-done | bytes 262176 | tf_op jit(solution)/shard_map/ppermute | solution.py:297
  159.2 1.4 reshape.2013
  (73 shorter events, 8.0 us)
Async XLA Ops:
  1.2 10.0 %collective-permute-start.8 = (f32[54,256]{1,0:T(8,128)S(1)}, f32[54,256]{1,0:T(8,128)S(1)}, u32[]{:S(2)}, u32[]{:S(2)}) collective-permute-start(f32[54,256]{1,0:T(8,128)S(1)} %constant_dynamic-slice_fusion), channel_id=1, source_target_pairs={{0,12},{4,0},{8,4},{12,8},{1,13},{5,1},{9,5},{13,9},{2,14},{6,2},{... | collective-permute-start | bytes 165896 | tf_op jit(solution)/shard_map/ppermute | solution.py:297
  1.3 12.0 %collective-permute-start.7 = (f32[54,256]{1,0:T(8,128)S(1)}, f32[54,256]{1,0:T(8,128)S(1)}, u32[]{:S(2)}, u32[]{:S(2)}) collective-permute-start(f32[54,256]{1,0:T(8,128)S(1)} %constant_dynamic-slice_fusion), channel_id=1, source_target_pairs={{0,8},{4,12},{8,0},{12,4},{1,9},{5,13},{9,1},{13,5},{2,10},{6,14},... | collective-permute-start | bytes 165896 | tf_op jit(solution)/shard_map/ppermute | solution.py:297
  3.7 9.6 %collective-permute-start.6 = (f32[54,256]{1,0:T(8,128)S(1)}, f32[54,256]{1,0:T(8,128)S(1)}, u32[]{:S(2)}, u32[]{:S(2)}) collective-permute-start(f32[54,256]{1,0:T(8,128)S(1)} %constant_dynamic-slice_fusion), channel_id=1, source_target_pairs={{0,4},{4,8},{8,12},{12,0},{1,5},{5,9},{9,13},{13,1},{2,6},{6,10},{... | collective-permute-start | bytes 165896 | tf_op jit(solution)/shard_map/ppermute | solution.py:297
  7.6 1.5 copy-start
  7.6 12.4 %copy-start.1 = (s32[8,3]{0,1:T(4,128)S(1)}, s32[8,3]{0,1:T(4,128)}, u32[]{:S(2)}) copy-start(s32[8,3]{0,1:T(4,128)} %param.6) | copy-start | bytes 292
  7.7 25.2 %collective-permute-start.2 = (f32[48,1024]{1,0:T(8,128)S(1)}, f32[48,1024]{1,0:T(8,128)S(1)}, u32[]{:S(2)}, u32[]{:S(2)}) collective-permute-start(f32[48,1024]{1,0:T(8,128)S(1)} %get-tuple-element.145), channel_id=1, source_target_pairs={{0,12},{4,0},{8,4},{12,8},{1,13},{5,1},{9,5},{13,9},{2,14},{6,2},{... | collective-permute-start | bytes 589832 | tf_op jit(solution)/shard_map/ppermute | solution.py:297
  7.8 25.1 %collective-permute-start.1 = (f32[48,1024]{1,0:T(8,128)S(1)}, f32[48,1024]{1,0:T(8,128)S(1)}, u32[]{:S(2)}, u32[]{:S(2)}) collective-permute-start(f32[48,1024]{1,0:T(8,128)S(1)} %get-tuple-element.146), channel_id=1, source_target_pairs={{0,8},{4,12},{8,0},{12,4},{1,9},{5,13},{9,1},{13,5},{2,10},{6,14},... | collective-permute-start | bytes 589832 | tf_op jit(solution)/shard_map/ppermute | solution.py:297
  11.2 21.7 %collective-permute-start = (f32[48,1024]{1,0:T(8,128)S(1)}, f32[48,1024]{1,0:T(8,128)S(1)}, u32[]{:S(2)}, u32[]{:S(2)}) collective-permute-start(f32[48,1024]{1,0:T(8,128)S(1)} %get-tuple-element.147), channel_id=1, source_target_pairs={{0,4},{4,8},{8,12},{12,0},{1,5},{5,9},{9,13},{13,1},{2,6},{6,10},{... | collective-permute-start | bytes 589832 | tf_op jit(solution)/shard_map/ppermute | solution.py:297
  32.9 15.4 %collective-permute-start.3 = (f32[48,1024]{1,0:T(8,128)S(1)}, f32[48,1024]{1,0:T(8,128)S(1)}, u32[]{:S(2)}, u32[]{:S(2)}) collective-permute-start(f32[48,1024]{1,0:T(8,128)S(1)} %get-tuple-element.65), channel_id=1, source_target_pairs={{0,4},{4,8},{8,12},{12,0},{1,5},{5,9},{9,13},{13,1},{2,6},{6,10},{... | collective-permute-start | bytes 589832 | tf_op jit(solution)/shard_map/ppermute | solution.py:297
  32.9 17.1 %collective-permute-start.4 = (f32[48,1024]{1,0:T(8,128)S(1)}, f32[48,1024]{1,0:T(8,128)S(1)}, u32[]{:S(2)}, u32[]{:S(2)}) collective-permute-start(f32[48,1024]{1,0:T(8,128)S(1)} %get-tuple-element.66), channel_id=1, source_target_pairs={{0,8},{4,12},{8,0},{12,4},{1,9},{5,13},{9,1},{13,5},{2,10},{6,14},... | collective-permute-start | bytes 589832 | tf_op jit(solution)/shard_map/ppermute | solution.py:297
  34.8 18.0 %collective-permute-start.5 = (f32[48,1024]{1,0:T(8,128)S(1)}, f32[48,1024]{1,0:T(8,128)S(1)}, u32[]{:S(2)}, u32[]{:S(2)}) collective-permute-start(f32[48,1024]{1,0:T(8,128)S(1)} %get-tuple-element.67), channel_id=1, source_target_pairs={{0,12},{4,0},{8,4},{12,8},{1,13},{5,1},{9,5},{13,9},{2,14},{6,2},{... | collective-permute-start | bytes 589832 | tf_op jit(solution)/shard_map/ppermute | solution.py:297
  52.7 12.9 %collective-permute-start.9 = (f32[8,6,8,128]{3,2,1,0:T(8,128)S(1)}, f32[8,6,8,128]{3,2,1,0:T(8,128)S(1)}, u32[]{:S(2)}, u32[]{:S(2)}) collective-permute-start(f32[8,6,8,128]{3,2,1,0:T(8,128)S(1)} %get-tuple-element.84), channel_id=1, source_target_pairs={{0,4},{4,8},{8,12},{12,0},{1,5},{5,9},{9,13},{13,1},{2,6},{6,10},{... | collective-permute-start | bytes 589832 | tf_op jit(solution)/shard_map/ppermute | solution.py:297
  52.7 16.7 %collective-permute-start.10 = (f32[8,6,8,128]{3,2,1,0:T(8,128)S(1)}, f32[8,6,8,128]{3,2,1,0:T(8,128)S(1)}, u32[]{:S(2)}, u32[]{:S(2)}) collective-permute-start(f32[8,6,8,128]{3,2,1,0:T(8,128)S(1)} %get-tuple-element.85), channel_id=1, source_target_pairs={{0,8},{4,12},{8,0},{12,4},{1,9},{5,13},{9,1},{13,5},{2,10},{6,14},... | collective-permute-start | bytes 589832 | tf_op jit(solution)/shard_map/ppermute | solution.py:297
  53.1 18.0 %collective-permute-start.11 = (f32[8,6,8,128]{3,2,1,0:T(8,128)S(1)}, f32[8,6,8,128]{3,2,1,0:T(8,128)S(1)}, u32[]{:S(2)}, u32[]{:S(2)}) collective-permute-start(f32[8,6,8,128]{3,2,1,0:T(8,128)S(1)} %get-tuple-element.86), channel_id=1, source_target_pairs={{0,12},{4,0},{8,4},{12,8},{1,13},{5,1},{9,5},{13,9},{2,14},{6,2},{... | collective-permute-start | bytes 589832 | tf_op jit(solution)/shard_map/ppermute | solution.py:297
  71.2 19.8 %collective-permute-start.16 = (f32[4,8,6,8,128]{4,3,2,1,0:T(8,128)S(1)}, f32[4,8,6,8,128]{4,3,2,1,0:T(8,128)S(1)}, u32[]{:S(2)}, u32[]{:S(2)}) collective-permute-start(f32[4,8,6,8,128]{4,3,2,1,0:T(8,128)S(1)} %pad_maximum_fusion.1.refs_0_.refs_4_), channel_id=1, source_target_pairs={{0,2},{1,3},{2,0},{3,1},{4,6},{5,7},{6,4},{7,5},{8,10},{9,11},{10,... | collective-permute-start | bytes 2359304 | tf_op jit(solution)/shard_map/ppermute | solution.py:308
  71.5 5.7 %collective-permute-start.12 = (f32[8,6,8,128]{3,2,1,0:T(8,128)S(1)}, f32[8,6,8,128]{3,2,1,0:T(8,128)S(1)}, u32[]{:S(2)}, u32[]{:S(2)}) collective-permute-start(f32[8,6,8,128]{3,2,1,0:T(8,128)S(1)} %get-tuple-element.97), channel_id=1, source_target_pairs={{0,4},{4,8},{8,12},{12,0},{1,5},{5,9},{9,13},{13,1},{2,6},{6,10},{... | collective-permute-start | bytes 589832 | tf_op jit(solution)/shard_map/ppermute | solution.py:297
  71.6 16.4 %collective-permute-start.13 = (f32[8,6,8,128]{3,2,1,0:T(8,128)S(1)}, f32[8,6,8,128]{3,2,1,0:T(8,128)S(1)}, u32[]{:S(2)}, u32[]{:S(2)}) collective-permute-start(f32[8,6,8,128]{3,2,1,0:T(8,128)S(1)} %get-tuple-element.98), channel_id=1, source_target_pairs={{0,8},{4,12},{8,0},{12,4},{1,9},{5,13},{9,1},{13,5},{2,10},{6,14},... | collective-permute-start | bytes 589832 | tf_op jit(solution)/shard_map/ppermute | solution.py:297
  73.0 18.0 %collective-permute-start.14 = (f32[8,6,8,128]{3,2,1,0:T(8,128)S(1)}, f32[8,6,8,128]{3,2,1,0:T(8,128)S(1)}, u32[]{:S(2)}, u32[]{:S(2)}) collective-permute-start(f32[8,6,8,128]{3,2,1,0:T(8,128)S(1)} %get-tuple-element.99), channel_id=1, source_target_pairs={{0,12},{4,0},{8,4},{12,8},{1,13},{5,1},{9,5},{13,9},{2,14},{6,2},{... | collective-permute-start | bytes 589832 | tf_op jit(solution)/shard_map/ppermute | solution.py:297
  74.4 18.7 %collective-permute-start.17 = (f32[4,8,6,8,128]{4,3,2,1,0:T(8,128)S(1)}, f32[4,8,6,8,128]{4,3,2,1,0:T(8,128)S(1)}, u32[]{:S(2)}, u32[]{:S(2)}) collective-permute-start(f32[4,8,6,8,128]{4,3,2,1,0:T(8,128)S(1)} %pad_maximum_fusion.1.refs_0_.refs_4_), channel_id=1, source_target_pairs={{0,1},{1,0},{2,3},{3,2},{4,5},{5,4},{6,7},{7,6},{8,9},{9,8},{10,11... | collective-permute-start | bytes 2359304 | tf_op jit(solution)/shard_map/ppermute | solution.py:316
  91.0 2.5 %collective-permute-start.18 = (f32[4,8,6,8,128]{4,3,2,1,0:T(8,128)S(1)}, f32[4,8,6,8,128]{4,3,2,1,0:T(8,128)S(1)}, u32[]{:S(2)}, u32[]{:S(2)}) collective-permute-start(f32[4,8,6,8,128]{4,3,2,1,0:T(8,128)S(1)} %collective-permute-done.16.refs_1_), channel_id=1, source_target_pairs={{0,1},{1,0},{2,3},{3,2},{4,5},{5,4},{6,7},{7,6},{8,9},{9,8},{10,11... | collective-permute-start | bytes 2359304 | tf_op jit(solution)/shard_map/ppermute | solution.py:316
  91.6 19.9 %collective-permute-start.15 = (f32[4,8,6,8,128]{4,3,2,1,0:T(8,128)S(1)}, f32[4,8,6,8,128]{4,3,2,1,0:T(8,128)S(1)}, u32[]{:S(2)}, u32[]{:S(2)}) collective-permute-start(f32[4,8,6,8,128]{4,3,2,1,0:T(8,128)S(1)} %pad_maximum_fusion.refs_5_.refs_0_), channel_id=1, source_target_pairs={{0,2},{1,3},{2,0},{3,1},{4,6},{5,7},{6,4},{7,5},{8,10},{9,11},{10,... | collective-permute-start | bytes 2359304 | tf_op jit(solution)/shard_map/ppermute | solution.py:308
  92.8 21.7 %collective-permute-start.22 = (f32[4,8,6,8,128]{4,3,2,1,0:T(8,128)S(1)}, f32[4,8,6,8,128]{4,3,2,1,0:T(8,128)S(1)}, u32[]{:S(2)}, u32[]{:S(2)}) collective-permute-start(f32[4,8,6,8,128]{4,3,2,1,0:T(8,128)S(1)} %pad_maximum_fusion.refs_5_.refs_0_), channel_id=1, source_target_pairs={{0,1},{1,0},{2,3},{3,2},{4,5},{5,4},{6,7},{7,6},{8,9},{9,8},{10,11... | collective-permute-start | bytes 2359304 | tf_op jit(solution)/shard_map/ppermute | solution.py:316
  111.5 3.0 %collective-permute-start.23 = (f32[4,8,6,8,128]{4,3,2,1,0:T(8,128)S(1)}, f32[4,8,6,8,128]{4,3,2,1,0:T(8,128)S(1)}, u32[]{:S(2)}, u32[]{:S(2)}) collective-permute-start(f32[4,8,6,8,128]{4,3,2,1,0:T(8,128)S(1)} %collective-permute-done.15.refs_1_), channel_id=1, source_target_pairs={{0,1},{1,0},{2,3},{3,2},{4,5},{5,4},{6,7},{7,6},{8,9},{9,8},{10,11... | collective-permute-start | bytes 2359304 | tf_op jit(solution)/shard_map/ppermute | solution.py:316
  111.9 23.7 %collective-permute-start.19 = (f32[32,2048]{1,0:T(8,128)S(1)}, f32[32,2048]{1,0:T(8,128)S(1)}, u32[]{:S(2)}, u32[]{:S(2)}) collective-permute-start(f32[32,2048]{1,0:T(8,128)S(1)} %get-tuple-element.115), channel_id=1, source_target_pairs={{0,4},{4,8},{8,12},{12,0},{1,5},{5,9},{9,13},{13,1},{2,6},{6,10},{... | collective-permute-start | bytes 786440 | tf_op jit(solution)/shard_map/ppermute | solution.py:297
  111.9 23.7 %collective-permute-start.20 = (f32[32,2048]{1,0:T(8,128)S(1)}, f32[32,2048]{1,0:T(8,128)S(1)}, u32[]{:S(2)}, u32[]{:S(2)}) collective-permute-start(f32[32,2048]{1,0:T(8,128)S(1)} %get-tuple-element.116), channel_id=1, source_target_pairs={{0,8},{4,12},{8,0},{12,4},{1,9},{5,13},{9,1},{13,5},{2,10},{6,14},... | collective-permute-start | bytes 786440 | tf_op jit(solution)/shard_map/ppermute | solution.py:297
  113.0 23.7 %collective-permute-start.21 = (f32[32,2048]{1,0:T(8,128)S(1)}, f32[32,2048]{1,0:T(8,128)S(1)}, u32[]{:S(2)}, u32[]{:S(2)}) collective-permute-start(f32[32,2048]{1,0:T(8,128)S(1)} %get-tuple-element.117), channel_id=1, source_target_pairs={{0,12},{4,0},{8,4},{12,8},{1,13},{5,1},{9,5},{13,9},{2,14},{6,2},{... | collective-permute-start | bytes 786440 | tf_op jit(solution)/shard_map/ppermute | solution.py:297
  132.5 9.1 %collective-permute-start.24 = (f32[32,2048]{1,0:T(8,128)S(1)}, f32[32,2048]{1,0:T(8,128)S(1)}, u32[]{:S(2)}, u32[]{:S(2)}) collective-permute-start(f32[32,2048]{1,0:T(8,128)S(1)} %get-tuple-element.120), channel_id=1, source_target_pairs={{0,4},{4,8},{8,12},{12,0},{1,5},{5,9},{9,13},{13,1},{2,6},{6,10},{... | collective-permute-start | bytes 786440 | tf_op jit(solution)/shard_map/ppermute | solution.py:297
  132.7 24.4 %collective-permute-start.25 = (f32[32,2048]{1,0:T(8,128)S(1)}, f32[32,2048]{1,0:T(8,128)S(1)}, u32[]{:S(2)}, u32[]{:S(2)}) collective-permute-start(f32[32,2048]{1,0:T(8,128)S(1)} %get-tuple-element.121), channel_id=1, source_target_pairs={{0,8},{4,12},{8,0},{12,4},{1,9},{5,13},{9,1},{13,5},{2,10},{6,14},... | collective-permute-start | bytes 786440 | tf_op jit(solution)/shard_map/ppermute | solution.py:297
  135.6 23.5 %collective-permute-start.26 = (f32[32,2048]{1,0:T(8,128)S(1)}, f32[32,2048]{1,0:T(8,128)S(1)}, u32[]{:S(2)}, u32[]{:S(2)}) collective-permute-start(f32[32,2048]{1,0:T(8,128)S(1)} %get-tuple-element.122), channel_id=1, source_target_pairs={{0,12},{4,0},{8,4},{12,8},{1,13},{5,1},{9,5},{13,9},{2,14},{6,2},{... | collective-permute-start | bytes 786440 | tf_op jit(solution)/shard_map/ppermute | solution.py:297

commit v7 on v6

--- a/solution.py
+++ b/solution.py
@@ -361,7 +361,8 @@
     for c in range(chunks):
         sent = [lax.dynamic_index_in_dim(parts[c], lax.rem(tile + s, tiles), 0, keepdims=False) for s in range(tiles)]
         if c > 0:
-            fields[c - 1], sent = lax.optimization_barrier((fields[c - 1], sent))
+            for s in range(1, tiles):
+                fields[c - 1][s], sent[s] = lax.optimization_barrier((fields[c - 1][s], sent[s]))
         fields.append([along_tiles(block, s) for s, block in enumerate(sent)])
 
     k = jnp.arange(kt, dtype=jnp.int32)[:, None]
@@ -431,7 +432,9 @@
         if c + 1 < chunks:
             fields[c + 1], pieces = lax.optimization_barrier((fields[c + 1], pieces))
         if c > 0:
-            own, pieces = lax.optimization_barrier((own, pieces))
+            pieces = list(pieces)
+            for s in range(1, tiles):
+                own[s], pieces[s] = lax.optimization_barrier((own[s], pieces[s]))
             owns[c - 1] = jnp.stack(own)
         own = [along_tiles(pieces[s], s) for s in range(tiles)]
         owns.append(jnp.stack(own))

time: 161 us -> 160 us (level)
  waiting for transfers between devices: 48.2 us -> 45.6 us
  starting transfers between devices: 26.8 us -> 28.6 us
    ppermute x21, waiting for transfers between devices: 47.8 us -> 45.1 us  [along_tiles(): lax.ppermute(value, 'tile', [(i, (i + steps) % count) for i in range(coun...]
  transfers between devices with their start and end apart: 27 -> 27, of which waited for: 12 -> 10; matrix products, arithmetic and copies ran while one was open for 4% -> 4% of each run, Pallas kernels for 37% -> 37%
where the time goes in v7:
time: 160 us
  Pallas kernels  59 us (37%)
  waiting for transfers between devices  45.6 us (28%)
  starting transfers between devices  28.6 us (18%)
  blocking collectives  11.5 us (7%)
  between operations  6.62 us (4%)
  local copies, waits for them, and re-layouts  5.81 us (4%)
  other arithmetic  2.68 us (2%)
    ppermute x21, waiting for transfers between devices, along_tiles(): lax.ppermute(value, 'tile', [(i, (i + steps) % count) for i in range(coun...  45.1 us
    pallas_call x2, Pallas kernels, local(): pl.pallas_call(functools.partial(contract_kernel, vecs, chunks, slots, mo...  35.9 us
    ppermute x21, starting transfers between devices, along_tiles(): lax.ppermute(value, 'tile', [(i, (i + steps) % count) for i in range(coun...  22.5 us
    pallas_call x1, Pallas kernels, local(): call(out_shape=(*piece_shapes, jax.ShapeDtypeStruct((slots, kt, 18, LANES...  12.1 us
    all_gather x1, blocking collectives, local(): gauge = lax.all_gather(jnp.stack(shares), 'vec', axis=0)  11.5 us
    pallas_call x1, Pallas kernels, local(): call(out_shape=piece_shapes, in_specs=[smem] + [vmem] * (tiles + 1), out_...  11 us
    ppermute x4, starting transfers between devices, over_cores(): lax.ppermute(block, 'vec', [(i, i ^ 1) for i in range(count)])  4.61 us
  transfers between devices with their start and end apart: 27, of which 10 were waited for; matrix products, arithmetic and copies ran while one was open for 4% of the time, Pallas kernels for 37%

profile of v7, /device:TPU:9, one launch (start us, length us, event | category | flops | bytes accessed | tf_op | source)
XLA Modules:
  0.0 159.8 jit_solution(3984500196615725994)
XLA Ops:
  0.0 1.1 copy.14
  1.2 1.3 collective-permute-start.6
  2.5 1.1 collective-permute-start.7
  3.6 1.4 collective-permute-start.8
  5.0 1.5 fusion.90
  6.8 1.1 collective-permute-start.4
  10.5 1.2 collective-permute-start
  19.6 11.5 %all-gather = f32[16,54,256]{2,1,0:T(8,128)S(1)} all-gather(f32[4,54,256]{2,1,0:T(8,128)S(1)} %pad_maximum_fusion.3), channel_id=2, replica_groups=mesh['groups'=2,'tile'=4,'vec'=4] {'vec'}, dimensions={0}, use_global_device_ids=true | all-gather | bytes 1105920 | tf_op jit(solution)/shard_map/all_gather | solution.py:359
  31.4 2.3 %collective-permute-start.3 = (f32[48,1024]{1,0:T(8,128)S(1)}, f32[48,1024]{1,0:T(8,128)S(1)}, u32[]{:S(2)}, u32[]{:S(2)}) collective-permute-start(f32[48,1024]{1,0:T(8,128)S(1)} %get-tuple-element.61), channel_id=1, source_target_pairs={{0,8},{4,12},{8,0},{12,4},{1,9},{5,13},{9,1},{13,5},{2,10},{6,14},... | collective-permute-start | bytes 589832 | tf_op jit(solution)/shard_map/ppermute | solution.py:297
  33.7 2.2 %collective-permute-start.1 = (f32[48,1024]{1,0:T(8,128)S(1)}, f32[48,1024]{1,0:T(8,128)S(1)}, u32[]{:S(2)}, u32[]{:S(2)}) collective-permute-start(f32[48,1024]{1,0:T(8,128)S(1)} %get-tuple-element.60), channel_id=1, source_target_pairs={{0,4},{4,8},{8,12},{12,0},{1,5},{5,9},{9,13},{13,1},{2,6},{6,10},{... | collective-permute-start | bytes 589832 | tf_op jit(solution)/shard_map/ppermute | solution.py:297
  35.9 12.1 %chebyshev.2 = (f32[8,6,8,128]{3,2,1,0:T(8,128)S(1)}, f32[8,6,8,128]{3,2,1,0:T(8,128)S(1)}, f32[8,6,8,128]{3,2,1,0:T(8,128)S(1)}, f32[8,6,8,128]{3,2,1,0:T(8,128...) custom-call(s32[4]{0:T(128)S(1)} %pad_add_fusion.2.refs_0_, ...), custom_call_target="tpu_custom_call" | custom-call | flops 14155776000 | bytes 1572864 | tf_op jit(solution)/shard_map/chebyshev/pallas_call | solution.py:419
  48.0 2.3 %collective-permute-done.1.refs_2_ = f32[48,1024]{1,0:T(8,128)S(1)} collective-permute-done((f32[48,1024]{1,0:T(8,128)S(1)}, f32[48,1024]{1,0:T(8,128)S(1)}, u32[]{:S(2)}, u32[]{:S(2)}) %collective-permute-start.1) | collective-permute-done | bytes 196640 | tf_op jit(solution)/shard_map/ppermute | solution.py:297
  50.3 2.2 %collective-permute-start.9 = (f32[8,6,8,128]{3,2,1,0:T(8,128)S(1)}, f32[8,6,8,128]{3,2,1,0:T(8,128)S(1)}, u32[]{:S(2)}, u32[]{:S(2)}) collective-permute-start(f32[8,6,8,128]{3,2,1,0:T(8,128)S(1)} %get-tuple-element.83), channel_id=1, source_target_pairs={{0,4},{4,8},{8,12},{12,0},{1,5},{5,9},{9,13},{13,1},{2,6},{6,10},{... | collective-permute-start | bytes 589832 | tf_op jit(solution)/shard_map/ppermute | solution.py:297
  52.5 1.0 collective-permute-start.11
  53.6 11.0 %chebyshev.3 = (f32[8,6,8,128]{3,2,1,0:T(8,128)S(1)}, f32[8,6,8,128]{3,2,1,0:T(8,128)S(1)}, f32[8,6,8,128]{3,2,1,0:T(8,128)S(1)}, f32[8,6,8,128]{3,2,1,0:T(8,128)S(1)}) custom-call(s32[4]{0:T(128)S(1)} %pad_add_fusion.2.refs_0_, f32[48,1024]{1,0:T(8,128)S(1)} %get-tuple-element.77.refs_1_, f32[48,1024]{1,0:T(8,128)S(1)} %collective-permute-done.1.refs_2_, ...), custom_call_target="tpu_custom_call" | custom-call | flops 14155776000 | bytes 1572864 | tf_op jit(solution)/shard_map/chebyshev/pallas_call | solution.py:429
  64.7 3.5 %collective-permute-done.11 = f32[8,6,8,128]{3,2,1,0:T(8,128)S(1)} collective-permute-done((f32[8,6,8,128]{3,2,1,0:T(8,128)S(1)}, f32[8,6,8,128]{3,2,1,0:T(8,128)S(1)}, u32[]{:S(2)}, u32[]{:S(2)}) %collective-permute-start.11) | collective-permute-done | bytes 196640 | tf_op jit(solution)/shard_map/ppermute | solution.py:297
  68.2 2.1 %collective-permute-done.13 = f32[8,6,8,128]{3,2,1,0:T(8,128)S(1)} collective-permute-done((f32[8,6,8,128]{3,2,1,0:T(8,128)S(1)}, f32[8,6,8,128]{3,2,1,0:T(8,128)S(1)}, u32[]{:S(2)}, u32[]{:S(2)}) %collective-permute-start.13) | collective-permute-done | bytes 196640 | tf_op jit(solution)/shard_map/ppermute | solution.py:297
  71.7 1.5 collective-permute-start.14
  73.1 3.1 %collective-permute-start.17 = (f32[4,8,6,8,128]{4,3,2,1,0:T(8,128)S(1)}, f32[4,8,6,8,128]{4,3,2,1,0:T(8,128)S(1)}, u32[]{:S(2)}, u32[]{:S(2)}) collective-permute-start(f32[4,8,6,8,128]{4,3,2,1,0:T(8,128)S(1)} %pad_maximum_fusion.1.refs_0_.refs_4_), channel_id=1, source_target_pairs={{0,1},{1,0},{2,3},{3,2},{4,5},{5,4},{6,7},{7,6},{8,9},{9,8},{10,11... | collective-permute-start | bytes 2359304 | tf_op jit(solution)/shard_map/ppermute | solution.py:316
  76.3 10.2 %collective-permute-done.12 = f32[8,6,8,128]{3,2,1,0:T(8,128)S(1)} collective-permute-done((f32[8,6,8,128]{3,2,1,0:T(8,128)S(1)}, f32[8,6,8,128]{3,2,1,0:T(8,128)S(1)}, u32[]{:S(2)}, u32[]{:S(2)}) %collective-permute-start.12) | collective-permute-done | bytes 196640 | tf_op jit(solution)/shard_map/ppermute | solution.py:297
  86.4 3.2 %collective-permute-done.14 = f32[8,6,8,128]{3,2,1,0:T(8,128)S(1)} collective-permute-done((f32[8,6,8,128]{3,2,1,0:T(8,128)S(1)}, f32[8,6,8,128]{3,2,1,0:T(8,128)S(1)}, u32[]{:S(2)}, u32[]{:S(2)}) %collective-permute-start.14) | collective-permute-done | bytes 196640 | tf_op jit(solution)/shard_map/ppermute | solution.py:297
  90.4 1.1 collective-permute-start.15
  92.3 18.0 %contract.2 = (f32[32,2048]{1,0:T(8,128)S(1)}, f32[32,2048]{1,0:T(8,128)S(1)}, f32[32,2048]{1,0:T(8,128)S(1)}, f32[32,2048]{1,0:T(8,128)S(1)}) custom-call(s32[4,17]{1,0:T(4,128)S(1)} %pad_add_fusion.1.scal, f32[4,8,6,8,128]{4,3,2,1,0:T(8,128)S(1)} %pad_maximum_fusion.1.refs_0_.refs_4_, f32[4,8,6,8,128]{4,3,2,1,0:T(8,128)S(1)} %collective-permute-done.16.refs_1_, ...), custom_call_target="tpu_custom_call" | custom-call | flops 19327352832 | bytes 4194304 | tf_op jit(solution)/shard_map/contract/pallas_call | solution.py:463
  110.8 1.3 collective-permute-start.20
  112.1 1.5 collective-permute-start.21
  113.5 18.0 %contract.3 = (f32[32,2048]{1,0:T(8,128)S(1)}, f32[32,2048]{1,0:T(8,128)S(1)}, f32[32,2048]{1,0:T(8,128)S(1)}, f32[32,2048]{1,0:T(8,128)S(1)}) custom-call(s32[4,17]{1,0:T(4,128)S(1)} %pad_add_fusion.1.scal, f32[4,8,6,8,128]{4,3,2,1,0:T(8,128)S(1)} %pad_maximum_fusion.refs_5_.refs_0_, f32[4,8,6,8,128]{4,3,2,1,0:T(8,128)S(1)} %collective-permute-done.15.refs_1_, ...), custom_call_target="tpu_custom_call" | custom-call | flops 19327352832 | bytes 4194304 | tf_op jit(solution)/shard_map/contract/pallas_call | solution.py:463
  131.6 2.8 %collective-permute-start.25 = (f32[32,2048]{1,0:T(8,128)S(1)}, f32[32,2048]{1,0:T(8,128)S(1)}, u32[]{:S(2)}, u32[]{:S(2)}) collective-permute-start(f32[32,2048]{1,0:T(8,128)S(1)} %get-tuple-element.113), channel_id=1, source_target_pairs={{0,8},{4,12},{8,0},{12,4},{1,9},{5,13},{9,1},{13,5},{2,10},{6,14},... | collective-permute-start | bytes 786440 | tf_op jit(solution)/shard_map/ppermute | solution.py:297
  134.4 1.3 collective-permute-done.21
  135.8 4.4 %collective-permute-done.24 = f32[32,2048]{1,0:T(8,128)S(1)} collective-permute-done((f32[32,2048]{1,0:T(8,128)S(1)}, f32[32,2048]{1,0:T(8,128)S(1)}, u32[]{:S(2)}, u32[]{:S(2)}) %collective-permute-start.24) | collective-permute-done | bytes 262176 | tf_op jit(solution)/shard_map/ppermute | solution.py:297
  140.2 15.7 %collective-permute-done.25 = f32[32,2048]{1,0:T(8,128)S(1)} collective-permute-done((f32[32,2048]{1,0:T(8,128)S(1)}, f32[32,2048]{1,0:T(8,128)S(1)}, u32[]{:S(2)}, u32[]{:S(2)}) %collective-permute-start.25) | collective-permute-done | bytes 262176 | tf_op jit(solution)/shard_map/ppermute | solution.py:297
  155.9 2.4 %collective-permute-done.26 = f32[32,2048]{1,0:T(8,128)S(1)} collective-permute-done((f32[32,2048]{1,0:T(8,128)S(1)}, f32[32,2048]{1,0:T(8,128)S(1)}, u32[]{:S(2)}, u32[]{:S(2)}) %collective-permute-start.26) | collective-permute-done | bytes 262176 | tf_op jit(solution)/shard_map/ppermute | solution.py:297
  158.4 1.4 reshape.2013
  (73 shorter events, 8.5 us)
Async XLA Ops:
  1.2 9.3 %collective-permute-start.6 = (f32[54,256]{1,0:T(8,128)S(1)}, f32[54,256]{1,0:T(8,128)S(1)}, u32[]{:S(2)}, u32[]{:S(2)}) collective-permute-start(f32[54,256]{1,0:T(8,128)S(1)} %constant_dynamic-slice_fusion), channel_id=1, source_target_pairs={{0,4},{4,8},{8,12},{12,0},{1,5},{5,9},{9,13},{13,1},{2,6},{6,10},{... | collective-permute-start | bytes 165896 | tf_op jit(solution)/shard_map/ppermute | solution.py:297
  2.5 9.1 %collective-permute-start.7 = (f32[54,256]{1,0:T(8,128)S(1)}, f32[54,256]{1,0:T(8,128)S(1)}, u32[]{:S(2)}, u32[]{:S(2)}) collective-permute-start(f32[54,256]{1,0:T(8,128)S(1)} %constant_dynamic-slice_fusion), channel_id=1, source_target_pairs={{0,8},{4,12},{8,0},{12,4},{1,9},{5,13},{9,1},{13,5},{2,10},{6,14},... | collective-permute-start | bytes 165896 | tf_op jit(solution)/shard_map/ppermute | solution.py:297
  3.6 8.1 %collective-permute-start.8 = (f32[54,256]{1,0:T(8,128)S(1)}, f32[54,256]{1,0:T(8,128)S(1)}, u32[]{:S(2)}, u32[]{:S(2)}) collective-permute-start(f32[54,256]{1,0:T(8,128)S(1)} %constant_dynamic-slice_fusion), channel_id=1, source_target_pairs={{0,12},{4,0},{8,4},{12,8},{1,13},{5,1},{9,5},{13,9},{2,14},{6,2},{... | collective-permute-start | bytes 165896 | tf_op jit(solution)/shard_map/ppermute | solution.py:297
  6.7 1.6 copy-start
  6.7 11.9 %copy-start.1 = (s32[8,3]{0,1:T(4,128)S(1)}, s32[8,3]{0,1:T(4,128)}, u32[]{:S(2)}) copy-start(s32[8,3]{0,1:T(4,128)} %param.6) | copy-start | bytes 292
  6.8 24.3 %collective-permute-start.4 = (f32[48,1024]{1,0:T(8,128)S(1)}, f32[48,1024]{1,0:T(8,128)S(1)}, u32[]{:S(2)}, u32[]{:S(2)}) collective-permute-start(f32[48,1024]{1,0:T(8,128)S(1)} %get-tuple-element.137), channel_id=1, source_target_pairs={{0,12},{4,0},{8,4},{12,8},{1,13},{5,1},{9,5},{13,9},{2,14},{6,2},{... | collective-permute-start | bytes 589832 | tf_op jit(solution)/shard_map/ppermute | solution.py:297
  7.9 23.2 %collective-permute-start.2 = (f32[48,1024]{1,0:T(8,128)S(1)}, f32[48,1024]{1,0:T(8,128)S(1)}, u32[]{:S(2)}, u32[]{:S(2)}) collective-permute-start(f32[48,1024]{1,0:T(8,128)S(1)} %get-tuple-element.139), channel_id=1, source_target_pairs={{0,8},{4,12},{8,0},{12,4},{1,9},{5,13},{9,1},{13,5},{2,10},{6,14},... | collective-permute-start | bytes 589832 | tf_op jit(solution)/shard_map/ppermute | solution.py:297
  10.5 20.6 %collective-permute-start = (f32[48,1024]{1,0:T(8,128)S(1)}, f32[48,1024]{1,0:T(8,128)S(1)}, u32[]{:S(2)}, u32[]{:S(2)}) collective-permute-start(f32[48,1024]{1,0:T(8,128)S(1)} %get-tuple-element.140), channel_id=1, source_target_pairs={{0,4},{4,8},{8,12},{12,0},{1,5},{5,9},{9,13},{13,1},{2,6},{6,10},{... | collective-permute-start | bytes 589832 | tf_op jit(solution)/shard_map/ppermute | solution.py:297
  31.1 16.9 %collective-permute-start.5 = (f32[48,1024]{1,0:T(8,128)S(1)}, f32[48,1024]{1,0:T(8,128)S(1)}, u32[]{:S(2)}, u32[]{:S(2)}) collective-permute-start(f32[48,1024]{1,0:T(8,128)S(1)} %get-tuple-element.62), channel_id=1, source_target_pairs={{0,12},{4,0},{8,4},{12,8},{1,13},{5,1},{9,5},{13,9},{2,14},{6,2},{... | collective-permute-start | bytes 589832 | tf_op jit(solution)/shard_map/ppermute | solution.py:297
  31.4 16.6 %collective-permute-start.3 = (f32[48,1024]{1,0:T(8,128)S(1)}, f32[48,1024]{1,0:T(8,128)S(1)}, u32[]{:S(2)}, u32[]{:S(2)}) collective-permute-start(f32[48,1024]{1,0:T(8,128)S(1)} %get-tuple-element.61), channel_id=1, source_target_pairs={{0,8},{4,12},{8,0},{12,4},{1,9},{5,13},{9,1},{13,5},{2,10},{6,14},... | collective-permute-start | bytes 589832 | tf_op jit(solution)/shard_map/ppermute | solution.py:297
  33.7 16.6 %collective-permute-start.1 = (f32[48,1024]{1,0:T(8,128)S(1)}, f32[48,1024]{1,0:T(8,128)S(1)}, u32[]{:S(2)}, u32[]{:S(2)}) collective-permute-start(f32[48,1024]{1,0:T(8,128)S(1)} %get-tuple-element.60), channel_id=1, source_target_pairs={{0,4},{4,8},{8,12},{12,0},{1,5},{5,9},{9,13},{13,1},{2,6},{6,10},{... | collective-permute-start | bytes 589832 | tf_op jit(solution)/shard_map/ppermute | solution.py:297
  50.3 14.4 %collective-permute-start.9 = (f32[8,6,8,128]{3,2,1,0:T(8,128)S(1)}, f32[8,6,8,128]{3,2,1,0:T(8,128)S(1)}, u32[]{:S(2)}, u32[]{:S(2)}) collective-permute-start(f32[8,6,8,128]{3,2,1,0:T(8,128)S(1)} %get-tuple-element.83), channel_id=1, source_target_pairs={{0,4},{4,8},{8,12},{12,0},{1,5},{5,9},{9,13},{13,1},{2,6},{6,10},{... | collective-permute-start | bytes 589832 | tf_op jit(solution)/shard_map/ppermute | solution.py:297
  52.5 15.7 %collective-permute-start.11 = (f32[8,6,8,128]{3,2,1,0:T(8,128)S(1)}, f32[8,6,8,128]{3,2,1,0:T(8,128)S(1)}, u32[]{:S(2)}, u32[]{:S(2)}) collective-permute-start(f32[8,6,8,128]{3,2,1,0:T(8,128)S(1)} %get-tuple-element.86), channel_id=1, source_target_pairs={{0,8},{4,12},{8,0},{12,4},{1,9},{5,13},{9,1},{13,5},{2,10},{6,14},... | collective-permute-start | bytes 589832 | tf_op jit(solution)/shard_map/ppermute | solution.py:297
  53.5 16.9 %collective-permute-start.13 = (f32[8,6,8,128]{3,2,1,0:T(8,128)S(1)}, f32[8,6,8,128]{3,2,1,0:T(8,128)S(1)}, u32[]{:S(2)}, u32[]{:S(2)}) collective-permute-start(f32[8,6,8,128]{3,2,1,0:T(8,128)S(1)} %get-tuple-element.89), channel_id=1, source_target_pairs={{0,12},{4,0},{8,4},{12,8},{1,13},{5,1},{9,5},{13,9},{2,14},{6,2},{... | collective-permute-start | bytes 589832 | tf_op jit(solution)/shard_map/ppermute | solution.py:297
  70.4 19.3 %collective-permute-start.16 = (f32[4,8,6,8,128]{4,3,2,1,0:T(8,128)S(1)}, f32[4,8,6,8,128]{4,3,2,1,0:T(8,128)S(1)}, u32[]{:S(2)}, u32[]{:S(2)}) collective-permute-start(f32[4,8,6,8,128]{4,3,2,1,0:T(8,128)S(1)} %pad_maximum_fusion.1.refs_0_.refs_4_), channel_id=1, source_target_pairs={{0,2},{1,3},{2,0},{3,1},{4,6},{5,7},{6,4},{7,5},{8,10},{9,11},{10,... | collective-permute-start | bytes 2359304 | tf_op jit(solution)/shard_map/ppermute | solution.py:308
  70.7 5.6 %collective-permute-start.10 = (f32[8,6,8,128]{3,2,1,0:T(8,128)S(1)}, f32[8,6,8,128]{3,2,1,0:T(8,128)S(1)}, u32[]{:S(2)}, u32[]{:S(2)}) collective-permute-start(f32[8,6,8,128]{3,2,1,0:T(8,128)S(1)} %get-tuple-element.85), channel_id=1, source_target_pairs={{0,4},{4,8},{8,12},{12,0},{1,5},{5,9},{9,13},{13,1},{2,6},{6,10},{... | collective-permute-start | bytes 589832 | tf_op jit(solution)/shard_map/ppermute | solution.py:297
  70.7 15.7 %collective-permute-start.12 = (f32[8,6,8,128]{3,2,1,0:T(8,128)S(1)}, f32[8,6,8,128]{3,2,1,0:T(8,128)S(1)}, u32[]{:S(2)}, u32[]{:S(2)}) collective-permute-start(f32[8,6,8,128]{3,2,1,0:T(8,128)S(1)} %get-tuple-element.88), channel_id=1, source_target_pairs={{0,8},{4,12},{8,0},{12,4},{1,9},{5,13},{9,1},{13,5},{2,10},{6,14},... | collective-permute-start | bytes 589832 | tf_op jit(solution)/shard_map/ppermute | solution.py:297
  71.7 18.0 %collective-permute-start.14 = (f32[8,6,8,128]{3,2,1,0:T(8,128)S(1)}, f32[8,6,8,128]{3,2,1,0:T(8,128)S(1)}, u32[]{:S(2)}, u32[]{:S(2)}) collective-permute-start(f32[8,6,8,128]{3,2,1,0:T(8,128)S(1)} %get-tuple-element.91), channel_id=1, source_target_pairs={{0,12},{4,0},{8,4},{12,8},{1,13},{5,1},{9,5},{13,9},{2,14},{6,2},{... | collective-permute-start | bytes 589832 | tf_op jit(solution)/shard_map/ppermute | solution.py:297
  73.1 18.7 %collective-permute-start.17 = (f32[4,8,6,8,128]{4,3,2,1,0:T(8,128)S(1)}, f32[4,8,6,8,128]{4,3,2,1,0:T(8,128)S(1)}, u32[]{:S(2)}, u32[]{:S(2)}) collective-permute-start(f32[4,8,6,8,128]{4,3,2,1,0:T(8,128)S(1)} %pad_maximum_fusion.1.refs_0_.refs_4_), channel_id=1, source_target_pairs={{0,1},{1,0},{2,3},{3,2},{4,5},{5,4},{6,7},{7,6},{8,9},{9,8},{10,11... | collective-permute-start | bytes 2359304 | tf_op jit(solution)/shard_map/ppermute | solution.py:316
  89.7 2.6 %collective-permute-start.18 = (f32[4,8,6,8,128]{4,3,2,1,0:T(8,128)S(1)}, f32[4,8,6,8,128]{4,3,2,1,0:T(8,128)S(1)}, u32[]{:S(2)}, u32[]{:S(2)}) collective-permute-start(f32[4,8,6,8,128]{4,3,2,1,0:T(8,128)S(1)} %collective-permute-done.16.refs_1_), channel_id=1, source_target_pairs={{0,1},{1,0},{2,3},{3,2},{4,5},{5,4},{6,7},{7,6},{8,9},{9,8},{10,11... | collective-permute-start | bytes 2359304 | tf_op jit(solution)/shard_map/ppermute | solution.py:316
  90.4 19.9 %collective-permute-start.15 = (f32[4,8,6,8,128]{4,3,2,1,0:T(8,128)S(1)}, f32[4,8,6,8,128]{4,3,2,1,0:T(8,128)S(1)}, u32[]{:S(2)}, u32[]{:S(2)}) collective-permute-start(f32[4,8,6,8,128]{4,3,2,1,0:T(8,128)S(1)} %pad_maximum_fusion.refs_5_.refs_0_), channel_id=1, source_target_pairs={{0,2},{1,3},{2,0},{3,1},{4,6},{5,7},{6,4},{7,5},{8,10},{9,11},{10,... | collective-permute-start | bytes 2359304 | tf_op jit(solution)/shard_map/ppermute | solution.py:308
  91.5 22.0 %collective-permute-start.22 = (f32[4,8,6,8,128]{4,3,2,1,0:T(8,128)S(1)}, f32[4,8,6,8,128]{4,3,2,1,0:T(8,128)S(1)}, u32[]{:S(2)}, u32[]{:S(2)}) collective-permute-start(f32[4,8,6,8,128]{4,3,2,1,0:T(8,128)S(1)} %pad_maximum_fusion.refs_5_.refs_0_), channel_id=1, source_target_pairs={{0,1},{1,0},{2,3},{3,2},{4,5},{5,4},{6,7},{7,6},{8,9},{9,8},{10,11... | collective-permute-start | bytes 2359304 | tf_op jit(solution)/shard_map/ppermute | solution.py:316
  110.3 3.2 %collective-permute-start.23 = (f32[4,8,6,8,128]{4,3,2,1,0:T(8,128)S(1)}, f32[4,8,6,8,128]{4,3,2,1,0:T(8,128)S(1)}, u32[]{:S(2)}, u32[]{:S(2)}) collective-permute-start(f32[4,8,6,8,128]{4,3,2,1,0:T(8,128)S(1)} %collective-permute-done.15.refs_1_), channel_id=1, source_target_pairs={{0,1},{1,0},{2,3},{3,2},{4,5},{5,4},{6,7},{7,6},{8,9},{9,8},{10,11... | collective-permute-start | bytes 2359304 | tf_op jit(solution)/shard_map/ppermute | solution.py:316
  110.7 23.7 %collective-permute-start.19 = (f32[32,2048]{1,0:T(8,128)S(1)}, f32[32,2048]{1,0:T(8,128)S(1)}, u32[]{:S(2)}, u32[]{:S(2)}) collective-permute-start(f32[32,2048]{1,0:T(8,128)S(1)} %get-tuple-element.107), channel_id=1, source_target_pairs={{0,4},{4,8},{8,12},{12,0},{1,5},{5,9},{9,13},{13,1},{2,6},{6,10},{... | collective-permute-start | bytes 786440 | tf_op jit(solution)/shard_map/ppermute | solution.py:297
  110.8 23.7 %collective-permute-start.20 = (f32[32,2048]{1,0:T(8,128)S(1)}, f32[32,2048]{1,0:T(8,128)S(1)}, u32[]{:S(2)}, u32[]{:S(2)}) collective-permute-start(f32[32,2048]{1,0:T(8,128)S(1)} %get-tuple-element.108), channel_id=1, source_target_pairs={{0,8},{4,12},{8,0},{12,4},{1,9},{5,13},{9,1},{13,5},{2,10},{6,14},... | collective-permute-start | bytes 786440 | tf_op jit(solution)/shard_map/ppermute | solution.py:297
  112.1 23.7 %collective-permute-start.21 = (f32[32,2048]{1,0:T(8,128)S(1)}, f32[32,2048]{1,0:T(8,128)S(1)}, u32[]{:S(2)}, u32[]{:S(2)}) collective-permute-start(f32[32,2048]{1,0:T(8,128)S(1)} %get-tuple-element.109), channel_id=1, source_target_pairs={{0,12},{4,0},{8,4},{12,8},{1,13},{5,1},{9,5},{13,9},{2,14},{6,2},{... | collective-permute-start | bytes 786440 | tf_op jit(solution)/shard_map/ppermute | solution.py:297
  131.5 8.7 %collective-permute-start.24 = (f32[32,2048]{1,0:T(8,128)S(1)}, f32[32,2048]{1,0:T(8,128)S(1)}, u32[]{:S(2)}, u32[]{:S(2)}) collective-permute-start(f32[32,2048]{1,0:T(8,128)S(1)} %get-tuple-element.112), channel_id=1, source_target_pairs={{0,4},{4,8},{8,12},{12,0},{1,5},{5,9},{9,13},{13,1},{2,6},{6,10},{... | collective-permute-start | bytes 786440 | tf_op jit(solution)/shard_map/ppermute | solution.py:297
  131.6 24.3 %collective-permute-start.25 = (f32[32,2048]{1,0:T(8,128)S(1)}, f32[32,2048]{1,0:T(8,128)S(1)}, u32[]{:S(2)}, u32[]{:S(2)}) collective-permute-start(f32[32,2048]{1,0:T(8,128)S(1)} %get-tuple-element.113), channel_id=1, source_target_pairs={{0,8},{4,12},{8,0},{12,4},{1,9},{5,13},{9,1},{13,5},{2,10},{6,14},... | collective-permute-start | bytes 786440 | tf_op jit(solution)/shard_map/ppermute | solution.py:297
  134.4 23.8 %collective-permute-start.26 = (f32[32,2048]{1,0:T(8,128)S(1)}, f32[32,2048]{1,0:T(8,128)S(1)}, u32[]{:S(2)}, u32[]{:S(2)}) collective-permute-start(f32[32,2048]{1,0:T(8,128)S(1)} %get-tuple-element.114), channel_id=1, source_target_pairs={{0,12},{4,0},{8,4},{12,8},{1,13},{5,1},{9,5},{13,9},{2,14},{6,2},{... | collective-permute-start | bytes 786440 | tf_op jit(solution)/shard_map/ppermute | solution.py:297

commit v8 on v7

--- a/solution.py
+++ b/solution.py
@@ -77,10 +77,12 @@
     lax.fori_loop(0, kt, one, 0, unroll=tiles <= 4)
 
 
-def filter_kernel(tiles, kt, rows, with_links, *refs):
+def filter_kernel(tiles, vecs, kt, rows, with_links, *refs):
     scal, slab_refs, refs = refs[0], refs[1 : 1 + tiles], refs[1 + tiles :]
     if with_links:
-        link_ref, piece_refs, (glink_ref, l_ref, a_ref, b_ref) = refs[0], refs[1 : 1 + tiles], refs[1 + tiles :]
+        link_refs, piece_refs, refs = refs[:vecs], refs[vecs : vecs + tiles], refs[vecs + tiles :]
+        glink_ref, l_ref, a_ref, b_ref = refs
+        slots = glink_ref.shape[0]
     else:
         l_ref, piece_refs, (a_ref, b_ref) = refs[0], refs[1 : 1 + tiles], refs[1 + tiles :]
     mine = scal[1]
@@ -117,10 +119,11 @@
             for c in range(comps):
                 a_ref[t * kt + k, c] = slab_refs[s][c * rows : (c + 1) * rows, lanes]
             if with_links:
-                share = link_ref.shape[3] // LANES
-                lanes = slice(k % share * LANES, (k % share + 1) * LANES)
+                share = kt // vecs
+                block, part = divmod(k, share)
+                n = t * kt + scal[2 + slots + block] * share + part
                 for m in range(3):
-                    l_ref[m, t * kt + k] = link_ref[k // share, s, 18 * m : 18 * m + 18, lanes]
+                    l_ref[m, n] = link_refs[block][s, 18 * m : 18 * m + 18, part * LANES : (part + 1) * LANES]
 
     if with_links:
 
@@ -347,7 +350,7 @@
     uses_y = jnp.any(heading == 1)
     uses_x = jnp.any(heading == 0)
     mode = jnp.where(uses_y, jnp.where(uses_x, 2, 0), 1).astype(jnp.int32)
-    scal = jnp.concatenate([jnp.stack([mode, tile.astype(jnp.int32)]), directions.astype(jnp.int32)])
+    scal = jnp.concatenate([jnp.stack([mode, tile.astype(jnp.int32)]), directions.astype(jnp.int32), block_owners()])
 
     parts = jnp.transpose(vectors, (0, 2, 1, 3)).reshape(6, tiles, chunks, nvc, sites)
     parts = jnp.transpose(parts, (2, 1, 0, 3, 4)).reshape(chunks, tiles, 6 * nvc, sites)
@@ -356,7 +359,8 @@
     shares = [along_tiles(link_share, s) for s in range(tiles)]
     shares, momenta, directions = lax.optimization_barrier((shares, momenta, directions))
     heading = directions % 3
-    gauge = lax.all_gather(jnp.stack(shares), "vec", axis=0)
+    gauge = over_chips(jnp.stack(shares))
+    gauge = gauge + over_cores(gauge)
     fields = []
     for c in range(chunks):
         sent = [lax.dynamic_index_in_dim(parts[c], lax.rem(tile + s, tiles), 0, keepdims=False) for s in range(tiles)]
@@ -407,7 +411,7 @@
         scratch = [pltpu.VMEM((nt, 6, nvc, LANES), f32)] * 2
         call = functools.partial(
             pl.pallas_call,
-            functools.partial(filter_kernel, tiles, kt, nvc, c == 0),
+            functools.partial(filter_kernel, tiles, vecs, kt, nvc, c == 0),
             scratch_shapes=scratch,
             compiler_params=pltpu.CompilerParams(vmem_limit_bytes=48 << 20),
             cost_estimate=pl.CostEstimate(
@@ -422,9 +426,9 @@
                     jax.ShapeDtypeStruct((slots, kt, 18, LANES), f32),
                     jax.ShapeDtypeStruct(link_shape, f32),
                 ),
-                in_specs=[smem] + [vmem] * (tiles + 1),
+                in_specs=[smem] + [vmem] * (tiles + vecs),
                 out_specs=(vmem,) * (tiles + 2),
-            )(scal, *fields[c], gauge)
+            )(scal, *fields[c], *gauge)
         else:
             pieces = call(out_shape=piece_shapes, in_specs=[smem] + [vmem] * (tiles + 1), out_specs=(vmem,) * tiles)(
                 scal, *fields[c], turned

time: 160 us -> 155 us (0.969)
  blocking collectives: 11.5 us -> 0 us
  waiting for transfers between devices: 45.6 us -> 50.8 us
  starting transfers between devices: 28.6 us -> 31.8 us
  Pallas kernels: 59 us -> 57.2 us
    all_gather x1 -> x0, blocking collectives: 11.5 us -> none  [local(): gauge = lax.all_gather(jnp.stack(shares), 'vec', axis=0)]
    ppermute x21, waiting for transfers between devices: 45.1 us -> 50.5 us  [along_tiles(): lax.ppermute(value, 'tile', [(i, (i + steps) % count) for i in range(coun...]
    ppermute x2 -> x3, starting transfers between devices: 1.43 us -> 3.82 us  [over_chips(): lax.ppermute(value, 'vec', [(i, (i + step) % count) for i in range(count)])]
    ppermute x4 -> x6, starting transfers between devices: 4.61 us -> 6.51 us  [over_cores(): lax.ppermute(block, 'vec', [(i, i ^ 1) for i in range(count)])]
  transfers between devices with their start and end apart: 27 -> 30, of which waited for: 10 -> 11; matrix products, arithmetic and copies ran while one was open for 4% -> 4% of each run, Pallas kernels for 37% -> 37%
where the time goes in v8:
time: 155 us
  Pallas kernels  57.2 us (37%)
  waiting for transfers between devices  50.8 us (33%)
  starting transfers between devices  31.8 us (21%)
  between operations  6.67 us (4%)
  local copies, waits for them, and re-layouts  5.83 us (4%)
  other arithmetic  2.63 us (2%)
    ppermute x21, waiting for transfers between devices, along_tiles(): lax.ppermute(value, 'tile', [(i, (i + steps) % count) for i in range(coun...  50.5 us
    pallas_call x2, Pallas kernels, local(): pl.pallas_call(functools.partial(contract_kernel, vecs, chunks, slots, mo...  35.9 us
    ppermute x21, starting transfers between devices, along_tiles(): lax.ppermute(value, 'tile', [(i, (i + steps) % count) for i in range(coun...  21.4 us
    pallas_call x1, Pallas kernels, local(): call(out_shape=(*piece_shapes, jax.ShapeDtypeStruct((slots, kt, 18, LANES...  11.1 us
    pallas_call x1, Pallas kernels, local(): call(out_shape=piece_shapes, in_specs=[smem] + [vmem] * (tiles + 1), out_...  10.2 us
    ppermute x6, starting transfers between devices, over_cores(): lax.ppermute(block, 'vec', [(i, i ^ 1) for i in range(count)])  6.51 us
    ppermute x3, starting transfers between devices, over_chips(): lax.ppermute(value, 'vec', [(i, (i + step) % count) for i in range(count)])  3.82 us
  transfers between devices with their start and end apart: 30, of which 11 were waited for; matrix products, arithmetic and copies ran while one was open for 4% of the time, Pallas kernels for 37%

profile of v8, /device:TPU:9, one launch (start us, length us, event | category | flops | bytes accessed | tf_op | source)
XLA Modules:
  0.0 154.9 jit_solution(8740612748874818173)
XLA Ops:
  1.2 1.3 collective-permute-start.6
  2.5 1.1 collective-permute-start.7
  3.6 1.4 collective-permute-start.8
  5.0 1.5 fusion.90
  6.8 1.1 collective-permute-start.4
  10.6 1.2 collective-permute-start
  11.8 1.3 collective-permute-start.9
  13.1 2.6 %collective-permute-start.10 = (f32[4,54,256]{2,1,0:T(8,128)S(1)}, f32[4,54,256]{2,1,0:T(8,128)S(1)}, u32[]{:S(2)}, u32[]{:S(2)}) collective-permute-start(f32[4,54,256]{2,1,0:T(8,128)S(1)} %pad_maximum_fusion.3.refs_5_), channel_id=1, source_target_pairs={{0,1},{1,0},{2,3},{3,2},{4,5},{5,4},{6,7},{7,6},{8,9},{9,8},{10,11... | collective-permute-start | bytes 663560 | tf_op jit(solution)/shard_map/ppermute | solution.py:319
  23.6 1.8 %collective-permute-done.refs_2_ = f32[48,1024]{1,0:T(8,128)S(1)} collective-permute-done((f32[48,1024]{1,0:T(8,128)S(1)}, f32[48,1024]{1,0:T(8,128)S(1)}, u32[]{:S(2)}, u32[]{:S(2)}) %collective-permute-start) | collective-permute-done | bytes 196640 | tf_op jit(solution)/shard_map/ppermute | solution.py:300
  25.9 2.9 %collective-permute-start.3 = (f32[48,1024]{1,0:T(8,128)S(1)}, f32[48,1024]{1,0:T(8,128)S(1)}, u32[]{:S(2)}, u32[]{:S(2)}) collective-permute-start(f32[48,1024]{1,0:T(8,128)S(1)} %get-tuple-element.61), channel_id=1, source_target_pairs={{0,8},{4,12},{8,0},{12,4},{1,9},{5,13},{9,1},{13,5},{2,10},{6,14},... | collective-permute-start | bytes 589832 | tf_op jit(solution)/shard_map/ppermute | solution.py:300
  28.8 11.1 %chebyshev.2 = (f32[8,6,8,128]{3,2,1,0:T(8,128)S(1)}, f32[8,6,8,128]{3,2,1,0:T(8,128)S(1)}, f32[8,6,8,128]{3,2,1,0:T(8,128)S(1)}, f32[8,6,8,128]{3,2,1,0:T(8,128...) custom-call(s32[8]{0:T(128)S(1)} %concatenate.12.refs_0_, ...), custom_call_target="tpu_custom_call" | custom-call | flops 14155776000 | bytes 1572864 | tf_op jit(solution)/shard_map/chebyshev/pallas_call | solution.py:423
  40.0 4.2 %collective-permute-done.1.refs_2_ = f32[48,1024]{1,0:T(8,128)S(1)} collective-permute-done((f32[48,1024]{1,0:T(8,128)S(1)}, f32[48,1024]{1,0:T(8,128)S(1)}, u32[]{:S(2)}, u32[]{:S(2)}) %collective-permute-start.1) | collective-permute-done | bytes 196640 | tf_op jit(solution)/shard_map/ppermute | solution.py:300
  44.2 2.2 %collective-permute-start.12 = (f32[8,6,8,128]{3,2,1,0:T(8,128)S(1)}, f32[8,6,8,128]{3,2,1,0:T(8,128)S(1)}, u32[]{:S(2)}, u32[]{:S(2)}) collective-permute-start(f32[8,6,8,128]{3,2,1,0:T(8,128)S(1)} %get-tuple-element.83), channel_id=1, source_target_pairs={{0,4},{4,8},{8,12},{12,0},{1,5},{5,9},{9,13},{13,1},{2,6},{6,10},{... | collective-permute-start | bytes 589832 | tf_op jit(solution)/shard_map/ppermute | solution.py:300
  46.4 2.0 %collective-permute-start.14 = (f32[8,6,8,128]{3,2,1,0:T(8,128)S(1)}, f32[8,6,8,128]{3,2,1,0:T(8,128)S(1)}, u32[]{:S(2)}, u32[]{:S(2)}) collective-permute-start(f32[8,6,8,128]{3,2,1,0:T(8,128)S(1)} %get-tuple-element.86), channel_id=1, source_target_pairs={{0,8},{4,12},{8,0},{12,4},{1,9},{5,13},{9,1},{13,5},{2,10},{6,14},... | collective-permute-start | bytes 589832 | tf_op jit(solution)/shard_map/ppermute | solution.py:300
  48.4 10.2 %chebyshev.3 = (f32[8,6,8,128]{3,2,1,0:T(8,128)S(1)}, f32[8,6,8,128]{3,2,1,0:T(8,128)S(1)}, f32[8,6,8,128]{3,2,1,0:T(8,128)S(1)}, f32[8,6,8,128]{3,2,1,0:T(8,128)S(1)}) custom-call(s32[8]{0:T(128)S(1)} %concatenate.12.refs_0_, f32[48,1024]{1,0:T(8,128)S(1)} %get-tuple-element.77.refs_1_, f32[48,1024]{1,0:T(8,128)S(1)} %collective-permute-done.1.refs_2_, ...), custom_call_target="tpu_custom_call" | custom-call | flops 14155776000 | bytes 1572864 | tf_op jit(solution)/shard_map/chebyshev/pallas_call | solution.py:433
  58.6 4.3 %collective-permute-done.14 = f32[8,6,8,128]{3,2,1,0:T(8,128)S(1)} collective-permute-done((f32[8,6,8,128]{3,2,1,0:T(8,128)S(1)}, f32[8,6,8,128]{3,2,1,0:T(8,128)S(1)}, u32[]{:S(2)}, u32[]{:S(2)}) %collective-permute-start.14) | collective-permute-done | bytes 196640 | tf_op jit(solution)/shard_map/ppermute | solution.py:300
  62.8 1.7 %collective-permute-done.16 = f32[8,6,8,128]{3,2,1,0:T(8,128)S(1)} collective-permute-done((f32[8,6,8,128]{3,2,1,0:T(8,128)S(1)}, f32[8,6,8,128]{3,2,1,0:T(8,128)S(1)}, u32[]{:S(2)}, u32[]{:S(2)}) %collective-permute-start.16) | collective-permute-done | bytes 196640 | tf_op jit(solution)/shard_map/ppermute | solution.py:300
  64.6 1.3 collective-permute-start.19
  66.3 1.5 collective-permute-start.17
  67.7 2.5 %collective-permute-start.20 = (f32[4,8,6,8,128]{4,3,2,1,0:T(8,128)S(1)}, f32[4,8,6,8,128]{4,3,2,1,0:T(8,128)S(1)}, u32[]{:S(2)}, u32[]{:S(2)}) collective-permute-start(f32[4,8,6,8,128]{4,3,2,1,0:T(8,128)S(1)} %pad_maximum_fusion.1.refs_0_.refs_4_), channel_id=1, source_target_pairs={{0,1},{1,0},{2,3},{3,2},{4,5},{5,4},{6,7},{7,6},{8,9},{9,8},{10,11... | collective-permute-start | bytes 2359304 | tf_op jit(solution)/shard_map/ppermute | solution.py:319
  70.7 10.6 %collective-permute-done.15 = f32[8,6,8,128]{3,2,1,0:T(8,128)S(1)} collective-permute-done((f32[8,6,8,128]{3,2,1,0:T(8,128)S(1)}, f32[8,6,8,128]{3,2,1,0:T(8,128)S(1)}, u32[]{:S(2)}, u32[]{:S(2)}) %collective-permute-start.15) | collective-permute-done | bytes 196640 | tf_op jit(solution)/shard_map/ppermute | solution.py:300
  81.3 3.0 %collective-permute-done.17 = f32[8,6,8,128]{3,2,1,0:T(8,128)S(1)} collective-permute-done((f32[8,6,8,128]{3,2,1,0:T(8,128)S(1)}, f32[8,6,8,128]{3,2,1,0:T(8,128)S(1)}, u32[]{:S(2)}, u32[]{:S(2)}) %collective-permute-start.17) | collective-permute-done | bytes 196640 | tf_op jit(solution)/shard_map/ppermute | solution.py:300
  84.9 1.3 collective-permute-start.18
  86.8 18.0 %contract.2 = (f32[32,2048]{1,0:T(8,128)S(1)}, f32[32,2048]{1,0:T(8,128)S(1)}, f32[32,2048]{1,0:T(8,128)S(1)}, f32[32,2048]{1,0:T(8,128)S(1)}) custom-call(s32[4,17]{1,0:T(4,128)S(1)} %pad_add_fusion.1.scal, f32[4,8,6,8,128]{4,3,2,1,0:T(8,128)S(1)} %pad_maximum_fusion.1.refs_0_.refs_4_, f32[4,8,6,8,128]{4,3,2,1,0:T(8,128)S(1)} %collective-permute-done.19.refs_1_, ...), custom_call_target="tpu_custom_call" | custom-call | flops 19327352832 | bytes 4194304 | tf_op jit(solution)/shard_map/contract/pallas_call | solution.py:467
  105.2 2.0 %collective-permute-start.23 = (f32[32,2048]{1,0:T(8,128)S(1)}, f32[32,2048]{1,0:T(8,128)S(1)}, u32[]{:S(2)}, u32[]{:S(2)}) collective-permute-start(f32[32,2048]{1,0:T(8,128)S(1)} %get-tuple-element.108), channel_id=1, source_target_pairs={{0,8},{4,12},{8,0},{12,4},{1,9},{5,13},{9,1},{13,5},{2,10},{6,14},... | collective-permute-start | bytes 786440 | tf_op jit(solution)/shard_map/ppermute | solution.py:300
  107.2 1.5 collective-permute-start.24
  108.7 18.0 %contract.3 = (f32[32,2048]{1,0:T(8,128)S(1)}, f32[32,2048]{1,0:T(8,128)S(1)}, f32[32,2048]{1,0:T(8,128)S(1)}, f32[32,2048]{1,0:T(8,128)S(1)}) custom-call(s32[4,17]{1,0:T(4,128)S(1)} %pad_add_fusion.1.scal, f32[4,8,6,8,128]{4,3,2,1,0:T(8,128)S(1)} %pad_maximum_fusion.refs_5_.refs_0_, f32[4,8,6,8,128]{4,3,2,1,0:T(8,128)S(1)} %collective-permute-done.18.refs_1_, ...), custom_call_target="tpu_custom_call" | custom-call | flops 19327352832 | bytes 4194304 | tf_op jit(solution)/shard_map/contract/pallas_call | solution.py:467
  126.7 2.2 %collective-permute-start.28 = (f32[32,2048]{1,0:T(8,128)S(1)}, f32[32,2048]{1,0:T(8,128)S(1)}, u32[]{:S(2)}, u32[]{:S(2)}) collective-permute-start(f32[32,2048]{1,0:T(8,128)S(1)} %get-tuple-element.113), channel_id=1, source_target_pairs={{0,8},{4,12},{8,0},{12,4},{1,9},{5,13},{9,1},{13,5},{2,10},{6,14},... | collective-permute-start | bytes 786440 | tf_op jit(solution)/shard_map/ppermute | solution.py:300
  128.9 12.8 %collective-permute-done.24 = f32[32,2048]{1,0:T(8,128)S(1)} collective-permute-done((f32[32,2048]{1,0:T(8,128)S(1)}, f32[32,2048]{1,0:T(8,128)S(1)}, u32[]{:S(2)}, u32[]{:S(2)}) %collective-permute-start.24) | collective-permute-done | bytes 262176 | tf_op jit(solution)/shard_map/ppermute | solution.py:300
  141.7 8.6 %collective-permute-done.28 = f32[32,2048]{1,0:T(8,128)S(1)} collective-permute-done((f32[32,2048]{1,0:T(8,128)S(1)}, f32[32,2048]{1,0:T(8,128)S(1)}, u32[]{:S(2)}, u32[]{:S(2)}) %collective-permute-start.28) | collective-permute-done | bytes 262176 | tf_op jit(solution)/shard_map/ppermute | solution.py:300
  150.4 3.0 %collective-permute-done.29 = f32[32,2048]{1,0:T(8,128)S(1)} collective-permute-done((f32[32,2048]{1,0:T(8,128)S(1)}, f32[32,2048]{1,0:T(8,128)S(1)}, u32[]{:S(2)}, u32[]{:S(2)}) %collective-permute-start.29) | collective-permute-done | bytes 262176 | tf_op jit(solution)/shard_map/ppermute | solution.py:300
  153.5 1.4 reshape.2013
  (78 shorter events, 9.0 us)
Async XLA Ops:
  1.2 9.4 %collective-permute-start.6 = (f32[54,256]{1,0:T(8,128)S(1)}, f32[54,256]{1,0:T(8,128)S(1)}, u32[]{:S(2)}, u32[]{:S(2)}) collective-permute-start(f32[54,256]{1,0:T(8,128)S(1)} %constant_dynamic-slice_fusion), channel_id=1, source_target_pairs={{0,4},{4,8},{8,12},{12,0},{1,5},{5,9},{9,13},{13,1},{2,6},{6,10},{... | collective-permute-start | bytes 165896 | tf_op jit(solution)/shard_map/ppermute | solution.py:300
  2.5 9.2 %collective-permute-start.7 = (f32[54,256]{1,0:T(8,128)S(1)}, f32[54,256]{1,0:T(8,128)S(1)}, u32[]{:S(2)}, u32[]{:S(2)}) collective-permute-start(f32[54,256]{1,0:T(8,128)S(1)} %constant_dynamic-slice_fusion), channel_id=1, source_target_pairs={{0,8},{4,12},{8,0},{12,4},{1,9},{5,13},{9,1},{13,5},{2,10},{6,14},... | collective-permute-start | bytes 165896 | tf_op jit(solution)/shard_map/ppermute | solution.py:300
  3.6 8.1 %collective-permute-start.8 = (f32[54,256]{1,0:T(8,128)S(1)}, f32[54,256]{1,0:T(8,128)S(1)}, u32[]{:S(2)}, u32[]{:S(2)}) collective-permute-start(f32[54,256]{1,0:T(8,128)S(1)} %constant_dynamic-slice_fusion), channel_id=1, source_target_pairs={{0,12},{4,0},{8,4},{12,8},{1,13},{5,1},{9,5},{13,9},{2,14},{6,2},{... | collective-permute-start | bytes 165896 | tf_op jit(solution)/shard_map/ppermute | solution.py:300
  6.7 1.6 %copy-start = (s32[2]{0:T(128)S(1)}, s32[2]{0:T(128)}, u32[]{:S(2)}) copy-start(s32[2]{0:T(128)} %param.7) | copy-start | bytes 28
  6.7 15.9 %copy-start.1 = (s32[8,3]{0,1:T(4,128)S(1)}, s32[8,3]{0,1:T(4,128)}, u32[]{:S(2)}) copy-start(s32[8,3]{0,1:T(4,128)} %param.6) | copy-start | bytes 292
  6.8 16.8 %collective-permute-start.4 = (f32[48,1024]{1,0:T(8,128)S(1)}, f32[48,1024]{1,0:T(8,128)S(1)}, u32[]{:S(2)}, u32[]{:S(2)}) collective-permute-start(f32[48,1024]{1,0:T(8,128)S(1)} %get-tuple-element.137), channel_id=1, source_target_pairs={{0,12},{4,0},{8,4},{12,8},{1,13},{5,1},{9,5},{13,9},{2,14},{6,2},{... | collective-permute-start | bytes 589832 | tf_op jit(solution)/shard_map/ppermute | solution.py:300
  7.9 15.7 %collective-permute-start.2 = (f32[48,1024]{1,0:T(8,128)S(1)}, f32[48,1024]{1,0:T(8,128)S(1)}, u32[]{:S(2)}, u32[]{:S(2)}) collective-permute-start(f32[48,1024]{1,0:T(8,128)S(1)} %get-tuple-element.139), channel_id=1, source_target_pairs={{0,8},{4,12},{8,0},{12,4},{1,9},{5,13},{9,1},{13,5},{2,10},{6,14},... | collective-permute-start | bytes 589832 | tf_op jit(solution)/shard_map/ppermute | solution.py:300
  10.6 14.9 %collective-permute-start = (f32[48,1024]{1,0:T(8,128)S(1)}, f32[48,1024]{1,0:T(8,128)S(1)}, u32[]{:S(2)}, u32[]{:S(2)}) collective-permute-start(f32[48,1024]{1,0:T(8,128)S(1)} %get-tuple-element.140), channel_id=1, source_target_pairs={{0,4},{4,8},{8,12},{12,0},{1,5},{5,9},{9,13},{13,1},{2,6},{6,10},{... | collective-permute-start | bytes 589832 | tf_op jit(solution)/shard_map/ppermute | solution.py:300
  11.8 11.7 %collective-permute-start.9 = (f32[4,54,256]{2,1,0:T(8,128)S(1)}, f32[4,54,256]{2,1,0:T(8,128)S(1)}, u32[]{:S(2)}, u32[]{:S(2)}) collective-permute-start(f32[4,54,256]{2,1,0:T(8,128)S(1)} %pad_maximum_fusion.3.refs_5_), channel_id=1, source_target_pairs={{0,2},{1,3},{2,0},{3,1},{4,6},{5,7},{6,4},{7,5},{8,10},{9,11},{10,... | collective-permute-start | bytes 663560 | tf_op jit(solution)/shard_map/ppermute | solution.py:311
  13.1 15.7 %collective-permute-start.10 = (f32[4,54,256]{2,1,0:T(8,128)S(1)}, f32[4,54,256]{2,1,0:T(8,128)S(1)}, u32[]{:S(2)}, u32[]{:S(2)}) collective-permute-start(f32[4,54,256]{2,1,0:T(8,128)S(1)} %pad_maximum_fusion.3.refs_5_), channel_id=1, source_target_pairs={{0,1},{1,0},{2,3},{3,2},{4,5},{5,4},{6,7},{7,6},{8,9},{9,8},{10,11... | collective-permute-start | bytes 663560 | tf_op jit(solution)/shard_map/ppermute | solution.py:319
  23.5 5.3 %collective-permute-start.11 = (f32[4,54,256]{2,1,0:T(8,128)S(1)}, f32[4,54,256]{2,1,0:T(8,128)S(1)}, u32[]{:S(2)}, u32[]{:S(2)}) collective-permute-start(f32[4,54,256]{2,1,0:T(8,128)S(1)} %collective-permute-done.9.refs_6_), channel_id=1, source_target_pairs={{0,1},{1,0},{2,3},{3,2},{4,5},{5,4},{6,7},{7,6},{8,9},{9,8},{10,11... | collective-permute-start | bytes 663560 | tf_op jit(solution)/shard_map/ppermute | solution.py:319
  25.4 14.5 %collective-permute-start.5 = (f32[48,1024]{1,0:T(8,128)S(1)}, f32[48,1024]{1,0:T(8,128)S(1)}, u32[]{:S(2)}, u32[]{:S(2)}) collective-permute-start(f32[48,1024]{1,0:T(8,128)S(1)} %get-tuple-element.62), channel_id=1, source_target_pairs={{0,12},{4,0},{8,4},{12,8},{1,13},{5,1},{9,5},{13,9},{2,14},{6,2},{... | collective-permute-start | bytes 589832 | tf_op jit(solution)/shard_map/ppermute | solution.py:300
  25.9 14.1 %collective-permute-start.3 = (f32[48,1024]{1,0:T(8,128)S(1)}, f32[48,1024]{1,0:T(8,128)S(1)}, u32[]{:S(2)}, u32[]{:S(2)}) collective-permute-start(f32[48,1024]{1,0:T(8,128)S(1)} %get-tuple-element.61), channel_id=1, source_target_pairs={{0,8},{4,12},{8,0},{12,4},{1,9},{5,13},{9,1},{13,5},{2,10},{6,14},... | collective-permute-start | bytes 589832 | tf_op jit(solution)/shard_map/ppermute | solution.py:300
  28.8 15.4 %collective-permute-start.1 = (f32[48,1024]{1,0:T(8,128)S(1)}, f32[48,1024]{1,0:T(8,128)S(1)}, u32[]{:S(2)}, u32[]{:S(2)}) collective-permute-start(f32[48,1024]{1,0:T(8,128)S(1)} %get-tuple-element.60), channel_id=1, source_target_pairs={{0,4},{4,8},{8,12},{12,0},{1,5},{5,9},{9,13},{13,1},{2,6},{6,10},{... | collective-permute-start | bytes 589832 | tf_op jit(solution)/shard_map/ppermute | solution.py:300
  44.2 14.4 %collective-permute-start.12 = (f32[8,6,8,128]{3,2,1,0:T(8,128)S(1)}, f32[8,6,8,128]{3,2,1,0:T(8,128)S(1)}, u32[]{:S(2)}, u32[]{:S(2)}) collective-permute-start(f32[8,6,8,128]{3,2,1,0:T(8,128)S(1)} %get-tuple-element.83), channel_id=1, source_target_pairs={{0,4},{4,8},{8,12},{12,0},{1,5},{5,9},{9,13},{13,1},{2,6},{6,10},{... | collective-permute-start | bytes 589832 | tf_op jit(solution)/shard_map/ppermute | solution.py:300
  46.4 16.4 %collective-permute-start.14 = (f32[8,6,8,128]{3,2,1,0:T(8,128)S(1)}, f32[8,6,8,128]{3,2,1,0:T(8,128)S(1)}, u32[]{:S(2)}, u32[]{:S(2)}) collective-permute-start(f32[8,6,8,128]{3,2,1,0:T(8,128)S(1)} %get-tuple-element.86), channel_id=1, source_target_pairs={{0,8},{4,12},{8,0},{12,4},{1,9},{5,13},{9,1},{13,5},{2,10},{6,14},... | collective-permute-start | bytes 589832 | tf_op jit(solution)/shard_map/ppermute | solution.py:300
  48.4 16.2 %collective-permute-start.16 = (f32[8,6,8,128]{3,2,1,0:T(8,128)S(1)}, f32[8,6,8,128]{3,2,1,0:T(8,128)S(1)}, u32[]{:S(2)}, u32[]{:S(2)}) collective-permute-start(f32[8,6,8,128]{3,2,1,0:T(8,128)S(1)} %get-tuple-element.89), channel_id=1, source_target_pairs={{0,12},{4,0},{8,4},{12,8},{1,13},{5,1},{9,5},{13,9},{2,14},{6,2},{... | collective-permute-start | bytes 589832 | tf_op jit(solution)/shard_map/ppermute | solution.py:300
  64.6 19.7 %collective-permute-start.19 = (f32[4,8,6,8,128]{4,3,2,1,0:T(8,128)S(1)}, f32[4,8,6,8,128]{4,3,2,1,0:T(8,128)S(1)}, u32[]{:S(2)}, u32[]{:S(2)}) collective-permute-start(f32[4,8,6,8,128]{4,3,2,1,0:T(8,128)S(1)} %pad_maximum_fusion.1.refs_0_.refs_4_), channel_id=1, source_target_pairs={{0,2},{1,3},{2,0},{3,1},{4,6},{5,7},{6,4},{7,5},{8,10},{9,11},{10,... | collective-permute-start | bytes 2359304 | tf_op jit(solution)/shard_map/ppermute | solution.py:311
  65.9 4.8 %collective-permute-start.13 = (f32[8,6,8,128]{3,2,1,0:T(8,128)S(1)}, f32[8,6,8,128]{3,2,1,0:T(8,128)S(1)}, u32[]{:S(2)}, u32[]{:S(2)}) collective-permute-start(f32[8,6,8,128]{3,2,1,0:T(8,128)S(1)} %get-tuple-element.85), channel_id=1, source_target_pairs={{0,4},{4,8},{8,12},{12,0},{1,5},{5,9},{9,13},{13,1},{2,6},{6,10},{... | collective-permute-start | bytes 589832 | tf_op jit(solution)/shard_map/ppermute | solution.py:300
  65.9 15.4 %collective-permute-start.15 = (f32[8,6,8,128]{3,2,1,0:T(8,128)S(1)}, f32[8,6,8,128]{3,2,1,0:T(8,128)S(1)}, u32[]{:S(2)}, u32[]{:S(2)}) collective-permute-start(f32[8,6,8,128]{3,2,1,0:T(8,128)S(1)} %get-tuple-element.88), channel_id=1, source_target_pairs={{0,8},{4,12},{8,0},{12,4},{1,9},{5,13},{9,1},{13,5},{2,10},{6,14},... | collective-permute-start | bytes 589832 | tf_op jit(solution)/shard_map/ppermute | solution.py:300
  66.3 18.0 %collective-permute-start.17 = (f32[8,6,8,128]{3,2,1,0:T(8,128)S(1)}, f32[8,6,8,128]{3,2,1,0:T(8,128)S(1)}, u32[]{:S(2)}, u32[]{:S(2)}) collective-permute-start(f32[8,6,8,128]{3,2,1,0:T(8,128)S(1)} %get-tuple-element.91), channel_id=1, source_target_pairs={{0,12},{4,0},{8,4},{12,8},{1,13},{5,1},{9,5},{13,9},{2,14},{6,2},{... | collective-permute-start | bytes 589832 | tf_op jit(solution)/shard_map/ppermute | solution.py:300
  67.7 18.8 %collective-permute-start.20 = (f32[4,8,6,8,128]{4,3,2,1,0:T(8,128)S(1)}, f32[4,8,6,8,128]{4,3,2,1,0:T(8,128)S(1)}, u32[]{:S(2)}, u32[]{:S(2)}) collective-permute-start(f32[4,8,6,8,128]{4,3,2,1,0:T(8,128)S(1)} %pad_maximum_fusion.1.refs_0_.refs_4_), channel_id=1, source_target_pairs={{0,1},{1,0},{2,3},{3,2},{4,5},{5,4},{6,7},{7,6},{8,9},{9,8},{10,11... | collective-permute-start | bytes 2359304 | tf_op jit(solution)/shard_map/ppermute | solution.py:319
  84.3 2.5 %collective-permute-start.21 = (f32[4,8,6,8,128]{4,3,2,1,0:T(8,128)S(1)}, f32[4,8,6,8,128]{4,3,2,1,0:T(8,128)S(1)}, u32[]{:S(2)}, u32[]{:S(2)}) collective-permute-start(f32[4,8,6,8,128]{4,3,2,1,0:T(8,128)S(1)} %collective-permute-done.19.refs_1_), channel_id=1, source_target_pairs={{0,1},{1,0},{2,3},{3,2},{4,5},{5,4},{6,7},{7,6},{8,9},{9,8},{10,11... | collective-permute-start | bytes 2359304 | tf_op jit(solution)/shard_map/ppermute | solution.py:319
  84.9 19.9 %collective-permute-start.18 = (f32[4,8,6,8,128]{4,3,2,1,0:T(8,128)S(1)}, f32[4,8,6,8,128]{4,3,2,1,0:T(8,128)S(1)}, u32[]{:S(2)}, u32[]{:S(2)}) collective-permute-start(f32[4,8,6,8,128]{4,3,2,1,0:T(8,128)S(1)} %pad_maximum_fusion.refs_5_.refs_0_), channel_id=1, source_target_pairs={{0,2},{1,3},{2,0},{3,1},{4,6},{5,7},{6,4},{7,5},{8,10},{9,11},{10,... | collective-permute-start | bytes 2359304 | tf_op jit(solution)/shard_map/ppermute | solution.py:311
  86.2 22.5 %collective-permute-start.25 = (f32[4,8,6,8,128]{4,3,2,1,0:T(8,128)S(1)}, f32[4,8,6,8,128]{4,3,2,1,0:T(8,128)S(1)}, u32[]{:S(2)}, u32[]{:S(2)}) collective-permute-start(f32[4,8,6,8,128]{4,3,2,1,0:T(8,128)S(1)} %pad_maximum_fusion.refs_5_.refs_0_), channel_id=1, source_target_pairs={{0,1},{1,0},{2,3},{3,2},{4,5},{5,4},{6,7},{7,6},{8,9},{9,8},{10,11... | collective-permute-start | bytes 2359304 | tf_op jit(solution)/shard_map/ppermute | solution.py:319
  104.8 3.9 %collective-permute-start.26 = (f32[4,8,6,8,128]{4,3,2,1,0:T(8,128)S(1)}, f32[4,8,6,8,128]{4,3,2,1,0:T(8,128)S(1)}, u32[]{:S(2)}, u32[]{:S(2)}) collective-permute-start(f32[4,8,6,8,128]{4,3,2,1,0:T(8,128)S(1)} %collective-permute-done.18.refs_1_), channel_id=1, source_target_pairs={{0,1},{1,0},{2,3},{3,2},{4,5},{5,4},{6,7},{7,6},{8,9},{9,8},{10,11... | collective-permute-start | bytes 2359304 | tf_op jit(solution)/shard_map/ppermute | solution.py:319
  105.2 23.7 %collective-permute-start.22 = (f32[32,2048]{1,0:T(8,128)S(1)}, f32[32,2048]{1,0:T(8,128)S(1)}, u32[]{:S(2)}, u32[]{:S(2)}) collective-permute-start(f32[32,2048]{1,0:T(8,128)S(1)} %get-tuple-element.107), channel_id=1, source_target_pairs={{0,4},{4,8},{8,12},{12,0},{1,5},{5,9},{9,13},{13,1},{2,6},{6,10},{... | collective-permute-start | bytes 786440 | tf_op jit(solution)/shard_map/ppermute | solution.py:300
  105.2 23.7 %collective-permute-start.23 = (f32[32,2048]{1,0:T(8,128)S(1)}, f32[32,2048]{1,0:T(8,128)S(1)}, u32[]{:S(2)}, u32[]{:S(2)}) collective-permute-start(f32[32,2048]{1,0:T(8,128)S(1)} %get-tuple-element.108), channel_id=1, source_target_pairs={{0,8},{4,12},{8,0},{12,4},{1,9},{5,13},{9,1},{13,5},{2,10},{6,14},... | collective-permute-start | bytes 786440 | tf_op jit(solution)/shard_map/ppermute | solution.py:300
  107.2 34.4 %collective-permute-start.24 = (f32[32,2048]{1,0:T(8,128)S(1)}, f32[32,2048]{1,0:T(8,128)S(1)}, u32[]{:S(2)}, u32[]{:S(2)}) collective-permute-start(f32[32,2048]{1,0:T(8,128)S(1)} %get-tuple-element.109), channel_id=1, source_target_pairs={{0,12},{4,0},{8,4},{12,8},{1,13},{5,1},{9,5},{13,9},{2,14},{6,2},{... | collective-permute-start | bytes 786440 | tf_op jit(solution)/shard_map/ppermute | solution.py:300
  126.7 15.1 %collective-permute-start.27 = (f32[32,2048]{1,0:T(8,128)S(1)}, f32[32,2048]{1,0:T(8,128)S(1)}, u32[]{:S(2)}, u32[]{:S(2)}) collective-permute-start(f32[32,2048]{1,0:T(8,128)S(1)} %get-tuple-element.112), channel_id=1, source_target_pairs={{0,4},{4,8},{8,12},{12,0},{1,5},{5,9},{9,13},{13,1},{2,6},{6,10},{... | collective-permute-start | bytes 786440 | tf_op jit(solution)/shard_map/ppermute | solution.py:300
  126.7 23.6 %collective-permute-start.28 = (f32[32,2048]{1,0:T(8,128)S(1)}, f32[32,2048]{1,0:T(8,128)S(1)}, u32[]{:S(2)}, u32[]{:S(2)}) collective-permute-start(f32[32,2048]{1,0:T(8,128)S(1)} %get-tuple-element.113), channel_id=1, source_target_pairs={{0,8},{4,12},{8,0},{12,4},{1,9},{5,13},{9,1},{13,5},{2,10},{6,14},... | collective-permute-start | bytes 786440 | tf_op jit(solution)/shard_map/ppermute | solution.py:300
  128.9 24.5 %collective-permute-start.29 = (f32[32,2048]{1,0:T(8,128)S(1)}, f32[32,2048]{1,0:T(8,128)S(1)}, u32[]{:S(2)}, u32[]{:S(2)}) collective-permute-start(f32[32,2048]{1,0:T(8,128)S(1)} %get-tuple-element.114), channel_id=1, source_target_pairs={{0,12},{4,0},{8,4},{12,8},{1,13},{5,1},{9,5},{13,9},{2,14},{6,2},{... | collective-permute-start | bytes 786440 | tf_op jit(solution)/shard_map/ppermute | solution.py:300
